TPU v7x, 128 devices: a whole 4x4x4 slice. The times are simulated.
128 devices in a mesh: down: 8 (over x_hi, z), cross: 16 (over y, x_lo, core).
Axes of the slice: x: 4 (x_hi: 2, x_lo: 2; x = x_hi * 2 + x_lo), y: 4, z: 4, core: 2. Of those that a mesh axis runs over, the one named last changes fastest.
Arguments:
- right_side: float32 [3, 35, 32, 8192], P(None, None, 'down', 'cross'), may hold values from -48 to 48
- stiffness: float32 [32, 8192], P('down', 'cross'), may hold values from 1 to 8
- coefficients: float32 [5, 32, 8192], P(None, 'down', 'cross'), may hold values from -0.73 to 3.001, as said below
- stencil_weights: float32 [13], replicated, may hold values from 0.05 to 0.3
Outputs:
- solution_field: float32 [3, 35, 32, 8192], P(None, None, 'down', 'cross')
- residual: float32 [3, 35, 32, 8192], P(None, None, 'down', 'cross')
Inputs may be any that keep to these rules, and one draw needn't show every extreme that they name: `coefficients`: entry 0 at every cell lies between 0.5 and 3 and exceeds the sum of the magnitudes of entries 1 to 4 at that cell.
All inputs are finite; a program needn't handle non-finite values.
Results may differ from a plain program's by a relative error of at most 0.04.
Values sent between devices are 32-bit elements; how exact they have to be, the bound alone decides.
No kernel may reach another device: no remote copies, remote signals or barrier semaphores. Data moves between devices by JAX's collectives and lax.ppermute only.
A program may use at most 128 MiB of HBM per device.

v0:
```python
import functools
import math

import jax
import jax.numpy as jnp
import numpy as np
from jax import lax
from jax.experimental import pallas as pl
from jax.experimental.pallas import tpu as pltpu
from jax.sharding import PartitionSpec as P

CZ = 32
VARS = 4
DEG = 3
TERMS = 5
COMPS = 3
MODES = 35
FIELDS = COMPS * MODES
STIFF = FIELDS + TERMS
ROWS = 4
LANES = 128
WIDE = 64


def multi_indices(count_left, budget_left):
    if count_left == 0:
        return [()]
    return [
        (leading,) + remainder
        for leading in range(budget_left + 1)
        for remainder in multi_indices(count_left - 1, budget_left - leading)
    ]


def chaos_terms():
    picked = sorted(
        multi_indices(VARS, DEG),
        key=lambda multi_index: (sum(multi_index),)
        + tuple((-entry_value for entry_value in multi_index)),
    )
    position = {multi_index: number for number, multi_index in enumerate(picked)}
    terms = [[] for mode in picked]
    for variable in range(VARS):
        for multi_index in picked:
            raised = list(multi_index)
            raised[variable] += 1
            raised = tuple(raised)
            if raised in position:
                degree = multi_index[variable]
                here, there = position[multi_index], position[raised]
                terms[here].append((variable, degree, there))
                terms[there].append((variable, degree, here))
    values = [(n + 1) / math.sqrt((2 * n + 1) * (2 * n + 3)) for n in range(DEG)]
    return terms, values


CHAOS, CHAOS_VALUES = chaos_terms()
TABLE = 1 + VARS * DEG


def tap_slots():
    own = np.arange(LANES)
    place = np.concatenate([own, own[:WIDE] + LANES, own[WIDE:] - LANES])
    y_in, z_in = place // CZ, place % CZ
    y_out, z_out = own // CZ, own % CZ
    dy = y_in[:, None] - y_out[None, :]
    dz = z_in[:, None] - z_out[None, :]
    near = (abs(dy) <= 1) & (abs(dz) <= 1)
    parts = []
    for dx in (0, 1, -1):
        linear = 9 * (dx + 1) + 3 * (dy + 1) + (dz + 1)
        slot = np.minimum(linear, 26 - linear)
        parts.append(np.where(near, slot, 13))
    return np.concatenate(parts, axis=1).astype(np.int32)


SLOTS = tap_slots()


def stencil_matrix(weights):
    slots = jnp.asarray(SLOTS)
    full = jnp.zeros(slots.shape, jnp.float32)
    for number in range(13):
        full = jnp.where(slots == number, 0.5 * weights[number], full)
    high = lax.reduce_precision(full, 8, 7)
    low = (full - high).astype(jnp.bfloat16)
    high = high.astype(jnp.bfloat16)
    return jnp.concatenate([high, high, low], axis=0)


def mix(table, load, mode, total):
    for variable, degree, other in CHAOS[mode]:
        total = total + table[1 + variable * DEG + degree] * load(other)
    return total


def window(high, low, now, chunks):
    after, before = (now + 1) % chunks, (now + chunks - 1) % chunks
    shape = high.shape[1:]
    left = lax.broadcasted_iota(jnp.int32, shape, 1) < WIDE
    own_high, own_low = high[now], low[now]
    mix_high = jnp.where(left, high[after], high[before])
    mix_low = jnp.where(left, low[after], low[before])
    return jnp.concatenate([own_high, mix_high, own_low, mix_low, own_high, mix_high], axis=1)


def stencil(high, low, now, chunks, matrix, out):
    parts = jnp.dot(
        window(high, low, now, chunks), matrix[...], preferred_element_type=jnp.float32
    )
    shape = out.shape
    centre = parts[:, :LANES].reshape(shape)
    ahead = parts[:, LANES : 2 * LANES].reshape(shape)
    behind = parts[:, 2 * LANES :].reshape(shape)
    out[...] = centre + pltpu.roll(ahead, 7, 1) + pltpu.roll(behind, 1, 1)


def split(value, high, low, now):
    value = value.reshape(high.shape[1:])
    top = value.astype(jnp.bfloat16)
    high[now] = top
    low[now] = (value - top.astype(jnp.float32)).astype(jnp.bfloat16)


def operator_kernel(
    chunks,
    own_ref, extra_ref, left_ref, right_ref, upper_ref, lower_ref, matrix_ref, sum_ref,
    image_ref, second_ref, sums_ref,
    field, field_high, field_low, grown, grown_high, grown_low,
    first_near, second_near, image, image_high, image_low, coef_table, diag_table,
):
    edge = chunks - 1
    for k in range(edge):
        lanes = pl.ds(k * LANES, LANES)
        field[k, :FIELDS, 0:ROWS, :] = own_ref[:, :, lanes]
        field[k, FIELDS : STIFF + 1, 0:ROWS, :] = extra_ref[:, :, lanes]
    field[edge, : STIFF + 1, 0:ROWS, :] = jnp.concatenate([right_ref[...], left_ref[...]], axis=2)
    for k in range(chunks):
        lanes = pl.ds(k * LANES, LANES)
        field[k, : STIFF + 1, ROWS : ROWS + 2, :] = upper_ref[:, :, lanes]
        field[k, : STIFF + 1, ROWS + 2 : ROWS + 4, :] = lower_ref[:, :, lanes]
        field[k, STIFF + 1] = jnp.zeros((8, LANES), jnp.float32)
        image[k, FIELDS] = jnp.zeros((8, LANES), jnp.float32)
    grown[FIELDS] = jnp.zeros((8, LANES), jnp.float32)

    def fill(table, k, values):
        table[k, 0] = values[0]
        for variable in range(VARS):
            for degree in range(DEG):
                table[k, 1 + variable * DEG + degree] = values[1 + variable] * CHAOS_VALUES[degree]

    def load_table(table, k):
        return [table[k, entry] for entry in range(TABLE)]

    @pl.loop(0, chunks)
    def grow(k):
        fill(coef_table, k, [field[k, FIELDS + term] for term in range(TERMS)])
        table = load_table(coef_table, k)

        @pl.loop(0, COMPS)
        def each(comp):
            base = comp * MODES
            for mode in range(MODES):
                load = lambda other: field[k, base + other]
                grown[base + mode] = mix(table, load, mode, table[0] * load(mode))

        split(grown[...], grown_high, grown_low, k)
        split(field[k], field_high, field_low, k)

    @pl.loop(0, chunks)
    def first(k):
        stencil(field_high, field_low, k, chunks, matrix_ref, first_near)
        stencil(grown_high, grown_low, k, chunks, matrix_ref, second_near)
        weight_sum = sum_ref[0]
        fill(
            diag_table,
            k,
            [
                field[k, FIELDS + term] * weight_sum + first_near[FIELDS + term]
                for term in range(TERMS)
            ],
        )
        coef = load_table(coef_table, k)
        diag = load_table(diag_table, k)
        stiff = field[k, STIFF]
        inside = stiff > 0.0

        @pl.loop(0, COMPS)
        def each(comp):
            base = comp * MODES
            for mode in range(MODES):
                load = lambda other: field[k, base + other]
                near = lambda other: first_near[base + other]
                value = mix(diag, load, mode, (stiff + diag[0]) * load(mode))
                value = value - mix(coef, near, mode, coef[0] * near(mode) + second_near[base + mode])
                image[k, base + mode] = jnp.where(inside, value, 0.0)

    @pl.loop(0, chunks)
    def regrow(k):
        table = load_table(coef_table, k)

        @pl.loop(0, COMPS)
        def each(comp):
            base = comp * MODES
            for mode in range(MODES):
                load = lambda other: image[k, base + other]
                grown[base + mode] = mix(table, load, mode, table[0] * load(mode))

        split(grown[...], grown_high, grown_low, k)
        split(image[k], image_high, image_low, k)

    third_near = first_near.at[pl.ds(0, FIELDS + 1)]
    zero = jnp.zeros((8, LANES), jnp.float32)

    def second(k, sums):
        stencil(image_high, image_low, k, chunks, matrix_ref, third_near)
        stencil(grown_high, grown_low, k, chunks, matrix_ref, second_near)
        coef = load_table(coef_table, k)
        diag = load_table(diag_table, k)
        stiff = field[k, STIFF]
        lanes = pl.ds(pl.multiple_of(k * LANES, LANES), LANES)

        def each(comp, sums):
            rr, rq, qq, qz = sums
            base = comp * MODES
            for mode in range(MODES):
                load = lambda other: image[k, base + other]
                near = lambda other: third_near[base + other]
                start, here = field[k, base + mode], load(mode)
                value = mix(diag, load, mode, (stiff + diag[0]) * here)
                value = value - mix(coef, near, mode, coef[0] * near(mode) + second_near[base + mode])
                image_ref[base + mode, :, lanes] = here[:ROWS]
                second_ref[base + mode, :, lanes] = value[:ROWS]
                rr, rq, qq, qz = rr + start * start, rq + start * here, qq + here * here, qz + here * value
            return rr, rq, qq, qz

        return lax.fori_loop(0, COMPS, each, sums)

    sums = lax.fori_loop(0, edge, second, (zero, zero, zero, zero))
    inner = lax.broadcasted_iota(jnp.int32, (8, LANES), 0) < ROWS
    lane = lax.broadcasted_iota(jnp.int32, sums_ref.shape, 1)
    row = jnp.zeros(sums_ref.shape, jnp.float32)
    for number, value in enumerate(sums):
        row = jnp.where(lane == number, jnp.sum(jnp.where(inner, value, 0.0)), row)
    sums_ref[...] = row


def finish_kernel(sums_ref, start_ref, image_ref, second_ref, field_ref, residual_ref):
    total = jnp.sum(sums_ref[...], axis=0, keepdims=True)
    lane = lax.broadcasted_iota(jnp.int32, total.shape, 1)
    rr, rq, qq, qz = [
        jnp.sum(jnp.where(lane == number, total, 0.0), axis=1, keepdims=True)[None]
        for number in range(4)
    ]
    step = rr / rq
    fresh = rr - 2.0 * step * rq + step * step * qq
    grow = 1.0 + fresh / rr
    curvature = grow * grow * rq - 2.0 * grow * step * qq + step * step * qz
    later = fresh / curvature
    both = step + later * grow
    cross = later * step
    start, image, second = start_ref[...], image_ref[...], second_ref[...]
    field_ref[...] = both * start - cross * image
    residual_ref[...] = start - both * image + cross * second


def shift(value, axis, by):
    size = lax.axis_size(axis)
    return lax.ppermute(value, axis, [(i, i + by) for i in range(size) if 0 <= i + by < size])


def per_device(right_side, stiffness, coefficients, stencil_weights):
    columns = right_side.shape[3]
    chunks = columns // LANES + 1
    devices = lax.axis_size("down") * lax.axis_size("cross")
    own = right_side.reshape(FIELDS, ROWS, columns)
    extra = jnp.concatenate([coefficients, stiffness[None]], axis=0)
    all_fields = jnp.concatenate([own, extra], axis=0)
    right = shift(all_fields[:, :, :WIDE], "cross", -1)
    left = shift(all_fields[:, :, columns - WIDE :], "cross", 1)
    wide = jnp.concatenate([all_fields, right, left], axis=2)
    upper = shift(wide[:, :2], "down", -1)
    lower = shift(wide[:, ROWS - 2 :], "down", 1)
    matrix = stencil_matrix(stencil_weights)
    weight_sum = jnp.sum(stencil_weights).reshape(1)
    vmem = pl.BlockSpec(memory_space=pltpu.VMEM)
    count = FIELDS + 1
    f32, bf16 = jnp.float32, jnp.bfloat16
    image, second, sums = pl.pallas_call(
        functools.partial(operator_kernel, chunks),
        out_shape=(
            jax.ShapeDtypeStruct(own.shape, f32),
            jax.ShapeDtypeStruct(own.shape, f32),
            jax.ShapeDtypeStruct((devices, LANES), f32),
        ),
        in_specs=[vmem] * 7 + [pl.BlockSpec(memory_space=pltpu.SMEM)],
        out_specs=(vmem, vmem, vmem),
        scratch_shapes=[
            pltpu.VMEM((chunks, STIFF + 2, 8, LANES), f32),
            pltpu.VMEM((chunks, (STIFF + 2) * 8, LANES), bf16),
            pltpu.VMEM((chunks, (STIFF + 2) * 8, LANES), bf16),
            pltpu.VMEM((count, 8, LANES), f32),
            pltpu.VMEM((chunks, count * 8, LANES), bf16),
            pltpu.VMEM((chunks, count * 8, LANES), bf16),
            pltpu.VMEM((STIFF + 2, 8, LANES), f32),
            pltpu.VMEM((count, 8, LANES), f32),
            pltpu.VMEM((chunks, count, 8, LANES), f32),
            pltpu.VMEM((chunks, count * 8, LANES), bf16),
            pltpu.VMEM((chunks, count * 8, LANES), bf16),
            pltpu.VMEM((chunks, TABLE, 8, LANES), f32),
            pltpu.VMEM((chunks, TABLE, 8, LANES), f32),
        ],
        compiler_params=pltpu.CompilerParams(vmem_limit_bytes=48 * 1024 * 1024),
        name="operator",
    )(own, extra, left, right, upper, lower, matrix, weight_sum)
    sums = lax.all_to_all(sums, ("down", "cross"), 0, 0, tiled=True)
    solution_field, residual = pl.pallas_call(
        finish_kernel,
        out_shape=(jax.ShapeDtypeStruct(own.shape, f32), jax.ShapeDtypeStruct(own.shape, f32)),
        in_specs=[vmem] * 4,
        out_specs=(vmem, vmem),
        compiler_params=pltpu.CompilerParams(vmem_limit_bytes=32 * 1024 * 1024),
        name="finish",
    )(sums, own, image, second)
    return solution_field.reshape(right_side.shape), residual.reshape(right_side.shape)


def solution(mesh):
    return jax.shard_map(
        per_device,
        mesh=mesh,
        in_specs=(
            P(None, None, "down", "cross"),
            P("down", "cross"),
            P(None, "down", "cross"),
            P(),
        ),
        out_specs=(P(None, None, "down", "cross"), P(None, None, "down", "cross")),
        check_vma=False,
    )
```

profile of v0, /device:TPU:1, one launch (start us, length us, event | category | flops | bytes accessed | tf_op | source)
XLA Modules:
  0.0 76.8 jit_solution(13122802672162697985)
XLA Ops:
  0.7 1.4 %pad_maximum_fusion.2 = (f32[111,4,64]{2,1,0:T(4,128)S(1)}, f32[111,4,64]{2,1,0:T(4,128)S(1)}) fusion(f32[1,4,512]{2,1,0:T(4,128)} %bitcast.28, f32[5,4,512]{2,1,0:T(4,128)} %param.7, f32[105,4,512]{2,1,0:T(4,128)} %bitcast.22), kind=kLoop, calls=%fused_computation.6 | loop fusion | flops 113664 | bytes 1136640 | tf_op jit(solution)/shard_map/concatenate | solution.py:278
  2.0 3.3 %collective-permute-start.1 = (f32[111,4,64]{2,1,0:T(4,128)S(1)}, f32[111,4,64]{2,1,0:T(4,128)S(1)}, u32[]{:S(2)}, u32[]{:S(2)}) collective-permute-start(f32[111,4,64]{2,1,0:T(4,128)S(1)} %get-tuple-element.14), channel_id=1, source_target_pairs={{1,0},{2,1},{3,2},{4,3},{5,4},{6,5},{7,6},{8,7},{9,8},{10,9},{11,1... | collective-permute-start | bytes 341000 | tf_op jit(solution)/shard_map/ppermute | solution.py:269
  5.4 3.1 %collective-permute-start = (f32[111,4,64]{2,1,0:T(4,128)S(1)}, f32[111,4,64]{2,1,0:T(4,128)S(1)}, u32[]{:S(2)}, u32[]{:S(2)}) collective-permute-start(f32[111,4,64]{2,1,0:T(4,128)S(1)} %get-tuple-element.15), channel_id=1, source_target_pairs={{0,1},{1,2},{2,3},{3,4},{4,5},{5,6},{6,7},{7,8},{8,9},{9,10},{10,1... | collective-permute-start | bytes 341000 | tf_op jit(solution)/shard_map/ppermute | solution.py:269
  8.5 0.7 reduce_sum.9
  9.2 1.1 %collective-permute-done.1.right_ref = f32[111,4,64]{2,1,0:T(4,128)S(1)} collective-permute-done((f32[111,4,64]{2,1,0:T(4,128)S(1)}, f32[111,4,64]{2,1,0:T(4,128)S(1)}, u32[]{:S(2)}, u32[]{:S(2)}) %collective-permute-start.1) | collective-permute-done | bytes 113696 | tf_op jit(solution)/shard_map/ppermute | solution.py:269
  10.2 1.2 %collective-permute-done.left_ref = f32[111,4,64]{2,1,0:T(4,128)S(1)} collective-permute-done((f32[111,4,64]{2,1,0:T(4,128)S(1)}, f32[111,4,64]{2,1,0:T(4,128)S(1)}, u32[]{:S(2)}, u32[]{:S(2)}) %collective-permute-start) | collective-permute-done | bytes 113696 | tf_op jit(solution)/shard_map/ppermute | solution.py:269
  11.4 0.3 pad_maximum_fusion
  11.8 0.0 copy-start.1
  11.8 0.0 copy-start.2
  11.8 0.0 copy-start.4
  11.8 0.0 copy-start.5
  11.8 0.0 copy-start.6
  11.8 0.0 copy-start.7
  11.9 0.4 fusion.1
  12.4 3.6 %collective-permute-start.3 = (f32[111,2,640]{2,1,0:T(2,128)S(1)}, f32[111,2,640]{2,1,0:T(2,128)S(1)}, u32[]{:S(2)}, u32[]{:S(2)}) collective-permute-start(f32[111,2,640]{2,1,0:T(2,128)S(1)} %get-tuple-element.12), channel_id=1, source_target_pairs={{0,16},{16,32},{32,48},{48,64},{64,80},{80,96},{96,112},{1,17},{17... | collective-permute-start | bytes 1704968 | tf_op jit(solution)/shard_map/ppermute | solution.py:269
  16.0 1.3 %collective-permute-start.2 = (f32[111,2,640]{2,1,0:T(2,128)S(1)}, f32[111,2,640]{2,1,0:T(2,128)S(1)}, u32[]{:S(2)}, u32[]{:S(2)}) collective-permute-start(f32[111,2,640]{2,1,0:T(2,128)S(1)} %get-tuple-element.13), channel_id=1, source_target_pairs={{16,0},{32,16},{48,32},{64,48},{80,64},{96,80},{112,96},{17,1},{33... | collective-permute-start | bytes 1704968 | tf_op jit(solution)/shard_map/ppermute | solution.py:269
  17.3 0.7 fusion.2
  26.3 0.5 fusion
  26.8 0.5 reduce-precision_convert_fusion
  27.4 0.1 pad_maximum_fusion.1.matrix_ref
  27.4 3.3 %collective-permute-done.2.upper_ref = f32[111,2,640]{2,1,0:T(2,128)S(1)} collective-permute-done((f32[111,2,640]{2,1,0:T(2,128)S(1)}, f32[111,2,640]{2,1,0:T(2,128)S(1)}, u32[]{:S(2)}, u32[]{:S(2)}) %collective-permute-start.2) | collective-permute-done | bytes 568352 | tf_op jit(solution)/shard_map/ppermute | solution.py:269
  30.8 21.0 %operator.1 = (f32[105,4,512]{2,1,0:T(4,128)S(1)}, f32[105,4,512]{2,1,0:T(4,128)S(1)}, f32[128,128]{1,0:T(8,128)S(1)}) custom-call(f32[105,4,512]{2,1,0:T(4,128)S(1)} %bitcast.24, f32[6,4,512]{2,1,0:T(4,128)S(1)} %pad_maximum_fusion.5.extra_ref, f32[111,4,64]{2,1,0:T(4,128)S(1)} %collective-permute-done.left_ref, ...), custom_call_target="tpu_custom_call" | custom-call | tf_op jit(solution)/shard_map/operator/pallas_call | solution.py:289
  51.7 23.5 %all_to_all.11 = f32[128,1,128]{2,1,0:T(1,128)S(1)} all-to-all(f32[128,1,128]{2,1,0:T(1,128)S(1)} %bitcast.27), channel_id=1, replica_groups=mesh['down'=8,'cross'=16] {'down','cross'}, dimensions={0} | all-to-all | bytes 131072 | tf_op jit(solution)/shard_map/all_to_all | solution.py:316
  75.2 1.6 %finish.1 = (f32[105,4,512]{2,1,0:T(4,128)}, f32[105,4,512]{2,1,0:T(4,128)}) custom-call(f32[128,128]{1,0:T(8,128)S(1)} %bitcast.26, f32[105,4,512]{2,1,0:T(4,128)S(1)} %bitcast.25, f32[105,4,512]{2,1,0:T(4,128)S(1)} %get-tuple-element.8.image_ref, f32[105,4,512]{2,1,0:T(4,128)S(1)} %get-tuple-element.9.second_ref), custom_call_target="tpu_custom_call" | custom-call | tf_op jit(solution)/shard_map/finish/pallas_call | solution.py:317
  (30 shorter events, 0.1 us)
Async XLA Ops:
  0.6 10.8 %copy-start.14 = (f32[5,4,512]{2,1,0:T(4,128)S(1)}, f32[5,4,512]{2,1,0:T(4,128)}, u32[]{:S(2)}) copy-start(f32[5,4,512]{2,1,0:T(4,128)} %param.7) | copy-start | bytes 122884
  0.6 10.8 %copy-start.16 = (f32[4,512]{1,0:T(4,128)S(1)}, f32[4,512]{1,0:T(4,128)}, u32[]{:S(2)}) copy-start(f32[4,512]{1,0:T(4,128)} %param.6) | copy-start | bytes 24580
  0.7 10.8 %copy-start = (f32[3,35,4,512]{3,2,1,0:T(4,128)S(1)}, f32[3,35,4,512]{3,2,1,0:T(4,128)}, u32[]{:S(2)}) copy-start(f32[3,35,4,512]{3,2,1,0:T(4,128)} %param.5) | copy-start | bytes 2580484
  0.7 7.8 %copy-start.15 = (f32[13]{0:T(128)S(1)}, f32[13]{0:T(128)}, u32[]{:S(2)}) copy-start(f32[13]{0:T(128)} %param.8) | copy-start | bytes 160
  2.0 8.2 %collective-permute-start.1 = (f32[111,4,64]{2,1,0:T(4,128)S(1)}, f32[111,4,64]{2,1,0:T(4,128)S(1)}, u32[]{:S(2)}, u32[]{:S(2)}) collective-permute-start(f32[111,4,64]{2,1,0:T(4,128)S(1)} %get-tuple-element.14), channel_id=1, source_target_pairs={{1,0},{2,1},{3,2},{4,3},{5,4},{6,5},{7,6},{8,7},{9,8},{10,9},{11,1... | collective-permute-start | bytes 341000 | tf_op jit(solution)/shard_map/ppermute | solution.py:269
  5.4 6.0 %collective-permute-start = (f32[111,4,64]{2,1,0:T(4,128)S(1)}, f32[111,4,64]{2,1,0:T(4,128)S(1)}, u32[]{:S(2)}, u32[]{:S(2)}) collective-permute-start(f32[111,4,64]{2,1,0:T(4,128)S(1)} %get-tuple-element.15), channel_id=1, source_target_pairs={{0,1},{1,2},{2,3},{3,4},{4,5},{5,6},{6,7},{7,8},{8,9},{9,10},{10,1... | collective-permute-start | bytes 341000 | tf_op jit(solution)/shard_map/ppermute | solution.py:269
  11.8 14.4 %copy-start.1 = (pred[256,384]{1,0:T(32,128)(4,1)S(1)}, pred[256,384]{1,0:T(32,128)(4,1)}, u32[]{:S(2)}) copy-start(pred[256,384]{1,0:T(32,128)(4,1)} %constant.62) | copy-start | bytes 294916
  11.8 14.4 %copy-start.2 = (pred[256,384]{1,0:T(32,128)(4,1)S(1)}, pred[256,384]{1,0:T(32,128)(4,1)}, u32[]{:S(2)}) copy-start(pred[256,384]{1,0:T(32,128)(4,1)} %constant.61) | copy-start | bytes 294916
  11.8 14.4 %copy-start.3 = (pred[256,384]{1,0:T(32,128)(4,1)S(1)}, pred[256,384]{1,0:T(32,128)(4,1)}, u32[]{:S(2)}) copy-start(pred[256,384]{1,0:T(32,128)(4,1)} %constant.60) | copy-start | bytes 294916
  11.8 14.4 %copy-start.4 = (pred[256,384]{1,0:T(32,128)(4,1)S(1)}, pred[256,384]{1,0:T(32,128)(4,1)}, u32[]{:S(2)}) copy-start(pred[256,384]{1,0:T(32,128)(4,1)} %constant.59) | copy-start | bytes 294916
  11.8 14.4 %copy-start.5 = (pred[256,384]{1,0:T(32,128)(4,1)S(1)}, pred[256,384]{1,0:T(32,128)(4,1)}, u32[]{:S(2)}) copy-start(pred[256,384]{1,0:T(32,128)(4,1)} %constant.58) | copy-start | bytes 294916
  11.8 14.4 %copy-start.6 = (pred[256,384]{1,0:T(32,128)(4,1)S(1)}, pred[256,384]{1,0:T(32,128)(4,1)}, u32[]{:S(2)}) copy-start(pred[256,384]{1,0:T(32,128)(4,1)} %constant.57) | copy-start | bytes 294916
  11.8 14.4 %copy-start.7 = (pred[256,384]{1,0:T(32,128)(4,1)S(1)}, pred[256,384]{1,0:T(32,128)(4,1)}, u32[]{:S(2)}) copy-start(pred[256,384]{1,0:T(32,128)(4,1)} %constant.56) | copy-start | bytes 294916
  11.8 14.4 %copy-start.8 = (pred[256,384]{1,0:T(32,128)(4,1)S(1)}, pred[256,384]{1,0:T(32,128)(4,1)}, u32[]{:S(2)}) copy-start(pred[256,384]{1,0:T(32,128)(4,1)} %constant.55) | copy-start | bytes 294916
  11.9 14.4 %copy-start.9 = (pred[256,384]{1,0:T(32,128)(4,1)S(1)}, pred[256,384]{1,0:T(32,128)(4,1)}, u32[]{:S(2)}) copy-start(pred[256,384]{1,0:T(32,128)(4,1)} %constant.54) | copy-start | bytes 294916
  11.9 14.4 %copy-start.10 = (pred[256,384]{1,0:T(32,128)(4,1)S(1)}, pred[256,384]{1,0:T(32,128)(4,1)}, u32[]{:S(2)}) copy-start(pred[256,384]{1,0:T(32,128)(4,1)} %constant.53) | copy-start | bytes 294916
  11.9 14.4 %copy-start.11 = (pred[256,384]{1,0:T(32,128)(4,1)S(1)}, pred[256,384]{1,0:T(32,128)(4,1)}, u32[]{:S(2)}) copy-start(pred[256,384]{1,0:T(32,128)(4,1)} %constant.52) | copy-start | bytes 294916
  11.9 14.4 %copy-start.12 = (pred[256,384]{1,0:T(32,128)(4,1)S(1)}, pred[256,384]{1,0:T(32,128)(4,1)}, u32[]{:S(2)}) copy-start(pred[256,384]{1,0:T(32,128)(4,1)} %constant.51) | copy-start | bytes 294916
  11.9 14.4 %copy-start.13 = (pred[256,384]{1,0:T(32,128)(4,1)S(1)}, pred[256,384]{1,0:T(32,128)(4,1)}, u32[]{:S(2)}) copy-start(pred[256,384]{1,0:T(32,128)(4,1)} %constant.50) | copy-start | bytes 294916
  12.4 15.1 %collective-permute-start.3 = (f32[111,2,640]{2,1,0:T(2,128)S(1)}, f32[111,2,640]{2,1,0:T(2,128)S(1)}, u32[]{:S(2)}, u32[]{:S(2)}) collective-permute-start(f32[111,2,640]{2,1,0:T(2,128)S(1)} %get-tuple-element.12), channel_id=1, source_target_pairs={{0,16},{16,32},{32,48},{48,64},{64,80},{80,96},{96,112},{1,17},{17... | collective-permute-start | bytes 1704968 | tf_op jit(solution)/shard_map/ppermute | solution.py:269
  16.0 14.8 %collective-permute-start.2 = (f32[111,2,640]{2,1,0:T(2,128)S(1)}, f32[111,2,640]{2,1,0:T(2,128)S(1)}, u32[]{:S(2)}, u32[]{:S(2)}) collective-permute-start(f32[111,2,640]{2,1,0:T(2,128)S(1)} %get-tuple-element.13), channel_id=1, source_target_pairs={{16,0},{32,16},{48,32},{64,48},{80,64},{96,80},{112,96},{17,1},{33... | collective-permute-start | bytes 1704968 | tf_op jit(solution)/shard_map/ppermute | solution.py:269
where the time goes:
time: 77.2 us; the launch traced here: 76.8 us
  blocking collectives  23.5 us (30%)
  Pallas kernels  22.5 us (29%)
  starting transfers between devices  11.3 us (15%)
  between operations  9.12 us (12%)
  waiting for transfers between devices  5.56 us (7%)
  other arithmetic  3.52 us (5%)
  local copies, waits for them, and re-layouts  1.26 us (2%)
    all_to_all x1, blocking collectives, per_device(): sums = lax.all_to_all(sums, ('down', 'cross'), 0, 0, tiled=True)  23.5 us
    pallas_call x1, Pallas kernels, per_device(): pl.pallas_call(functools.partial(operator_kernel, chunks), out_shape=(jax...  21 us
    ppermute x4, starting transfers between devices, shift(): lax.ppermute(value, axis, [(i, i + by) for i in range(size) if 0 <= i + b...  11.3 us
    ppermute x4, waiting for transfers between devices, shift(): lax.ppermute(value, axis, [(i, i + by) for i in range(size) if 0 <= i + b...  5.56 us
    pallas_call x1, Pallas kernels, per_device(): pl.pallas_call(finish_kernel, out_shape=(jax.ShapeDtypeStruct(own.shape,...  1.58 us
  transfers between devices with their start and end apart: 4, of which 3 were waited for; matrix products, arithmetic and copies ran while one was open for 3% of the time, Pallas kernels for 0%

commit v1 on v0

--- a/solution.py
+++ b/solution.py
@@ -77,15 +77,17 @@
 SLOTS = tap_slots()
 
 
-def stencil_matrix(weights):
-    slots = jnp.asarray(SLOTS)
+def matrix_kernel(weights_ref, slots_ref, matrix_ref):
+    slots = slots_ref[...]
     full = jnp.zeros(slots.shape, jnp.float32)
     for number in range(13):
-        full = jnp.where(slots == number, 0.5 * weights[number], full)
-    high = lax.reduce_precision(full, 8, 7)
-    low = (full - high).astype(jnp.bfloat16)
-    high = high.astype(jnp.bfloat16)
-    return jnp.concatenate([high, high, low], axis=0)
+        full = jnp.where(slots == number, 0.5 * weights_ref[number], full)
+    high = full.astype(jnp.bfloat16)
+    low = (full - high.astype(jnp.float32)).astype(jnp.bfloat16)
+    rows = slots.shape[0]
+    matrix_ref[:rows] = high
+    matrix_ref[rows : 2 * rows] = high
+    matrix_ref[2 * rows :] = low
 
 
 def mix(table, load, mode, total):
@@ -124,7 +126,8 @@
 
 def operator_kernel(
     chunks,
-    own_ref, extra_ref, left_ref, right_ref, upper_ref, lower_ref, matrix_ref, sum_ref,
+    own_ref, extra_ref, left_ref, right_ref, upper_ref, lower_ref, upper_corner_ref, lower_corner_ref,
+    matrix_ref, weights_ref,
     image_ref, second_ref, sums_ref,
     field, field_high, field_low, grown, grown_high, grown_low,
     first_near, second_near, image, image_high, image_low, coef_table, diag_table,
@@ -136,9 +139,10 @@
         field[k, FIELDS : STIFF + 1, 0:ROWS, :] = extra_ref[:, :, lanes]
     field[edge, : STIFF + 1, 0:ROWS, :] = jnp.concatenate([right_ref[...], left_ref[...]], axis=2)
     for k in range(chunks):
-        lanes = pl.ds(k * LANES, LANES)
-        field[k, : STIFF + 1, ROWS : ROWS + 2, :] = upper_ref[:, :, lanes]
-        field[k, : STIFF + 1, ROWS + 2 : ROWS + 4, :] = lower_ref[:, :, lanes]
+        lanes = pl.ds(k * LANES if k < edge else 0, LANES)
+        upper, lower = (upper_ref, lower_ref) if k < edge else (upper_corner_ref, lower_corner_ref)
+        field[k, : STIFF + 1, ROWS : ROWS + 2, :] = upper[:, :, lanes]
+        field[k, : STIFF + 1, ROWS + 2 : ROWS + 4, :] = lower[:, :, lanes]
         field[k, STIFF + 1] = jnp.zeros((8, LANES), jnp.float32)
         image[k, FIELDS] = jnp.zeros((8, LANES), jnp.float32)
     grown[FIELDS] = jnp.zeros((8, LANES), jnp.float32)
@@ -171,7 +175,7 @@
     def first(k):
         stencil(field_high, field_low, k, chunks, matrix_ref, first_near)
         stencil(grown_high, grown_low, k, chunks, matrix_ref, second_near)
-        weight_sum = sum_ref[0]
+        weight_sum = sum(weights_ref[number] for number in range(13))
         fill(
             diag_table,
             k,
@@ -278,14 +282,22 @@
     all_fields = jnp.concatenate([own, extra], axis=0)
     right = shift(all_fields[:, :, :WIDE], "cross", -1)
     left = shift(all_fields[:, :, columns - WIDE :], "cross", 1)
-    wide = jnp.concatenate([all_fields, right, left], axis=2)
-    upper = shift(wide[:, :2], "down", -1)
-    lower = shift(wide[:, ROWS - 2 :], "down", 1)
-    matrix = stencil_matrix(stencil_weights)
-    weight_sum = jnp.sum(stencil_weights).reshape(1)
+    upper = shift(all_fields[:, :2], "down", -1)
+    lower = shift(all_fields[:, ROWS - 2 :], "down", 1)
+    rims = jnp.concatenate([right, left], axis=2)
+    upper_corner = shift(rims[:, :2], "down", -1)
+    lower_corner = shift(rims[:, ROWS - 2 :], "down", 1)
     vmem = pl.BlockSpec(memory_space=pltpu.VMEM)
     count = FIELDS + 1
     f32, bf16 = jnp.float32, jnp.bfloat16
+    smem = pl.BlockSpec(memory_space=pltpu.SMEM)
+    matrix = pl.pallas_call(
+        matrix_kernel,
+        out_shape=jax.ShapeDtypeStruct((3 * SLOTS.shape[0], SLOTS.shape[1]), bf16),
+        in_specs=[smem, vmem],
+        out_specs=vmem,
+        name="matrix",
+    )(stencil_weights, jnp.asarray(SLOTS))
     image, second, sums = pl.pallas_call(
         functools.partial(operator_kernel, chunks),
         out_shape=(
@@ -293,7 +305,7 @@
             jax.ShapeDtypeStruct(own.shape, f32),
             jax.ShapeDtypeStruct((devices, LANES), f32),
         ),
-        in_specs=[vmem] * 7 + [pl.BlockSpec(memory_space=pltpu.SMEM)],
+        in_specs=[vmem] * 9 + [smem],
         out_specs=(vmem, vmem, vmem),
         scratch_shapes=[
             pltpu.VMEM((chunks, STIFF + 2, 8, LANES), f32),
@@ -312,7 +324,7 @@
         ],
         compiler_params=pltpu.CompilerParams(vmem_limit_bytes=48 * 1024 * 1024),
         name="operator",
-    )(own, extra, left, right, upper, lower, matrix, weight_sum)
+    )(own, extra, left, right, upper, lower, upper_corner, lower_corner, matrix, stencil_weights)
     sums = lax.all_to_all(sums, ("down", "cross"), 0, 0, tiled=True)
     solution_field, residual = pl.pallas_call(
         finish_kernel,

time: 77.2 us -> 84.6 us (1.096)
  blocking collectives: 23.5 us -> 32.3 us
  between operations: 9.12 us -> 0.76 us
  starting transfers between devices: 11.3 us -> 17.4 us
  Pallas kernels: 22.5 us -> 24.7 us
  other arithmetic: 3.52 us -> 2.35 us
    all_to_all x1, blocking collectives: 23.5 us -> 32.3 us  [per_device(): sums = lax.all_to_all(sums, ('down', 'cross'), 0, 0, tiled=True)]
    ppermute x4 -> x6, starting transfers between devices: 11.3 us -> 17.4 us  [shift(): lax.ppermute(value, axis, [(i, i + by) for i in range(size) if 0 <= i + b...]
    pallas_call x0 -> x1, Pallas kernels: none -> 2.21 us  [per_device(): pl.pallas_call(matrix_kernel, out_shape=jax.ShapeDtypeStruct((3 * SLOTS.s...]
    convert_element_type x2 -> x0, other arithmetic: 1.08 us -> none  [the longest x1 0.55 us: stencil_matrix(): low = (full - high).astype(jnp.bfloat16)]
    unnamed x34 -> x10, local copies, waits for them, and re-layouts: 0.11 us -> 1.08 us
    ppermute x4 -> x6, waiting for transfers between devices: 5.56 us -> 5.06 us  [shift(): lax.ppermute(value, axis, [(i, i + by) for i in range(size) if 0 <= i + b...]
  transfers between devices with their start and end apart: 4 -> 6, of which waited for: 3 -> 3; matrix products, arithmetic and copies ran while one was open for 3% -> 1% of each run, Pallas kernels for 0% -> 3%
where the time goes in v1:
time: 84.6 us; the launch traced here: 84.2 us
  blocking collectives  32.3 us (38%)
  Pallas kernels  24.7 us (29%)
  starting transfers between devices  17.4 us (21%)
  waiting for transfers between devices  5.06 us (6%)
  other arithmetic  2.35 us (3%)
  local copies, waits for them, and re-layouts  1.62 us (2%)
    all_to_all x1, blocking collectives, per_device(): sums = lax.all_to_all(sums, ('down', 'cross'), 0, 0, tiled=True)  32.3 us
    pallas_call x1, Pallas kernels, per_device(): pl.pallas_call(functools.partial(operator_kernel, chunks), out_shape=(jax...  20.9 us
    ppermute x6, starting transfers between devices, shift(): lax.ppermute(value, axis, [(i, i + by) for i in range(size) if 0 <= i + b...  17.4 us
    ppermute x6, waiting for transfers between devices, shift(): lax.ppermute(value, axis, [(i, i + by) for i in range(size) if 0 <= i + b...  5.06 us
    pallas_call x1, Pallas kernels, per_device(): pl.pallas_call(matrix_kernel, out_shape=jax.ShapeDtypeStruct((3 * SLOTS.s...  2.21 us
  transfers between devices with their start and end apart: 6, of which 3 were waited for; matrix products, arithmetic and copies ran while one was open for 1% of the time, Pallas kernels for 3%

profile of v1, /device:TPU:1, one launch (start us, length us, event | category | flops | bytes accessed | tf_op | source)
XLA Modules:
  0.0 84.2 jit_solution(3586741024524995010)
XLA Ops:
  0.6 1.4 %pad_maximum_fusion = f32[111,4,512]{2,1,0:T(4,128)S(1)} fusion(f32[1,4,512]{2,1,0:T(4,128)} %bitcast.13, f32[5,4,512]{2,1,0:T(4,128)} %param.7, f32[105,4,512]{2,1,0:T(4,128)} %bitcast.8), kind=kLoop, calls=%fused_computation | loop fusion | flops 454656 | bytes 1818624 | tf_op jit(solution)/shard_map/concatenate | solution.py:282
  2.0 0.4 fusion.1
  2.4 4.4 %collective-permute-start.3 = (f32[111,2,512]{2,1,0:T(2,128)S(1)}, f32[111,2,512]{2,1,0:T(2,128)S(1)}, u32[]{:S(2)}, u32[]{:S(2)}) collective-permute-start(f32[111,2,512]{2,1,0:T(2,128)S(1)} %get-tuple-element.12), channel_id=1, source_target_pairs={{0,16},{16,32},{32,48},{48,64},{64,80},{80,96},{96,112},{1,17},{17... | collective-permute-start | bytes 1363976 | tf_op jit(solution)/shard_map/ppermute | solution.py:273
  6.8 1.3 %collective-permute-start.2 = (f32[111,2,512]{2,1,0:T(2,128)S(1)}, f32[111,2,512]{2,1,0:T(2,128)S(1)}, u32[]{:S(2)}, u32[]{:S(2)}) collective-permute-start(f32[111,2,512]{2,1,0:T(2,128)S(1)} %get-tuple-element.13), channel_id=1, source_target_pairs={{16,0},{32,16},{48,32},{64,48},{80,64},{96,80},{112,96},{17,1},{33... | collective-permute-start | bytes 1363976 | tf_op jit(solution)/shard_map/ppermute | solution.py:273
  8.1 0.2 fusion.2
  8.3 2.9 %collective-permute-start.1 = (f32[111,4,64]{2,1,0:T(4,128)S(1)}, f32[111,4,64]{2,1,0:T(4,128)S(1)}, u32[]{:S(2)}, u32[]{:S(2)}) collective-permute-start(f32[111,4,64]{2,1,0:T(4,128)S(1)} %get-tuple-element.14), channel_id=1, source_target_pairs={{1,0},{2,1},{3,2},{4,3},{5,4},{6,5},{7,6},{8,7},{9,8},{10,9},{11,1... | collective-permute-start | bytes 341000 | tf_op jit(solution)/shard_map/ppermute | solution.py:273
  11.2 0.0 copy-start
  11.2 3.1 %collective-permute-start = (f32[111,4,64]{2,1,0:T(4,128)S(1)}, f32[111,4,64]{2,1,0:T(4,128)S(1)}, u32[]{:S(2)}, u32[]{:S(2)}) collective-permute-start(f32[111,4,64]{2,1,0:T(4,128)S(1)} %get-tuple-element.15), channel_id=1, source_target_pairs={{0,1},{1,2},{2,3},{3,4},{4,5},{5,6},{6,7},{7,8},{8,9},{9,10},{10,1... | collective-permute-start | bytes 341000 | tf_op jit(solution)/shard_map/ppermute | solution.py:273
  14.3 1.9 %collective-permute-done.1.right_ref = f32[111,4,64]{2,1,0:T(4,128)S(1)} collective-permute-done((f32[111,4,64]{2,1,0:T(4,128)S(1)}, f32[111,4,64]{2,1,0:T(4,128)S(1)}, u32[]{:S(2)}, u32[]{:S(2)}) %collective-permute-start.1) | collective-permute-done | bytes 113696 | tf_op jit(solution)/shard_map/ppermute | solution.py:273
  16.2 1.0 %collective-permute-done.left_ref = f32[111,4,64]{2,1,0:T(4,128)S(1)} collective-permute-done((f32[111,4,64]{2,1,0:T(4,128)S(1)}, f32[111,4,64]{2,1,0:T(4,128)S(1)}, u32[]{:S(2)}, u32[]{:S(2)}) %collective-permute-start) | collective-permute-done | bytes 113696 | tf_op jit(solution)/shard_map/ppermute | solution.py:273
  17.2 0.9 %pad_maximum_fusion.1 = (f32[111,2,128]{2,1,0:T(2,128)}, f32[111,2,128]{2,1,0:T(2,128)S(1)}) fusion(f32[111,4,64]{2,1,0:T(4,128)S(1)} %collective-permute-done.left_ref, f32[111,4,64]{2,1,0:T(4,128)S(1)} %collective-permute-done.1.right_ref), kind=kLoop, calls=%fused_computation.4 | loop fusion | flops 56832 | bytes 454656 | tf_op jit(solution)/shard_map/concatenate | solution.py:287
  18.2 4.3 %collective-permute-start.5 = (f32[111,2,128]{2,1,0:T(2,128)}, f32[111,2,128]{2,1,0:T(2,128)S(1)}, u32[]{:S(2)}, u32[]{:S(2)}) collective-permute-start(f32[111,2,128]{2,1,0:T(2,128)} %get-tuple-element.16), channel_id=1, source_target_pairs={{0,16},{16,32},{32,48},{48,64},{64,80},{80,96},{96,112},{1,17},{17... | collective-permute-start | bytes 341000 | tf_op jit(solution)/shard_map/ppermute | solution.py:273
  22.4 0.0 copy-start.3
  22.5 0.0 copy-start.4
  22.5 1.4 %collective-permute-start.4 = (f32[111,2,128]{2,1,0:T(2,128)S(1)}, f32[111,2,128]{2,1,0:T(2,128)S(1)}, u32[]{:S(2)}, u32[]{:S(2)}) collective-permute-start(f32[111,2,128]{2,1,0:T(2,128)S(1)} %get-tuple-element.17), channel_id=1, source_target_pairs={{16,0},{32,16},{48,32},{64,48},{80,64},{96,80},{112,96},{17,1},{33... | collective-permute-start | bytes 341000 | tf_op jit(solution)/shard_map/ppermute | solution.py:273
  23.9 2.2 %matrix.1.matrix_ref = bf16[768,384]{1,0:T(8,128)(2,1)} custom-call(f32[13]{0:T(128)} %weights_ref.3, s32[256,384]{1,0:T(8,128)} %constant.2.clone.slots_ref), custom_call_target="tpu_custom_call" | custom-call | tf_op jit(solution)/shard_map/matrix/pallas_call | solution.py:294
  26.1 0.0 collective-permute-done.5.lower_corner_ref
  26.2 2.1 %collective-permute-done.4.upper_corner_ref = f32[111,2,128]{2,1,0:T(2,128)S(1)} collective-permute-done((f32[111,2,128]{2,1,0:T(2,128)S(1)}, f32[111,2,128]{2,1,0:T(2,128)S(1)}, u32[]{:S(2)}, u32[]{:S(2)}) %collective-permute-start.4) | collective-permute-done | bytes 113696 | tf_op jit(solution)/shard_map/ppermute | solution.py:273
  28.3 0.0 collective-permute-done.3.lower_ref
  28.3 0.0 copy-start.1
  28.3 1.1 %copy-done.1 = bf16[768,384]{1,0:T(8,128)(2,1)S(1)} copy-done((bf16[768,384]{1,0:T(8,128)(2,1)S(1)}, bf16[768,384]{1,0:T(8,128)(2,1)}, u32[]{:S(2)}) %copy-start.1) | copy-done | bytes 589848
  29.4 20.9 %operator.1 = (f32[105,4,512]{2,1,0:T(4,128)S(1)}, f32[105,4,512]{2,1,0:T(4,128)S(1)}, f32[128,128]{1,0:T(8,128)S(1)}) custom-call(f32[105,4,512]{2,1,0:T(4,128)S(1)} %bitcast.9, f32[6,4,512]{2,1,0:T(4,128)S(1)} %pad_maximum_fusion.2.extra_ref, f32[111,4,64]{2,1,0:T(4,128)S(1)} %collective-permute-done.left_ref, ...), custom_call_target="tpu_custom_call" | custom-call | tf_op jit(solution)/shard_map/operator/pallas_call | solution.py:301
  50.3 32.3 %all_to_all.11 = f32[128,1,128]{2,1,0:T(1,128)S(1)} all-to-all(f32[128,1,128]{2,1,0:T(1,128)S(1)} %bitcast.12), channel_id=1, replica_groups=mesh['down'=8,'cross'=16] {'down','cross'}, dimensions={0} | all-to-all | bytes 131072 | tf_op jit(solution)/shard_map/all_to_all | solution.py:328
  82.6 1.6 %finish.1 = (f32[105,4,512]{2,1,0:T(4,128)}, f32[105,4,512]{2,1,0:T(4,128)}) custom-call(f32[128,128]{1,0:T(8,128)S(1)} %bitcast.11, f32[105,4,512]{2,1,0:T(4,128)S(1)} %bitcast.10, f32[105,4,512]{2,1,0:T(4,128)S(1)} %get-tuple-element.8.image_ref, f32[105,4,512]{2,1,0:T(4,128)S(1)} %get-tuple-element.9.second_ref), custom_call_target="tpu_custom_call" | custom-call | tf_op jit(solution)/shard_map/finish/pallas_call | solution.py:329
  (7 shorter events, 0.0 us)
Async XLA Ops:
  2.4 25.9 %collective-permute-start.3 = (f32[111,2,512]{2,1,0:T(2,128)S(1)}, f32[111,2,512]{2,1,0:T(2,128)S(1)}, u32[]{:S(2)}, u32[]{:S(2)}) collective-permute-start(f32[111,2,512]{2,1,0:T(2,128)S(1)} %get-tuple-element.12), channel_id=1, source_target_pairs={{0,16},{16,32},{32,48},{48,64},{64,80},{80,96},{96,112},{1,17},{17... | collective-permute-start | bytes 1363976 | tf_op jit(solution)/shard_map/ppermute | solution.py:273
  6.8 21.5 %collective-permute-start.2 = (f32[111,2,512]{2,1,0:T(2,128)S(1)}, f32[111,2,512]{2,1,0:T(2,128)S(1)}, u32[]{:S(2)}, u32[]{:S(2)}) collective-permute-start(f32[111,2,512]{2,1,0:T(2,128)S(1)} %get-tuple-element.13), channel_id=1, source_target_pairs={{16,0},{32,16},{48,32},{64,48},{80,64},{96,80},{112,96},{17,1},{33... | collective-permute-start | bytes 1363976 | tf_op jit(solution)/shard_map/ppermute | solution.py:273
  8.3 7.9 %collective-permute-start.1 = (f32[111,4,64]{2,1,0:T(4,128)S(1)}, f32[111,4,64]{2,1,0:T(4,128)S(1)}, u32[]{:S(2)}, u32[]{:S(2)}) collective-permute-start(f32[111,4,64]{2,1,0:T(4,128)S(1)} %get-tuple-element.14), channel_id=1, source_target_pairs={{1,0},{2,1},{3,2},{4,3},{5,4},{6,5},{7,6},{8,7},{9,8},{10,9},{11,1... | collective-permute-start | bytes 341000 | tf_op jit(solution)/shard_map/ppermute | solution.py:273
  11.2 17.1 %copy-start = (f32[3,35,4,512]{3,2,1,0:T(4,128)S(1)}, f32[3,35,4,512]{3,2,1,0:T(4,128)}, u32[]{:S(2)}) copy-start(f32[3,35,4,512]{3,2,1,0:T(4,128)} %param.5) | copy-start | bytes 2580484
  11.2 6.1 %collective-permute-start = (f32[111,4,64]{2,1,0:T(4,128)S(1)}, f32[111,4,64]{2,1,0:T(4,128)S(1)}, u32[]{:S(2)}, u32[]{:S(2)}) collective-permute-start(f32[111,4,64]{2,1,0:T(4,128)S(1)} %get-tuple-element.15), channel_id=1, source_target_pairs={{0,1},{1,2},{2,3},{3,4},{4,5},{5,6},{6,7},{7,8},{8,9},{9,10},{10,1... | collective-permute-start | bytes 341000 | tf_op jit(solution)/shard_map/ppermute | solution.py:273
  18.2 8.0 %collective-permute-start.5 = (f32[111,2,128]{2,1,0:T(2,128)}, f32[111,2,128]{2,1,0:T(2,128)S(1)}, u32[]{:S(2)}, u32[]{:S(2)}) collective-permute-start(f32[111,2,128]{2,1,0:T(2,128)} %get-tuple-element.16), channel_id=1, source_target_pairs={{0,16},{16,32},{32,48},{48,64},{64,80},{80,96},{96,112},{1,17},{17... | collective-permute-start | bytes 341000 | tf_op jit(solution)/shard_map/ppermute | solution.py:273
  22.4 3.7 %copy-start.3 = (f32[5,4,512]{2,1,0:T(4,128)S(1)}, f32[5,4,512]{2,1,0:T(4,128)}, u32[]{:S(2)}) copy-start(f32[5,4,512]{2,1,0:T(4,128)} %param.7) | copy-start | bytes 122884
  22.5 3.7 %copy-start.4 = (f32[4,512]{1,0:T(4,128)S(1)}, f32[4,512]{1,0:T(4,128)}, u32[]{:S(2)}) copy-start(f32[4,512]{1,0:T(4,128)} %param.6) | copy-start | bytes 24580
  22.5 5.8 %collective-permute-start.4 = (f32[111,2,128]{2,1,0:T(2,128)S(1)}, f32[111,2,128]{2,1,0:T(2,128)S(1)}, u32[]{:S(2)}, u32[]{:S(2)}) collective-permute-start(f32[111,2,128]{2,1,0:T(2,128)S(1)} %get-tuple-element.17), channel_id=1, source_target_pairs={{16,0},{32,16},{48,32},{64,48},{80,64},{96,80},{112,96},{17,1},{33... | collective-permute-start | bytes 341000 | tf_op jit(solution)/shard_map/ppermute | solution.py:273
  26.1 2.2 %copy-start.2 = (f32[13]{0:T(128)S(1)}, f32[13]{0:T(128)}, u32[]{:S(2)}) copy-start(f32[13]{0:T(128)} %weights_ref.3) | copy-start | bytes 160
  28.3 1.1 %copy-start.1 = (bf16[768,384]{1,0:T(8,128)(2,1)S(1)}, bf16[768,384]{1,0:T(8,128)(2,1)}, u32[]{:S(2)}) copy-start(bf16[768,384]{1,0:T(8,128)(2,1)} %matrix.1.matrix_ref) | copy-start | bytes 1769476

commit v2 on v1

--- a/solution.py
+++ b/solution.py
@@ -16,7 +16,8 @@
 COMPS = 3
 MODES = 35
 FIELDS = COMPS * MODES
-STIFF = FIELDS + TERMS
+EXTRAS = TERMS + 1
+GROUPS = (1, 2)
 ROWS = 4
 LANES = 128
 WIDE = 64
@@ -125,27 +126,39 @@
 
 
 def operator_kernel(
-    chunks,
-    own_ref, extra_ref, left_ref, right_ref, upper_ref, lower_ref, upper_corner_ref, lower_corner_ref,
-    matrix_ref, weights_ref,
+    chunks, comps, cross_at, last,
+    own_ref, extra_ref, left_ref, right_ref, upper_ref, lower_ref, upper_extra_ref, lower_extra_ref,
+    matrix_ref, weights_ref, before_ref,
     image_ref, second_ref, sums_ref,
     field, field_high, field_low, grown, grown_high, grown_low,
     first_near, second_near, image, image_high, image_low, coef_table, diag_table,
 ):
     edge = chunks - 1
-    for k in range(edge):
+    fields = comps * MODES
+    stiff_at = fields + TERMS
+    own, extra = pl.ds(0, fields), pl.ds(fields, EXTRAS)
+    cross_own, cross_extra = pl.ds(cross_at, fields), pl.ds(MODES, EXTRAS)
+    for k in range(chunks):
         lanes = pl.ds(k * LANES, LANES)
-        field[k, :FIELDS, 0:ROWS, :] = own_ref[:, :, lanes]
-        field[k, FIELDS : STIFF + 1, 0:ROWS, :] = extra_ref[:, :, lanes]
-    field[edge, : STIFF + 1, 0:ROWS, :] = jnp.concatenate([right_ref[...], left_ref[...]], axis=2)
-    for k in range(chunks):
-        lanes = pl.ds(k * LANES if k < edge else 0, LANES)
-        upper, lower = (upper_ref, lower_ref) if k < edge else (upper_corner_ref, lower_corner_ref)
-        field[k, : STIFF + 1, ROWS : ROWS + 2, :] = upper[:, :, lanes]
-        field[k, : STIFF + 1, ROWS + 2 : ROWS + 4, :] = lower[:, :, lanes]
-        field[k, STIFF + 1] = jnp.zeros((8, LANES), jnp.float32)
-        image[k, FIELDS] = jnp.zeros((8, LANES), jnp.float32)
-    grown[FIELDS] = jnp.zeros((8, LANES), jnp.float32)
+        if k < edge:
+            field[k, own, 0:ROWS, :] = own_ref[:, :, lanes]
+            field[k, extra, 0:ROWS, :] = extra_ref[:, :, lanes]
+        else:
+            for to, here in ((own, cross_own), (extra, cross_extra)):
+                field[k, to, 0:ROWS, :] = jnp.concatenate([right_ref[here], left_ref[here]], axis=2)
+        for first_row, ref, extra_ref_here in (
+            (ROWS, upper_ref, upper_extra_ref),
+            (ROWS + 2, lower_ref, lower_extra_ref),
+        ):
+            rows = pl.ds(first_row, 2)
+            field[k, own, rows, :] = ref[pl.ds(0, fields), :, lanes]
+            field[k, extra, rows, :] = extra_ref_here[pl.ds(MODES, EXTRAS), :, lanes]
+        for spare in range(fields + EXTRAS, field.shape[1]):
+            field[k, spare] = jnp.zeros((8, LANES), jnp.float32)
+        for spare in range(fields, image.shape[1]):
+            image[k, spare] = jnp.zeros((8, LANES), jnp.float32)
+    for spare in range(fields, grown.shape[0]):
+        grown[spare] = jnp.zeros((8, LANES), jnp.float32)
 
     def fill(table, k, values):
         table[k, 0] = values[0]
@@ -158,10 +171,10 @@
 
     @pl.loop(0, chunks)
     def grow(k):
-        fill(coef_table, k, [field[k, FIELDS + term] for term in range(TERMS)])
+        fill(coef_table, k, [field[k, fields + term] for term in range(TERMS)])
         table = load_table(coef_table, k)
 
-        @pl.loop(0, COMPS)
+        @pl.loop(0, comps)
         def each(comp):
             base = comp * MODES
             for mode in range(MODES):
@@ -180,16 +193,16 @@
             diag_table,
             k,
             [
-                field[k, FIELDS + term] * weight_sum + first_near[FIELDS + term]
+                field[k, fields + term] * weight_sum + first_near[fields + term]
                 for term in range(TERMS)
             ],
         )
         coef = load_table(coef_table, k)
         diag = load_table(diag_table, k)
-        stiff = field[k, STIFF]
+        stiff = field[k, stiff_at]
         inside = stiff > 0.0
 
-        @pl.loop(0, COMPS)
+        @pl.loop(0, comps)
         def each(comp):
             base = comp * MODES
             for mode in range(MODES):
@@ -203,7 +216,7 @@
     def regrow(k):
         table = load_table(coef_table, k)
 
-        @pl.loop(0, COMPS)
+        @pl.loop(0, comps)
         def each(comp):
             base = comp * MODES
             for mode in range(MODES):
@@ -213,7 +226,7 @@
         split(grown[...], grown_high, grown_low, k)
         split(image[k], image_high, image_low, k)
 
-    third_near = first_near.at[pl.ds(0, FIELDS + 1)]
+    third_near = first_near.at[pl.ds(0, image.shape[1])]
     zero = jnp.zeros((8, LANES), jnp.float32)
 
     def second(k, sums):
@@ -221,7 +234,7 @@
         stencil(grown_high, grown_low, k, chunks, matrix_ref, second_near)
         coef = load_table(coef_table, k)
         diag = load_table(diag_table, k)
-        stiff = field[k, STIFF]
+        stiff = field[k, stiff_at]
         lanes = pl.ds(pl.multiple_of(k * LANES, LANES), LANES)
 
         def each(comp, sums):
@@ -238,18 +251,24 @@
                 rr, rq, qq, qz = rr + start * start, rq + start * here, qq + here * here, qz + here * value
             return rr, rq, qq, qz
 
-        return lax.fori_loop(0, COMPS, each, sums)
+        return lax.fori_loop(0, comps, each, sums)
 
     sums = lax.fori_loop(0, edge, second, (zero, zero, zero, zero))
     inner = lax.broadcasted_iota(jnp.int32, (8, LANES), 0) < ROWS
-    lane = lax.broadcasted_iota(jnp.int32, sums_ref.shape, 1)
-    row = jnp.zeros(sums_ref.shape, jnp.float32)
-    for number, value in enumerate(sums):
-        row = jnp.where(lane == number, jnp.sum(jnp.where(inner, value, 0.0)), row)
-    sums_ref[...] = row
-
-
-def finish_kernel(sums_ref, start_ref, image_ref, second_ref, field_ref, residual_ref):
+    sums = [jnp.where(inner, value, 0.0) + before_ref[n] for n, value in enumerate(sums)]
+    if last:
+        lane = lax.broadcasted_iota(jnp.int32, sums_ref.shape, 1)
+        row = jnp.zeros(sums_ref.shape, jnp.float32)
+        for number, value in enumerate(sums):
+            row = jnp.where(lane == number, jnp.sum(value), row)
+        sums_ref[...] = row
+    else:
+        for number, value in enumerate(sums):
+            sums_ref[number] = value
+
+
+def finish_kernel(sums_ref, start_ref, *refs):
+    *parts, field_ref, residual_ref = refs
     total = jnp.sum(sums_ref[...], axis=0, keepdims=True)
     lane = lax.broadcasted_iota(jnp.int32, total.shape, 1)
     rr, rq, qq, qz = [
@@ -263,9 +282,13 @@
     later = fresh / curvature
     both = step + later * grow
     cross = later * step
-    start, image, second = start_ref[...], image_ref[...], second_ref[...]
-    field_ref[...] = both * start - cross * image
-    residual_ref[...] = start - both * image + cross * second
+    at = 0
+    for image_ref, second_ref in zip(parts[::2], parts[1::2]):
+        here = pl.ds(at, image_ref.shape[0])
+        at += image_ref.shape[0]
+        start, image, second = start_ref[here], image_ref[...], second_ref[...]
+        field_ref[here] = both * start - cross * image
+        residual_ref[here] = start - both * image + cross * second
 
 
 def shift(value, axis, by):
@@ -279,18 +302,13 @@
     devices = lax.axis_size("down") * lax.axis_size("cross")
     own = right_side.reshape(FIELDS, ROWS, columns)
     extra = jnp.concatenate([coefficients, stiffness[None]], axis=0)
-    all_fields = jnp.concatenate([own, extra], axis=0)
+    all_fields = jnp.concatenate([own[:MODES], extra, own[MODES:]], axis=0)
     right = shift(all_fields[:, :, :WIDE], "cross", -1)
     left = shift(all_fields[:, :, columns - WIDE :], "cross", 1)
-    upper = shift(all_fields[:, :2], "down", -1)
-    lower = shift(all_fields[:, ROWS - 2 :], "down", 1)
-    rims = jnp.concatenate([right, left], axis=2)
-    upper_corner = shift(rims[:, :2], "down", -1)
-    lower_corner = shift(rims[:, ROWS - 2 :], "down", 1)
+    wide = jnp.concatenate([all_fields, right, left], axis=2)
     vmem = pl.BlockSpec(memory_space=pltpu.VMEM)
-    count = FIELDS + 1
+    smem = pl.BlockSpec(memory_space=pltpu.SMEM)
     f32, bf16 = jnp.float32, jnp.bfloat16
-    smem = pl.BlockSpec(memory_space=pltpu.SMEM)
     matrix = pl.pallas_call(
         matrix_kernel,
         out_shape=jax.ShapeDtypeStruct((3 * SLOTS.shape[0], SLOTS.shape[1]), bf16),
@@ -298,42 +316,61 @@
         out_specs=vmem,
         name="matrix",
     )(stencil_weights, jnp.asarray(SLOTS))
-    image, second, sums = pl.pallas_call(
-        functools.partial(operator_kernel, chunks),
-        out_shape=(
-            jax.ShapeDtypeStruct(own.shape, f32),
-            jax.ShapeDtypeStruct(own.shape, f32),
-            jax.ShapeDtypeStruct((devices, LANES), f32),
-        ),
-        in_specs=[vmem] * 9 + [smem],
-        out_specs=(vmem, vmem, vmem),
-        scratch_shapes=[
-            pltpu.VMEM((chunks, STIFF + 2, 8, LANES), f32),
-            pltpu.VMEM((chunks, (STIFF + 2) * 8, LANES), bf16),
-            pltpu.VMEM((chunks, (STIFF + 2) * 8, LANES), bf16),
-            pltpu.VMEM((count, 8, LANES), f32),
-            pltpu.VMEM((chunks, count * 8, LANES), bf16),
-            pltpu.VMEM((chunks, count * 8, LANES), bf16),
-            pltpu.VMEM((STIFF + 2, 8, LANES), f32),
-            pltpu.VMEM((count, 8, LANES), f32),
-            pltpu.VMEM((chunks, count, 8, LANES), f32),
-            pltpu.VMEM((chunks, count * 8, LANES), bf16),
-            pltpu.VMEM((chunks, count * 8, LANES), bf16),
-            pltpu.VMEM((chunks, TABLE, 8, LANES), f32),
-            pltpu.VMEM((chunks, TABLE, 8, LANES), f32),
-        ],
-        compiler_params=pltpu.CompilerParams(vmem_limit_bytes=48 * 1024 * 1024),
-        name="operator",
-    )(own, extra, left, right, upper, lower, upper_corner, lower_corner, matrix, stencil_weights)
+    halos, begin = [], 0
+    for comps in GROUPS:
+        count = comps * MODES + (EXTRAS if begin == 0 else 0)
+        part = wide[begin : begin + count]
+        halos.append((begin, shift(part[:, :2], "down", -1), shift(part[:, ROWS - 2 :], "down", 1)))
+        begin += count
+    images, at = [], 0
+    sums = jnp.zeros((4, 8, LANES), f32)
+    for number, (comps, (cross_at, upper, lower)) in enumerate(zip(GROUPS, halos)):
+        last = number == len(GROUPS) - 1
+        fields = comps * MODES
+        here = own[at : at + fields]
+        at += fields
+        count = fields + fields % 2
+        wider = fields + EXTRAS + fields % 2
+        image, second, sums = pl.pallas_call(
+            functools.partial(operator_kernel, chunks, comps, cross_at, last),
+            out_shape=(
+                jax.ShapeDtypeStruct(here.shape, f32),
+                jax.ShapeDtypeStruct(here.shape, f32),
+                jax.ShapeDtypeStruct((devices, LANES) if last else sums.shape, f32),
+            ),
+            in_specs=[vmem] * 9 + [smem, vmem],
+            out_specs=(vmem, vmem, vmem),
+            scratch_shapes=[
+                pltpu.VMEM((chunks, wider, 8, LANES), f32),
+                pltpu.VMEM((chunks, wider * 8, LANES), bf16),
+                pltpu.VMEM((chunks, wider * 8, LANES), bf16),
+                pltpu.VMEM((count, 8, LANES), f32),
+                pltpu.VMEM((chunks, count * 8, LANES), bf16),
+                pltpu.VMEM((chunks, count * 8, LANES), bf16),
+                pltpu.VMEM((wider, 8, LANES), f32),
+                pltpu.VMEM((count, 8, LANES), f32),
+                pltpu.VMEM((chunks, count, 8, LANES), f32),
+                pltpu.VMEM((chunks, count * 8, LANES), bf16),
+                pltpu.VMEM((chunks, count * 8, LANES), bf16),
+                pltpu.VMEM((chunks, TABLE, 8, LANES), f32),
+                pltpu.VMEM((chunks, TABLE, 8, LANES), f32),
+            ],
+            compiler_params=pltpu.CompilerParams(vmem_limit_bytes=40 * 1024 * 1024),
+            cost_estimate=pl.CostEstimate(
+                flops=18 * fields * 8 * 768 * 384 * 2, bytes_accessed=0, transcendentals=0
+            ),
+            name="operator",
+        )(here, extra, left, right, upper, lower, halos[0][1], halos[0][2], matrix, stencil_weights, sums)
+        images += [image, second]
     sums = lax.all_to_all(sums, ("down", "cross"), 0, 0, tiled=True)
     solution_field, residual = pl.pallas_call(
         finish_kernel,
         out_shape=(jax.ShapeDtypeStruct(own.shape, f32), jax.ShapeDtypeStruct(own.shape, f32)),
-        in_specs=[vmem] * 4,
+        in_specs=[vmem] * (2 + len(images)),
         out_specs=(vmem, vmem),
         compiler_params=pltpu.CompilerParams(vmem_limit_bytes=32 * 1024 * 1024),
         name="finish",
-    )(sums, own, image, second)
+    )(sums, own, *images)
     return solution_field.reshape(right_side.shape), residual.reshape(right_side.shape)
 
 

time: 84.6 us -> 76.1 us (0.90)
  blocking collectives: 32.3 us -> 25.3 us
  other arithmetic: 2.35 us -> 0.76 us
  Pallas kernels: 24.7 us -> 26.2 us
  waiting for transfers between devices: 5.06 us -> 3.57 us
    all_to_all x1, blocking collectives: 32.3 us -> 25.3 us  [per_device(): sums = lax.all_to_all(sums, ('down', 'cross'), 0, 0, tiled=True)]
    slice x2 -> x3, local copies, waits for them, and re-layouts: 0.54 us -> 2.37 us  [the longest x1 1.1 us: per_device(): here = own[at:at + fields]]
    concatenate x2, other arithmetic: 2.33 us -> 0.52 us  [the longest x1 0.33 us: per_device(): wide = jnp.concatenate([all_fields, right, left], axis=2)]
    ppermute x6, waiting for transfers between devices: 5.06 us -> 3.57 us  [shift(): lax.ppermute(value, axis, [(i, i + by) for i in range(size) if 0 <= i + b...]
    pallas_call x1 -> x2, Pallas kernels: 20.9 us -> 22.4 us  [per_device(): pl.pallas_call(functools.partial(operator_kernel, chunks, comps, cross_at...]
    unnamed x10, local copies, waits for them, and re-layouts: 1.08 us -> 0.02 us
  transfers between devices with their start and end apart: 6 -> 6, of which waited for: 3 -> 3; matrix products, arithmetic and copies ran while one was open for 1% -> 1% of each run, Pallas kernels for 3% -> 13%
where the time goes in v2:
time: 76.1 us; the launch traced here: 75.8 us
  Pallas kernels  26.2 us (34%)
  blocking collectives  25.3 us (33%)
  starting transfers between devices  16.7 us (22%)
  waiting for transfers between devices  3.57 us (5%)
  local copies, waits for them, and re-layouts  2.4 us (3%)
  between operations  0.8 us (1%)
    all_to_all x1, blocking collectives, per_device(): sums = lax.all_to_all(sums, ('down', 'cross'), 0, 0, tiled=True)  25.3 us
    pallas_call x2, Pallas kernels, per_device(): pl.pallas_call(functools.partial(operator_kernel, chunks, comps, cross_at...  22.4 us
    ppermute x6, starting transfers between devices, shift(): lax.ppermute(value, axis, [(i, i + by) for i in range(size) if 0 <= i + b...  16.7 us
    ppermute x6, waiting for transfers between devices, shift(): lax.ppermute(value, axis, [(i, i + by) for i in range(size) if 0 <= i + b...  3.57 us
    pallas_call x1, Pallas kernels, per_device(): pl.pallas_call(matrix_kernel, out_shape=jax.ShapeDtypeStruct((3 * SLOTS.s...  2.21 us
    pallas_call x1, Pallas kernels, per_device(): pl.pallas_call(finish_kernel, out_shape=(jax.ShapeDtypeStruct(own.shape,...  1.6 us
  transfers between devices with their start and end apart: 6, of which 3 were waited for; matrix products, arithmetic and copies ran while one was open for 1% of the time, Pallas kernels for 13%

profile of v2, /device:TPU:1, one launch (start us, length us, event | category | flops | bytes accessed | tf_op | source)
XLA Modules:
  0.0 75.8 jit_solution(6274515317508461845)
XLA Ops:
  0.6 1.0 %slice_bitcast_fusion.own_ref = f32[35,4,512]{2,1,0:T(4,128)S(1)} fusion(f32[3,35,4,512]{3,2,1,0:T(4,128)} %param.5), kind=kLoop, calls=%fused_computation.1 | loop fusion | bytes 573440 | tf_op jit(solution)/shard_map/slice | solution.py:305
  1.6 1.1 %slice.38 = f32[2,35,4,512]{3,2,1,0:T(4,128)S(1)} slice(f32[3,35,4,512]{3,2,1,0:T(4,128)} %param.5), slice={[1:3], [0:35], [0:4], [0:512]} | slice | bytes 1146880 | tf_op jit(solution)/shard_map/slice | solution.py:330
  2.8 0.2 pad_maximum_fusion.1
  3.0 3.3 %collective-permute-start.1 = (f32[111,4,64]{2,1,0:T(4,128)S(1)}, f32[111,4,64]{2,1,0:T(4,128)S(1)}, u32[]{:S(2)}, u32[]{:S(2)}) collective-permute-start(f32[111,4,64]{2,1,0:T(4,128)S(1)} %get-tuple-element.22), channel_id=1, source_target_pairs={{1,0},{2,1},{3,2},{4,3},{5,4},{6,5},{7,6},{8,7},{9,8},{10,9},{11,1... | collective-permute-start | bytes 341000 | tf_op jit(solution)/shard_map/ppermute | solution.py:296
  6.3 3.1 %collective-permute-start = (f32[111,4,64]{2,1,0:T(4,128)S(1)}, f32[111,4,64]{2,1,0:T(4,128)S(1)}, u32[]{:S(2)}, u32[]{:S(2)}) collective-permute-start(f32[111,4,64]{2,1,0:T(4,128)S(1)} %get-tuple-element.23), channel_id=1, source_target_pairs={{0,1},{1,2},{2,3},{3,4},{4,5},{5,6},{6,7},{7,8},{8,9},{9,10},{10,1... | collective-permute-start | bytes 341000 | tf_op jit(solution)/shard_map/ppermute | solution.py:296
  9.4 2.2 %matrix.1.matrix_ref = bf16[768,384]{1,0:T(8,128)(2,1)} custom-call(f32[13]{0:T(128)} %weights_ref.5, s32[256,384]{1,0:T(8,128)} %constant.4.clone.slots_ref), custom_call_target="tpu_custom_call" | custom-call | tf_op jit(solution)/shard_map/matrix/pallas_call | solution.py:312
  11.6 0.0 collective-permute-done.1.right_ref
  11.6 0.7 collective-permute-done.left_ref
  12.3 0.2 pad_maximum_fusion.5
  12.6 3.6 %collective-permute-start.5 = (f32[41,2,640]{2,1,0:T(2,128)S(1)}, f32[41,2,640]{2,1,0:T(2,128)S(1)}, u32[]{:S(2)}, u32[]{:S(2)}) collective-permute-start(f32[41,2,640]{2,1,0:T(2,128)S(1)} %get-tuple-element.18), channel_id=1, source_target_pairs={{0,16},{16,32},{32,48},{48,64},{64,80},{80,96},{96,112},{1,17},{17... | collective-permute-start | bytes 629768 | tf_op jit(solution)/shard_map/ppermute | solution.py:296
  16.1 1.3 %collective-permute-start.4 = (f32[41,2,640]{2,1,0:T(2,128)S(1)}, f32[41,2,640]{2,1,0:T(2,128)S(1)}, u32[]{:S(2)}, u32[]{:S(2)}) collective-permute-start(f32[41,2,640]{2,1,0:T(2,128)S(1)} %get-tuple-element.19), channel_id=1, source_target_pairs={{16,0},{32,16},{48,32},{64,48},{80,64},{96,80},{112,96},{17,1},{33... | collective-permute-start | bytes 629768 | tf_op jit(solution)/shard_map/ppermute | solution.py:296
  17.4 0.3 pad_maximum_fusion
  17.8 0.0 copy-start.1
  17.8 0.0 copy-start.2
  17.8 0.3 fusion
  18.1 4.2 %collective-permute-start.3 = (f32[70,2,640]{2,1,0:T(2,128)S(1)}, f32[70,2,640]{2,1,0:T(2,128)S(1)}, u32[]{:S(2)}, u32[]{:S(2)}) collective-permute-start(f32[70,2,640]{2,1,0:T(2,128)S(1)} %get-tuple-element.20), channel_id=1, source_target_pairs={{0,16},{16,32},{32,48},{48,64},{64,80},{80,96},{96,112},{1,17},{17... | collective-permute-start | bytes 1075208 | tf_op jit(solution)/shard_map/ppermute | solution.py:296
  22.3 1.3 %collective-permute-start.2 = (f32[70,2,640]{2,1,0:T(2,128)S(1)}, f32[70,2,640]{2,1,0:T(2,128)S(1)}, u32[]{:S(2)}, u32[]{:S(2)}) collective-permute-start(f32[70,2,640]{2,1,0:T(2,128)S(1)} %get-tuple-element.21), channel_id=1, source_target_pairs={{16,0},{32,16},{48,32},{64,48},{80,64},{96,80},{112,96},{17,1},{33... | collective-permute-start | bytes 1075208 | tf_op jit(solution)/shard_map/ppermute | solution.py:296
  23.6 0.8 %collective-permute-done.4.upper_ref.upper_extra_ref = f32[41,2,640]{2,1,0:T(2,128)S(1)} collective-permute-done((f32[41,2,640]{2,1,0:T(2,128)S(1)}, f32[41,2,640]{2,1,0:T(2,128)S(1)}, u32[]{:S(2)}, u32[]{:S(2)}) %collective-permute-start.4) | collective-permute-done | bytes 209952 | tf_op jit(solution)/shard_map/ppermute | solution.py:296
  24.4 7.7 %operator.2 = (f32[35,4,512]{2,1,0:T(4,128)S(1)}, f32[35,4,512]{2,1,0:T(4,128)S(1)}, f32[4,8,128]{2,1,0:T(8,128)S(1)}) custom-call(f32[35,4,512]{2,1,0:T(4,128)S(1)} %slice_bitcast_fusion.own_ref, f32[6,4,512]{2,1,0:T(4,128)S(1)} %pad_maximum_fusion.7.extra_ref, f32[111,4,64]{2,1,0:T(4,128)S(1)} %collective-permute-done.left_ref, ...), custom_call_target="tpu_custom_call" | custom-call | flops 2972712960 | tf_op jit(solution)/shard_map/operator/pallas_call | solution.py:334
  32.1 0.0 collective-permute-done.3.lower_ref
  32.1 2.1 %collective-permute-done.2.upper_ref = f32[70,2,640]{2,1,0:T(2,128)S(1)} collective-permute-done((f32[70,2,640]{2,1,0:T(2,128)S(1)}, f32[70,2,640]{2,1,0:T(2,128)S(1)}, u32[]{:S(2)}, u32[]{:S(2)}) %collective-permute-start.2) | collective-permute-done | bytes 358432 | tf_op jit(solution)/shard_map/ppermute | solution.py:296
  34.2 14.7 %operator.3 = (f32[70,4,512]{2,1,0:T(4,128)S(1)}, f32[70,4,512]{2,1,0:T(4,128)S(1)}, f32[128,128]{1,0:T(8,128)S(1)}) custom-call(f32[70,4,512]{2,1,0:T(4,128)S(1)} %bitcast.14, f32[6,4,512]{2,1,0:T(4,128)S(1)} %pad_maximum_fusion.7.extra_ref, f32[111,4,64]{2,1,0:T(4,128)S(1)} %collective-permute-done.left_ref, ...), custom_call_target="tpu_custom_call" | custom-call | flops 5945425920 | tf_op jit(solution)/shard_map/operator/pallas_call | solution.py:334
  48.9 25.3 %all_to_all.11 = f32[128,1,128]{2,1,0:T(1,128)S(1)} all-to-all(f32[128,1,128]{2,1,0:T(1,128)S(1)} %bitcast.17), channel_id=1, replica_groups=mesh['down'=8,'cross'=16] {'down','cross'}, dimensions={0} | all-to-all | bytes 131072 | tf_op jit(solution)/shard_map/all_to_all | solution.py:365
  74.2 1.6 %finish.1 = (f32[105,4,512]{2,1,0:T(4,128)}, f32[105,4,512]{2,1,0:T(4,128)}) custom-call(f32[128,128]{1,0:T(8,128)S(1)} %bitcast.16, f32[105,4,512]{2,1,0:T(4,128)S(1)} %bitcast.15, f32[35,4,512]{2,1,0:T(4,128)S(1)} %get-tuple-element.12.refs_0_, f32[35,4,512]{2,1,0:T(4,128)S(1)} %get-tuple-element.13.refs_1_, f32[70,4,512]{2,1,0:T(4,128)S(1)} %get-tuple-element.14.refs_2_, ...), custom_call_target="tpu_custom_call" | custom-call | tf_op jit(solution)/shard_map/finish/pallas_call | solution.py:366
  (11 shorter events, 0.0 us)
Async XLA Ops:
  0.6 2.1 %copy-start.3 = (f32[5,4,512]{2,1,0:T(4,128)S(1)}, f32[5,4,512]{2,1,0:T(4,128)}, u32[]{:S(2)}) copy-start(f32[5,4,512]{2,1,0:T(4,128)} %param.7) | copy-start | bytes 122884
  0.6 2.1 %copy-start.4 = (f32[4,512]{1,0:T(4,128)S(1)}, f32[4,512]{1,0:T(4,128)}, u32[]{:S(2)}) copy-start(f32[4,512]{1,0:T(4,128)} %param.6) | copy-start | bytes 24580
  3.0 8.7 %collective-permute-start.1 = (f32[111,4,64]{2,1,0:T(4,128)S(1)}, f32[111,4,64]{2,1,0:T(4,128)S(1)}, u32[]{:S(2)}, u32[]{:S(2)}) collective-permute-start(f32[111,4,64]{2,1,0:T(4,128)S(1)} %get-tuple-element.22), channel_id=1, source_target_pairs={{1,0},{2,1},{3,2},{4,3},{5,4},{6,5},{7,6},{8,7},{9,8},{10,9},{11,1... | collective-permute-start | bytes 341000 | tf_op jit(solution)/shard_map/ppermute | solution.py:296
  6.3 6.0 %collective-permute-start = (f32[111,4,64]{2,1,0:T(4,128)S(1)}, f32[111,4,64]{2,1,0:T(4,128)S(1)}, u32[]{:S(2)}, u32[]{:S(2)}) collective-permute-start(f32[111,4,64]{2,1,0:T(4,128)S(1)} %get-tuple-element.23), channel_id=1, source_target_pairs={{0,1},{1,2},{2,3},{3,4},{4,5},{5,6},{6,7},{7,8},{8,9},{9,10},{10,1... | collective-permute-start | bytes 341000 | tf_op jit(solution)/shard_map/ppermute | solution.py:296
  12.6 11.0 %collective-permute-start.5 = (f32[41,2,640]{2,1,0:T(2,128)S(1)}, f32[41,2,640]{2,1,0:T(2,128)S(1)}, u32[]{:S(2)}, u32[]{:S(2)}) collective-permute-start(f32[41,2,640]{2,1,0:T(2,128)S(1)} %get-tuple-element.18), channel_id=1, source_target_pairs={{0,16},{16,32},{32,48},{48,64},{64,80},{80,96},{96,112},{1,17},{17... | collective-permute-start | bytes 629768 | tf_op jit(solution)/shard_map/ppermute | solution.py:296
  16.1 8.3 %collective-permute-start.4 = (f32[41,2,640]{2,1,0:T(2,128)S(1)}, f32[41,2,640]{2,1,0:T(2,128)S(1)}, u32[]{:S(2)}, u32[]{:S(2)}) collective-permute-start(f32[41,2,640]{2,1,0:T(2,128)S(1)} %get-tuple-element.19), channel_id=1, source_target_pairs={{16,0},{32,16},{48,32},{64,48},{80,64},{96,80},{112,96},{17,1},{33... | collective-permute-start | bytes 629768 | tf_op jit(solution)/shard_map/ppermute | solution.py:296
  17.8 6.6 %copy-start.1 = (bf16[768,384]{1,0:T(8,128)(2,1)S(1)}, bf16[768,384]{1,0:T(8,128)(2,1)}, u32[]{:S(2)}) copy-start(bf16[768,384]{1,0:T(8,128)(2,1)} %matrix.1.matrix_ref) | copy-start | bytes 1769476
  17.8 6.6 %copy-start.2 = (f32[13]{0:T(128)S(1)}, f32[13]{0:T(128)}, u32[]{:S(2)}) copy-start(f32[13]{0:T(128)} %weights_ref.5) | copy-start | bytes 160
  18.1 14.0 %collective-permute-start.3 = (f32[70,2,640]{2,1,0:T(2,128)S(1)}, f32[70,2,640]{2,1,0:T(2,128)S(1)}, u32[]{:S(2)}, u32[]{:S(2)}) collective-permute-start(f32[70,2,640]{2,1,0:T(2,128)S(1)} %get-tuple-element.20), channel_id=1, source_target_pairs={{0,16},{16,32},{32,48},{48,64},{64,80},{80,96},{96,112},{1,17},{17... | collective-permute-start | bytes 1075208 | tf_op jit(solution)/shard_map/ppermute | solution.py:296
  22.3 11.9 %collective-permute-start.2 = (f32[70,2,640]{2,1,0:T(2,128)S(1)}, f32[70,2,640]{2,1,0:T(2,128)S(1)}, u32[]{:S(2)}, u32[]{:S(2)}) collective-permute-start(f32[70,2,640]{2,1,0:T(2,128)S(1)} %get-tuple-element.21), channel_id=1, source_target_pairs={{16,0},{32,16},{48,32},{64,48},{80,64},{96,80},{112,96},{17,1},{33... | collective-permute-start | bytes 1075208 | tf_op jit(solution)/shard_map/ppermute | solution.py:296
  34.2 40.0 %copy-start = (f32[3,35,4,512]{3,2,1,0:T(4,128)S(1)}, f32[3,35,4,512]{3,2,1,0:T(4,128)}, u32[]{:S(2)}) copy-start(f32[3,35,4,512]{3,2,1,0:T(4,128)} %param.5) | copy-start | bytes 2580484

commit v3 on v1

v3 whole, which is shorter than its diff:
```python
import functools
import math

import jax
import jax.numpy as jnp
import numpy as np
from jax import lax
from jax.experimental import pallas as pl
from jax.experimental.pallas import tpu as pltpu
from jax.sharding import PartitionSpec as P

CZ = 32
VARS = 4
DEG = 3
TERMS = 5
COMPS = 3
MODES = 35
FIELDS = COMPS * MODES
STIFF = FIELDS + TERMS
ROWS = 4
LANES = 128
WIDE = 64


def multi_indices(count_left, budget_left):
    if count_left == 0:
        return [()]
    return [
        (leading,) + remainder
        for leading in range(budget_left + 1)
        for remainder in multi_indices(count_left - 1, budget_left - leading)
    ]


def chaos_terms():
    picked = sorted(
        multi_indices(VARS, DEG),
        key=lambda multi_index: (sum(multi_index),)
        + tuple((-entry_value for entry_value in multi_index)),
    )
    position = {multi_index: number for number, multi_index in enumerate(picked)}
    terms = [[] for mode in picked]
    for variable in range(VARS):
        for multi_index in picked:
            raised = list(multi_index)
            raised[variable] += 1
            raised = tuple(raised)
            if raised in position:
                degree = multi_index[variable]
                here, there = position[multi_index], position[raised]
                terms[here].append((variable, degree, there))
                terms[there].append((variable, degree, here))
    values = [(n + 1) / math.sqrt((2 * n + 1) * (2 * n + 3)) for n in range(DEG)]
    return terms, values


CHAOS, CHAOS_VALUES = chaos_terms()
TABLE = 1 + VARS * DEG


def tap_slots(y_in, y_out, reach):
    z = np.arange(CZ)
    y_in, z_in = np.repeat(y_in, CZ), np.tile(z, len(y_in))
    y_out, z_out = np.repeat(y_out, CZ), np.tile(z, len(y_out))
    dy = y_in[:, None] - y_out[None, :]
    dz = z_in[:, None] - z_out[None, :]
    near = (abs(dy) <= 1) & (abs(dz) <= 1) & np.repeat(np.repeat(reach, CZ, 0), CZ, 1)
    parts = []
    for dx in (0, 1, -1):
        linear = 9 * (dx + 1) + 3 * (dy + 1) + (dz + 1)
        slot = np.minimum(linear, 26 - linear)
        parts.append(np.where(near & (linear != 13), slot, 13))
    return np.concatenate(parts, axis=1).astype(np.int32)


def chunk_slots():
    y_in = np.array([0, 1, 2, 3, 4, 5, -2, -1])
    return tap_slots(y_in, np.arange(4), np.ones((8, 4), bool))


def rim_slots():
    far = 100
    y_in = np.array([16, 17, -2 - far, -1 - far, -far, 1 - far, 14, 15])
    y_out = np.array([15, 16, -1 - far, -far])
    reach = np.ones((8, 4), bool)
    reach[4:, 0] = False
    reach[4:, 3] = False
    return tap_slots(y_in, y_out, reach)


SLOTS = np.stack([chunk_slots(), rim_slots()])


def matrix_kernel(weights_ref, slots_ref, matrix_ref):
    slots = slots_ref[0]
    full = jnp.zeros(slots.shape, jnp.float32)
    for number in range(13):
        full = jnp.where(slots == number, 0.5 * weights_ref[number], full)
    high = full.astype(jnp.bfloat16)
    low = (full - high.astype(jnp.float32)).astype(jnp.bfloat16)
    rows = slots.shape[0]
    matrix_ref[0, :rows] = high
    matrix_ref[0, rows : 2 * rows] = high
    matrix_ref[0, 2 * rows :] = low


def mix(table, load, mode, total):
    for variable, degree, other in CHAOS[mode]:
        total = total + table[1 + variable * DEG + degree] * load(other)
    return total


def window(own, after, before):
    left = lax.broadcasted_iota(jnp.int32, own[0].shape, 1) < WIDE
    high, low = [jnp.where(left, ahead, behind) for ahead, behind in zip(after, before)]
    return jnp.concatenate([own[0], high, own[1], low, own[0], high], axis=1)


def stencil(own, after, before, matrix, out):
    parts = jnp.dot(
        window(own, after, before), matrix[...], preferred_element_type=jnp.float32
    )
    shape = out.shape
    centre = parts[:, :LANES].reshape(shape)
    ahead = parts[:, LANES : 2 * LANES].reshape(shape)
    behind = parts[:, 2 * LANES :].reshape(shape)
    out[...] = centre + pltpu.roll(ahead, 7, 1) + pltpu.roll(behind, 1, 1)


def halves(value):
    value = value.reshape(value.shape[0] * 8, LANES)
    high = value.astype(jnp.bfloat16)
    return high, (value - high.astype(jnp.float32)).astype(jnp.bfloat16)


def fill(table, values):
    table[0] = values[0]
    for variable in range(VARS):
        for degree in range(DEG):
            table[1 + variable * DEG + degree] = values[1 + variable] * CHAOS_VALUES[degree]


def load_table(table):
    return [table[entry] for entry in range(TABLE)]


def grow(field, table, out):
    table = load_table(table)

    @pl.loop(0, COMPS)
    def each(comp):
        base = comp * MODES
        for mode in range(MODES):
            load = lambda other: field[base + other]
            out[base + mode] = mix(table, load, mode, table[0] * load(mode))


def apply(field, near, grown_near, coef, diag, stiff, store):
    coef, diag = load_table(coef), load_table(diag)

    def each(comp, carry):
        base = comp * MODES
        for mode in range(MODES):
            load = lambda other: field[base + other]
            close = lambda other: near[base + other]
            value = mix(diag, load, mode, (stiff + diag[0]) * load(mode))
            value = value - mix(
                coef, close, mode, coef[0] * close(mode) + grown_near[base + mode]
            )
            carry = store(base + mode, value, carry)
        return carry

    return each


def finish_chunk(start, image, near, grown_near, coef, diag, stiff, image_out, second_out, lanes, sums):
    def store(number, value, sums):
        rr, rq, qq, qz = sums
        first, here = start[number], image[number]
        image_out[number, :, lanes] = here[:ROWS]
        second_out[number, :, lanes] = value[:ROWS]
        return rr + first * first, rq + first * here, qq + here * here, qz + here * value

    return lax.fori_loop(0, COMPS, apply(image, near, grown_near, coef, diag, stiff, store), sums)


def fill_diag(table, field, near, weights_ref):
    weight_sum = sum(weights_ref[number] for number in range(13))
    fill(table, [field[FIELDS + t] * weight_sum + near[FIELDS + t] for t in range(TERMS)])


def inner_kernel(
    own_ref, extra_ref, upper_ref, lower_ref, matrix_ref, weights_ref,
    field, grown_high, grown_low, outer_near, outer_grown_near,
    image, image_high, image_low, image_grown_high, image_grown_low, coef_table, diag_table,
    image_ref, second_ref, sums_ref,
    field_high, field_low, grown, near, grown_near,
):
    chunks = field.shape[0]
    for k in range(chunks):
        lanes = pl.ds(k * LANES, LANES)
        field[k, :FIELDS, 0:ROWS, :] = own_ref[:, :, lanes]
        field[k, FIELDS : STIFF + 1, 0:ROWS, :] = extra_ref[:, :, lanes]
        field[k, : STIFF + 1, ROWS : ROWS + 2, :] = upper_ref[:, :, lanes]
        field[k, : STIFF + 1, ROWS + 2 : ROWS + 4, :] = lower_ref[:, :, lanes]
        field[k, STIFF + 1] = jnp.zeros((8, LANES), jnp.float32)
        image[k, FIELDS] = jnp.zeros((8, LANES), jnp.float32)
    grown[FIELDS] = jnp.zeros((8, LANES), jnp.float32)
    for ref in (field_high, field_low, grown_high, grown_low):
        ref[chunks] = jnp.zeros(ref.shape[1:], jnp.bfloat16)

    def step(k):
        return lax.rem(k + 1, chunks + 1), lax.rem(k + chunks, chunks + 1)

    @pl.loop(0, chunks)
    def grow_field(k):
        fill(coef_table.at[k], [field[k, FIELDS + term] for term in range(TERMS)])
        grow(field.at[k], coef_table.at[k], grown)
        grown_high[k], grown_low[k] = halves(grown[...])
        field_high[k], field_low[k] = halves(field[k])

    @pl.loop(0, chunks)
    def first(k):
        after, before = step(k)
        for high, low, out in ((field_high, field_low, near), (grown_high, grown_low, grown_near)):
            stencil(*[(high[at], low[at]) for at in (k, after, before)], matrix_ref, out)
        fill_diag(diag_table.at[k], field.at[k], near, weights_ref)
        stiff = field[k, STIFF]
        inside = stiff > 0.0

        def store(number, value, carry):
            image[k, number] = jnp.where(inside, value, 0.0)
            return carry

        lax.fori_loop(
            0,
            COMPS,
            apply(field.at[k], near, grown_near, coef_table.at[k], diag_table.at[k], stiff, store),
            0,
        )

        @pl.when(k == 0)
        def _():
            outer_near[0] = near[...]
            outer_grown_near[0] = grown_near[...]

        @pl.when(k == chunks - 1)
        def _():
            outer_near[1] = near[...]
            outer_grown_near[1] = grown_near[...]

    @pl.loop(0, chunks)
    def grow_image(k):
        grow(image.at[k], coef_table.at[k], grown)
        image_grown_high[k], image_grown_low[k] = halves(grown[...])
        image_high[k], image_low[k] = halves(image[k])

    image_near = near.at[pl.ds(0, FIELDS + 1)]
    zero = jnp.zeros((8, LANES), jnp.float32)

    def second(k, sums):
        for high, low, out in (
            (image_high, image_low, image_near),
            (image_grown_high, image_grown_low, grown_near),
        ):
            stencil(*[(high[at], low[at]) for at in (k, k + 1, k - 1)], matrix_ref, out)
        lanes = pl.ds(pl.multiple_of((k - 1) * LANES, LANES), LANES)
        return finish_chunk(
            field.at[k], image.at[k], image_near, grown_near, coef_table.at[k], diag_table.at[k],
            field[k, STIFF], image_ref, second_ref, lanes, sums,
        )

    sums = lax.fori_loop(1, chunks - 1, second, (zero, zero, zero, zero))
    for number, value in enumerate(sums):
        sums_ref[number] = value


def outer_kernel(
    right_ref, left_ref, matrix_ref, rim_matrix_ref, weights_ref,
    field, grown_high, grown_low, outer_near, outer_grown_near,
    image, image_high, image_low, image_grown_high, image_grown_low, coef_table, diag_table, before_ref,
    image_ref, second_ref, sums_ref,
    edge, rim, grown, near, grown_near, rim_image, edge_image, coef, diag, edge_coef, ends,
):
    final = field.shape[0] - 1
    lane = lax.broadcasted_iota(jnp.int32, (8, LANES), 1)
    zero = jnp.zeros((8, LANES), jnp.float32)
    edge[: STIFF + 1] = jnp.concatenate([right_ref[...], left_ref[...]], axis=2)
    edge[STIFF + 1] = zero
    grown[FIELDS] = zero
    rim_image[FIELDS] = zero
    for side in range(2):
        ends[side, FIELDS] = zero
    edge_image[FIELDS] = zero

    def to_rim(last, beyond, begin):
        right = pltpu.roll(jnp.where(lane >= 3 * CZ, last, beyond), CZ, last.ndim - 1)
        left = pltpu.roll(jnp.where(lane < CZ, begin, beyond), LANES - CZ, last.ndim - 1)
        return jnp.where(lane < WIDE, right, left)

    fill(edge_coef, [edge[FIELDS + term] for term in range(TERMS)])
    grow(edge, edge_coef, grown)
    edge_parts = halves(edge[...])
    begin, last = halves(field[0]), halves(field[final])
    stencil(edge_parts, begin, last, rim_matrix_ref, near)
    stencil(
        halves(grown[...]),
        (grown_high[0], grown_low[0]),
        (grown_high[final], grown_low[final]),
        rim_matrix_ref,
        grown_near,
    )
    left_rim, right_rim = lane >= 3 * CZ, lane < CZ

    def own_part(last, begin):
        moved = jnp.where(right_rim, pltpu.roll(last, CZ, last.ndim - 1), 0.0)
        return jnp.where(left_rim, pltpu.roll(begin, LANES - CZ, last.ndim - 1), moved)

    near[...] = near[...] + own_part(outer_near[1], outer_near[0])
    grown_near[...] = grown_near[...] + own_part(outer_grown_near[1], outer_grown_near[0])
    rim[...] = to_rim(field[final], edge[...], field[0])
    fill(coef, [rim[FIELDS + term] for term in range(TERMS)])
    fill_diag(diag, rim, near, weights_ref)
    stiff = rim[STIFF]
    inside = stiff > 0.0

    def store(number, value, carry):
        rim_image[number] = jnp.where(inside, value, 0.0)
        return carry

    lax.fori_loop(0, COMPS, apply(rim, near, grown_near, coef, diag, stiff, store), 0)
    grow(rim_image, coef, grown)

    def from_rim(value):
        return pltpu.roll(value, CZ, value.ndim - 1), pltpu.roll(value, LANES - CZ, value.ndim - 1)

    def placed(begin, last, value):
        to_left, to_right = from_rim(value)
        return (
            jnp.where(lane < CZ, to_left, begin),
            jnp.where(lane >= 3 * CZ, to_right, last),
            jnp.where(lane < WIDE, to_right, to_left),
        )

    ends[0], ends[1], edge_image[...] = placed(image[0], image[final], rim_image[...])
    image_parts = [halves(ends[0]), halves(ends[1]), halves(edge_image[...])]

    def joined(ref_high, ref_low, k):
        return (ref_high[k].astype(jnp.float32) + ref_low[k].astype(jnp.float32)).reshape(
            grown.shape
        )

    grown_parts = [
        halves(value)
        for value in placed(
            joined(image_grown_high, image_grown_low, 0),
            joined(image_grown_high, image_grown_low, final),
            grown[...],
        )
    ]
    for entry in range(TABLE):
        to_left, to_right = from_rim(diag[entry])
        edge_coef[entry] = jnp.where(lane < CZ, to_left, diag_table[0, entry])
        coef[entry] = jnp.where(lane >= 3 * CZ, to_right, diag_table[final, entry])
    image_near = near.at[pl.ds(0, FIELDS + 1)]
    sums = tuple(before_ref[number] for number in range(4))
    for side, k, table in ((0, 0, edge_coef), (1, final, coef)):
        for (begin, last, beyond), high, low, out in (
            (image_parts, image_high, image_low, image_near),
            (grown_parts, image_grown_high, image_grown_low, grown_near),
        ):
            if side == 0:
                chunk = (begin, (high[1], low[1]), beyond)
            else:
                chunk = (last, beyond, (high[final - 1], low[final - 1]))
            stencil(*chunk, matrix_ref, out)
        sums = finish_chunk(
            field.at[k], ends.at[side], image_near, grown_near, coef_table.at[k], table,
            field[k, STIFF], image_ref, second_ref, pl.ds(side * LANES, LANES), sums,
        )
    inner = lax.broadcasted_iota(jnp.int32, (8, LANES), 0) < ROWS
    column = lax.broadcasted_iota(jnp.int32, sums_ref.shape, 1)
    row = jnp.zeros(sums_ref.shape, jnp.float32)
    for number, value in enumerate(sums):
        row = jnp.where(column == number, jnp.sum(jnp.where(inner, value, 0.0)), row)
    sums_ref[...] = row


def finish_kernel(sums_ref, start_ref, *refs):
    *parts, field_ref, residual_ref = refs
    total = jnp.sum(sums_ref[...], axis=0, keepdims=True)
    lane = lax.broadcasted_iota(jnp.int32, total.shape, 1)
    rr, rq, qq, qz = [
        jnp.sum(jnp.where(lane == number, total, 0.0), axis=1, keepdims=True)[None]
        for number in range(4)
    ]
    step = rr / rq
    fresh = rr - 2.0 * step * rq + step * step * qq
    grow = 1.0 + fresh / rr
    curvature = grow * grow * rq - 2.0 * grow * step * qq + step * step * qz
    later = fresh / curvature
    both = step + later * grow
    cross = later * step
    inner, outer = parts[:2], parts[2:]
    columns = start_ref.shape[2]
    for (image_ref, second_ref), source, at, width in (
        (outer, 0, 0, LANES),
        (inner, 0, LANES, columns - 2 * LANES),
        (outer, LANES, columns - LANES, LANES),
    ):
        there, here = pl.ds(source, width), pl.ds(at, width)
        start, image, second = start_ref[:, :, here], image_ref[:, :, there], second_ref[:, :, there]
        field_ref[:, :, here] = both * start - cross * image
        residual_ref[:, :, here] = start - both * image + cross * second


def shift(value, axis, by):
    size = lax.axis_size(axis)
    return lax.ppermute(value, axis, [(i, i + by) for i in range(size) if 0 <= i + by < size])


def per_device(right_side, stiffness, coefficients, stencil_weights):
    columns = right_side.shape[3]
    chunks = columns // LANES
    devices = lax.axis_size("down") * lax.axis_size("cross")
    own = right_side.reshape(FIELDS, ROWS, columns)
    extra = jnp.concatenate([coefficients, stiffness[None]], axis=0)
    all_fields = jnp.concatenate([own, extra], axis=0)
    upper = shift(all_fields[:, :2], "down", -1)
    lower = shift(all_fields[:, ROWS - 2 :], "down", 1)
    tall = jnp.concatenate([all_fields, upper, lower], axis=1)
    right = shift(tall[:, :, :WIDE], "cross", -1)
    left = shift(tall[:, :, columns - WIDE :], "cross", 1)
    vmem = pl.BlockSpec(memory_space=pltpu.VMEM)
    smem = pl.BlockSpec(memory_space=pltpu.SMEM)
    f32, bf16 = jnp.float32, jnp.bfloat16
    params = pltpu.CompilerParams(vmem_limit_bytes=32 * 1024 * 1024)
    matrices = pl.pallas_call(
        matrix_kernel,
        grid=(2,),
        out_shape=jax.ShapeDtypeStruct((2, 3 * SLOTS.shape[1], SLOTS.shape[2]), bf16),
        in_specs=[smem, pl.BlockSpec((1,) + SLOTS.shape[1:], lambda i: (i, 0, 0))],
        out_specs=pl.BlockSpec((1, 3 * SLOTS.shape[1], SLOTS.shape[2]), lambda i: (i, 0, 0)),
        name="matrix",
    )(stencil_weights, jnp.asarray(SLOTS))
    matrix, rim_matrix = matrices[0], matrices[1]
    shape = jax.ShapeDtypeStruct
    count, wider = FIELDS + 1, STIFF + 2
    tiles = lambda number: (number, 8, LANES)
    rows = lambda number: (number * 8, LANES)
    half = (FIELDS, ROWS, columns // 2)
    *kept, image, second, sums = pl.pallas_call(
        inner_kernel,
        out_shape=(
            shape((chunks,) + tiles(wider), f32),
            shape((chunks + 1,) + rows(count), bf16),
            shape((chunks + 1,) + rows(count), bf16),
            shape((2,) + tiles(wider), f32),
            shape((2,) + tiles(count), f32),
            shape((chunks,) + tiles(count), f32),
            shape((chunks,) + rows(count), bf16),
            shape((chunks,) + rows(count), bf16),
            shape((chunks,) + rows(count), bf16),
            shape((chunks,) + rows(count), bf16),
            shape((chunks,) + tiles(TABLE), f32),
            shape((chunks,) + tiles(TABLE), f32),
            shape(half, f32),
            shape(half, f32),
            shape(tiles(4), f32),
        ),
        in_specs=[vmem] * 5 + [smem],
        out_specs=(vmem,) * 15,
        scratch_shapes=[
            pltpu.VMEM((chunks + 1,) + rows(wider), bf16),
            pltpu.VMEM((chunks + 1,) + rows(wider), bf16),
            pltpu.VMEM(tiles(count), f32),
            pltpu.VMEM(tiles(wider), f32),
            pltpu.VMEM(tiles(count), f32),
        ],
        compiler_params=params,
        cost_estimate=pl.CostEstimate(flops=10**10, bytes_accessed=0, transcendentals=0),
        name="inner",
    )(own, extra, upper, lower, matrix, stencil_weights)
    outer_image, outer_second, sums = pl.pallas_call(
        outer_kernel,
        out_shape=(shape(half, f32), shape(half, f32), shape((devices, LANES), f32)),
        in_specs=[vmem] * 4 + [smem] + [vmem] * 13,
        out_specs=(vmem,) * 3,
        scratch_shapes=[
            pltpu.VMEM(tiles(wider), f32),
            pltpu.VMEM(tiles(wider), f32),
            pltpu.VMEM(tiles(count), f32),
            pltpu.VMEM(tiles(wider), f32),
            pltpu.VMEM(tiles(count), f32),
            pltpu.VMEM(tiles(count), f32),
            pltpu.VMEM(tiles(count), f32),
            pltpu.VMEM(tiles(TABLE), f32),
            pltpu.VMEM(tiles(TABLE), f32),
            pltpu.VMEM(tiles(TABLE), f32),
            pltpu.VMEM((2,) + tiles(count), f32),
        ],
        compiler_params=params,
        name="outer",
    )(right, left, matrix, rim_matrix, stencil_weights, *kept, sums)
    sums = lax.all_to_all(sums, ("down", "cross"), 0, 0, tiled=True)
    solution_field, residual = pl.pallas_call(
        finish_kernel,
        out_shape=(shape(own.shape, f32), shape(own.shape, f32)),
        in_specs=[vmem] * 6,
        out_specs=(vmem, vmem),
        compiler_params=params,
        name="finish",
    )(sums, own, image, second, outer_image, outer_second)
    return solution_field.reshape(right_side.shape), residual.reshape(right_side.shape)


def solution(mesh):
    return jax.shard_map(
        per_device,
        mesh=mesh,
        in_specs=(
            P(None, None, "down", "cross"),
            P("down", "cross"),
            P(None, "down", "cross"),
            P(),
        ),
        out_specs=(P(None, None, "down", "cross"), P(None, None, "down", "cross")),
        check_vma=False,
    )
```

time: 84.6 us -> 73.8 us (0.87)
  blocking collectives: 32.3 us -> 24.5 us
  starting transfers between devices: 17.4 us -> 12.9 us
  Pallas kernels: 24.7 us -> 26.7 us
    all_to_all x1, blocking collectives: 32.3 us -> 24.5 us  [per_device(): sums = lax.all_to_all(sums, ('down', 'cross'), 0, 0, tiled=True)]
    ppermute x6 -> x4, starting transfers between devices: 17.4 us -> 12.9 us  [shift(): lax.ppermute(value, axis, [(i, i + by) for i in range(size) if 0 <= i + b...]
    pallas_call x3 -> x4, Pallas kernels: 24.7 us -> 26.7 us  [the longest x1 15 us: per_device(): pl.pallas_call(inner_kernel, out_shape=(shape((chunks,) + tiles(wider), f...]
    squeeze x0 -> x1, local copies, waits for them, and re-layouts: none -> 1.44 us  [per_device(): matrix, rim_matrix = (matrices[0], matrices[1])]
    unnamed x10 -> x8, local copies, waits for them, and re-layouts: 1.08 us -> 0.03 us
    ppermute x6 -> x4, waiting for transfers between devices: 5.06 us -> 4.92 us  [shift(): lax.ppermute(value, axis, [(i, i + by) for i in range(size) if 0 <= i + b...]
  transfers between devices with their start and end apart: 6 -> 4, of which waited for: 3 -> 2; matrix products, arithmetic and copies ran while one was open for 1% -> 2% of each run, Pallas kernels for 3% -> 24%
where the time goes in v3:
time: 73.8 us; the launch traced here: 73.5 us
  Pallas kernels  26.7 us (36%)
  blocking collectives  24.5 us (33%)
  starting transfers between devices  12.9 us (17%)
  waiting for transfers between devices  4.92 us (7%)
  other arithmetic  1.91 us (3%)
  local copies, waits for them, and re-layouts  1.82 us (2%)
  between operations  0.76 us (1%)
    all_to_all x1, blocking collectives, per_device(): sums = lax.all_to_all(sums, ('down', 'cross'), 0, 0, tiled=True)  24.5 us
    pallas_call x1, Pallas kernels, per_device(): pl.pallas_call(inner_kernel, out_shape=(shape((chunks,) + tiles(wider), f...  15 us
    ppermute x4, starting transfers between devices, shift(): lax.ppermute(value, axis, [(i, i + by) for i in range(size) if 0 <= i + b...  12.9 us
    pallas_call x1, Pallas kernels, per_device(): pl.pallas_call(outer_kernel, out_shape=(shape(half, f32), shape(half, f32...  7.16 us
    ppermute x4, waiting for transfers between devices, shift(): lax.ppermute(value, axis, [(i, i + by) for i in range(size) if 0 <= i + b...  4.92 us
    pallas_call x1, Pallas kernels, per_device(): pl.pallas_call(matrix_kernel, grid=(2,), out_shape=jax.ShapeDtypeStruct((...  2.63 us
    pallas_call x1, Pallas kernels, per_device(): pl.pallas_call(finish_kernel, out_shape=(shape(own.shape, f32), shape(own...  1.93 us
  transfers between devices with their start and end apart: 4, of which 2 were waited for; matrix products, arithmetic and copies ran while one was open for 2% of the time, Pallas kernels for 24%

profile of v3, /device:TPU:1, one launch (start us, length us, event | category | flops | bytes accessed | tf_op | source)
XLA Modules:
  0.0 73.5 jit_solution(8428849834769759467)
XLA Ops:
  0.6 1.4 %pad_maximum_fusion = f32[111,4,512]{2,1,0:T(4,128)S(1)} fusion(f32[1,4,512]{2,1,0:T(4,128)} %bitcast.18, f32[5,4,512]{2,1,0:T(4,128)} %param.7, f32[105,4,512]{2,1,0:T(4,128)} %bitcast.12), kind=kLoop, calls=%fused_computation | loop fusion | flops 454656 | bytes 1818624 | tf_op jit(solution)/shard_map/concatenate | solution.py:428
  2.0 0.4 fusion
  2.4 0.0 copy-start.2
  2.4 0.0 copy-start.3
  2.4 1.4 %collective-permute-start = (f32[111,2,512]{2,1,0:T(2,128)S(1)}, f32[111,2,512]{2,1,0:T(2,128)S(1)}, u32[]{:S(2)}, u32[]{:S(2)}) collective-permute-start(f32[111,2,512]{2,1,0:T(2,128)S(1)} %get-tuple-element.46), channel_id=1, source_target_pairs={{16,0},{32,16},{48,32},{64,48},{80,64},{96,80},{112,96},{17,1},{33... | collective-permute-start | bytes 1363976 | tf_op jit(solution)/shard_map/ppermute | solution.py:419
  3.8 5.0 %collective-permute-start.1 = (f32[111,2,512]{2,1,0:T(2,128)S(1)}, f32[111,2,512]{2,1,0:T(2,128)S(1)}, u32[]{:S(2)}, u32[]{:S(2)}) collective-permute-start(f32[111,2,512]{2,1,0:T(2,128)S(1)} %get-tuple-element.47), channel_id=1, source_target_pairs={{0,16},{16,32},{32,48},{48,64},{64,80},{80,96},{96,112},{1,17},{17... | collective-permute-start | bytes 1363976 | tf_op jit(solution)/shard_map/ppermute | solution.py:419
  8.9 2.6 %matrix.1 = bf16[2,768,384]{2,1,0:T(8,128)(2,1)} custom-call(f32[13]{0:T(128)} %weights_ref.5, s32[2,256,384]{2,1,0:T(8,128)} %constant.2.clone.slots_ref), custom_call_target="tpu_custom_call" | custom-call | tf_op jit(solution)/shard_map/matrix/pallas_call | solution.py:438
  11.5 0.0 copy-done.2
  11.5 0.0 copy-done.3
  11.5 0.0 copy-start
  11.5 1.4 %slice_bitcast_fusion = (bf16[768,384]{1,0:T(8,128)(2,1)S(1)}, bf16[768,384]{1,0:T(8,128)(2,1)S(1)}) fusion(bf16[2,768,384]{2,1,0:T(8,128)(2,1)} %matrix.1), kind=kLoop, calls=%fused_computation.1 | loop fusion | bytes 2359296 | tf_op jit(solution)/shard_map/squeeze | solution.py:446
  13.0 0.0 copy-start.1
  13.0 4.1 %collective-permute-done.upper_ref = f32[111,2,512]{2,1,0:T(2,128)S(1)} collective-permute-done((f32[111,2,512]{2,1,0:T(2,128)S(1)}, f32[111,2,512]{2,1,0:T(2,128)S(1)}, u32[]{:S(2)}, u32[]{:S(2)}) %collective-permute-start) | collective-permute-done | bytes 454688 | tf_op jit(solution)/shard_map/ppermute | solution.py:419
  17.1 0.9 %collective-permute-done.1.lower_ref = f32[111,2,512]{2,1,0:T(2,128)S(1)} collective-permute-done((f32[111,2,512]{2,1,0:T(2,128)S(1)}, f32[111,2,512]{2,1,0:T(2,128)S(1)}, u32[]{:S(2)}, u32[]{:S(2)}) %collective-permute-start.1) | collective-permute-done | bytes 454688 | tf_op jit(solution)/shard_map/ppermute | solution.py:419
  17.9 0.0 copy-done
  17.9 0.5 pad_maximum_fusion.1
  18.4 3.5 %collective-permute-start.2 = (f32[111,8,64]{2,1,0:T(8,128)S(1)}, f32[111,8,64]{2,1,0:T(8,128)S(1)}, u32[]{:S(2)}, u32[]{:S(2)}) collective-permute-start(f32[111,8,64]{2,1,0:T(8,128)S(1)} %get-tuple-element.43), channel_id=1, source_target_pairs={{1,0},{2,1},{3,2},{4,3},{5,4},{6,5},{7,6},{8,7},{9,8},{10,9},{11,1... | collective-permute-start | bytes 681992 | tf_op jit(solution)/shard_map/ppermute | solution.py:419
  21.9 3.0 %collective-permute-start.3 = (f32[111,8,64]{2,1,0:T(8,128)S(1)}, f32[111,8,64]{2,1,0:T(8,128)S(1)}, u32[]{:S(2)}, u32[]{:S(2)}) collective-permute-start(f32[111,8,64]{2,1,0:T(8,128)S(1)} %get-tuple-element.42), channel_id=1, source_target_pairs={{0,1},{1,2},{2,3},{3,4},{4,5},{5,6},{6,7},{7,8},{8,9},{9,10},{10,1... | collective-permute-start | bytes 681992 | tf_op jit(solution)/shard_map/ppermute | solution.py:419
  24.9 15.0 %inner.1 = (f32[4,112,8,128]{3,2,1,0:T(8,128)S(1)}, bf16[5,848,128]{2,1,0:T(8,128)(2,1)S(1)}, bf16[5,848,128]{2,1,0:T(8,128)(2,1)S(1)}, f32[2,112,8,128]{3,2,1,0...) custom-call(f32[105,4,512]{2,1,0:T(4,128)S(1)} %bitcast.14, ...), custom_call_target="tpu_custom_call" | custom-call | flops 10000000000 | tf_op jit(solution)/shard_map/inner/pallas_call | solution.py:452
  39.9 0.0 collective-permute-done.2.right_ref
  39.9 0.0 collective-permute-done.3.left_ref
  39.9 7.2 %outer.1 = (f32[105,4,256]{2,1,0:T(4,128)S(1)}, f32[105,4,256]{2,1,0:T(4,128)S(1)}, f32[128,128]{1,0:T(8,128)S(1)}) custom-call(f32[111,8,64]{2,1,0:T(8,128)S(1)} %collective-permute-done.2.right_ref, f32[111,8,64]{2,1,0:T(8,128)S(1)} %collective-permute-done.3.left_ref, bf16[768,384]{1,0:T(8,128)(2,1)S(1)} %get-tuple-element.45.matrix_ref, ...), custom_call_target="tpu_custom_call" | custom-call | tf_op jit(solution)/shard_map/outer/pallas_call | solution.py:484
  47.1 24.5 %all_to_all.11 = f32[128,1,128]{2,1,0:T(1,128)S(1)} all-to-all(f32[128,1,128]{2,1,0:T(1,128)S(1)} %bitcast.17), channel_id=1, replica_groups=mesh['down'=8,'cross'=16] {'down','cross'}, dimensions={0} | all-to-all | bytes 131072 | tf_op jit(solution)/shard_map/all_to_all | solution.py:505
  71.6 1.9 %finish.1 = (f32[105,4,512]{2,1,0:T(4,128)}, f32[105,4,512]{2,1,0:T(4,128)}) custom-call(f32[128,128]{1,0:T(8,128)S(1)} %bitcast.16, f32[105,4,512]{2,1,0:T(4,128)S(1)} %bitcast.15, f32[105,4,256]{2,1,0:T(4,128)S(1)} %get-tuple-element.36.refs_0_, f32[105,4,256]{2,1,0:T(4,128)S(1)} %get-tuple-element.37.refs_1_, ...), custom_call_target="tpu_custom_call" | custom-call | tf_op jit(solution)/shard_map/finish/pallas_call | solution.py:506
  (2 shorter events, 0.0 us)
Async XLA Ops:
  2.4 9.1 %copy-start.2 = (f32[5,4,512]{2,1,0:T(4,128)S(1)}, f32[5,4,512]{2,1,0:T(4,128)}, u32[]{:S(2)}) copy-start(f32[5,4,512]{2,1,0:T(4,128)} %param.7) | copy-start | bytes 122884
  2.4 9.1 %copy-start.3 = (f32[4,512]{1,0:T(4,128)S(1)}, f32[4,512]{1,0:T(4,128)}, u32[]{:S(2)}) copy-start(f32[4,512]{1,0:T(4,128)} %param.6) | copy-start | bytes 24580
  2.4 14.6 %collective-permute-start = (f32[111,2,512]{2,1,0:T(2,128)S(1)}, f32[111,2,512]{2,1,0:T(2,128)S(1)}, u32[]{:S(2)}, u32[]{:S(2)}) collective-permute-start(f32[111,2,512]{2,1,0:T(2,128)S(1)} %get-tuple-element.46), channel_id=1, source_target_pairs={{16,0},{32,16},{48,32},{64,48},{80,64},{96,80},{112,96},{17,1},{33... | collective-permute-start | bytes 1363976 | tf_op jit(solution)/shard_map/ppermute | solution.py:419
  3.8 14.1 %collective-permute-start.1 = (f32[111,2,512]{2,1,0:T(2,128)S(1)}, f32[111,2,512]{2,1,0:T(2,128)S(1)}, u32[]{:S(2)}, u32[]{:S(2)}) collective-permute-start(f32[111,2,512]{2,1,0:T(2,128)S(1)} %get-tuple-element.47), channel_id=1, source_target_pairs={{0,16},{16,32},{32,48},{48,64},{64,80},{80,96},{96,112},{1,17},{17... | collective-permute-start | bytes 1363976 | tf_op jit(solution)/shard_map/ppermute | solution.py:419
  11.5 6.4 %copy-start = (f32[3,35,4,512]{3,2,1,0:T(4,128)S(1)}, f32[3,35,4,512]{3,2,1,0:T(4,128)}, u32[]{:S(2)}) copy-start(f32[3,35,4,512]{3,2,1,0:T(4,128)} %param.5) | copy-start | bytes 2580484
  13.0 11.9 %copy-start.1 = (f32[13]{0:T(128)S(1)}, f32[13]{0:T(128)}, u32[]{:S(2)}) copy-start(f32[13]{0:T(128)} %weights_ref.5) | copy-start | bytes 160
  18.4 21.5 %collective-permute-start.2 = (f32[111,8,64]{2,1,0:T(8,128)S(1)}, f32[111,8,64]{2,1,0:T(8,128)S(1)}, u32[]{:S(2)}, u32[]{:S(2)}) collective-permute-start(f32[111,8,64]{2,1,0:T(8,128)S(1)} %get-tuple-element.43), channel_id=1, source_target_pairs={{1,0},{2,1},{3,2},{4,3},{5,4},{6,5},{7,6},{8,7},{9,8},{10,9},{11,1... | collective-permute-start | bytes 681992 | tf_op jit(solution)/shard_map/ppermute | solution.py:419
  21.9 18.0 %collective-permute-start.3 = (f32[111,8,64]{2,1,0:T(8,128)S(1)}, f32[111,8,64]{2,1,0:T(8,128)S(1)}, u32[]{:S(2)}, u32[]{:S(2)}) collective-permute-start(f32[111,8,64]{2,1,0:T(8,128)S(1)} %get-tuple-element.42), channel_id=1, source_target_pairs={{0,1},{1,2},{2,3},{3,4},{4,5},{5,6},{6,7},{7,8},{8,9},{9,10},{10,1... | collective-permute-start | bytes 681992 | tf_op jit(solution)/shard_map/ppermute | solution.py:419

commit v4 on v3

--- a/solution.py
+++ b/solution.py
@@ -151,7 +151,7 @@
     def each(comp):
         base = comp * MODES
         for mode in range(MODES):
-            load = lambda other: field[base + other]
+            load = lambda other: field(base + other)
             out[base + mode] = mix(table, load, mode, table[0] * load(mode))
 
 
@@ -161,7 +161,7 @@
     def each(comp, carry):
         base = comp * MODES
         for mode in range(MODES):
-            load = lambda other: field[base + other]
+            load = lambda other: field(base + other)
             close = lambda other: near[base + other]
             value = mix(diag, load, mode, (stiff + diag[0]) * load(mode))
             value = value - mix(
@@ -176,7 +176,7 @@
 def finish_chunk(start, image, near, grown_near, coef, diag, stiff, image_out, second_out, lanes, sums):
     def store(number, value, sums):
         rr, rq, qq, qz = sums
-        first, here = start[number], image[number]
+        first, here = start(number), image(number)
         image_out[number, :, lanes] = here[:ROWS]
         second_out[number, :, lanes] = value[:ROWS]
         return rr + first * first, rq + first * here, qq + here * here, qz + here * value
@@ -186,24 +186,27 @@
 
 def fill_diag(table, field, near, weights_ref):
     weight_sum = sum(weights_ref[number] for number in range(13))
-    fill(table, [field[FIELDS + t] * weight_sum + near[FIELDS + t] for t in range(TERMS)])
+    fill(table, [field(FIELDS + t) * weight_sum + near[FIELDS + t] for t in range(TERMS)])
+
+
+def chunk_of(ref, k):
+    lanes = pl.ds(pl.multiple_of(k * LANES, LANES), LANES)
+    return lambda number: ref[number, :, lanes]
+
+
+def entry_of(ref):
+    return lambda number: ref[number]
 
 
 def inner_kernel(
-    own_ref, extra_ref, upper_ref, lower_ref, matrix_ref, weights_ref,
-    field, grown_high, grown_low, outer_near, outer_grown_near,
+    tall_ref, matrix_ref, weights_ref,
+    grown_high, grown_low, outer_near, outer_grown_near,
     image, image_high, image_low, image_grown_high, image_grown_low, coef_table, diag_table,
     image_ref, second_ref, sums_ref,
     field_high, field_low, grown, near, grown_near,
 ):
-    chunks = field.shape[0]
+    chunks = image.shape[0]
     for k in range(chunks):
-        lanes = pl.ds(k * LANES, LANES)
-        field[k, :FIELDS, 0:ROWS, :] = own_ref[:, :, lanes]
-        field[k, FIELDS : STIFF + 1, 0:ROWS, :] = extra_ref[:, :, lanes]
-        field[k, : STIFF + 1, ROWS : ROWS + 2, :] = upper_ref[:, :, lanes]
-        field[k, : STIFF + 1, ROWS + 2 : ROWS + 4, :] = lower_ref[:, :, lanes]
-        field[k, STIFF + 1] = jnp.zeros((8, LANES), jnp.float32)
         image[k, FIELDS] = jnp.zeros((8, LANES), jnp.float32)
     grown[FIELDS] = jnp.zeros((8, LANES), jnp.float32)
     for ref in (field_high, field_low, grown_high, grown_low):
@@ -214,18 +217,20 @@
 
     @pl.loop(0, chunks)
     def grow_field(k):
-        fill(coef_table.at[k], [field[k, FIELDS + term] for term in range(TERMS)])
-        grow(field.at[k], coef_table.at[k], grown)
+        field = chunk_of(tall_ref, k)
+        fill(coef_table.at[k], [field(FIELDS + term) for term in range(TERMS)])
+        grow(field, coef_table.at[k], grown)
         grown_high[k], grown_low[k] = halves(grown[...])
-        field_high[k], field_low[k] = halves(field[k])
+        field_high[k], field_low[k] = halves(field(slice(None)))
 
     @pl.loop(0, chunks)
     def first(k):
         after, before = step(k)
+        field = chunk_of(tall_ref, k)
         for high, low, out in ((field_high, field_low, near), (grown_high, grown_low, grown_near)):
-            stencil(*[(high[at], low[at]) for at in (k, after, before)], matrix_ref, out)
-        fill_diag(diag_table.at[k], field.at[k], near, weights_ref)
-        stiff = field[k, STIFF]
+            stencil(*[(high[at], low[at]) for at in (k, after, before)], matrix_ref.at[0], out)
+        fill_diag(diag_table.at[k], field, near, weights_ref)
+        stiff = field(STIFF)
         inside = stiff > 0.0
 
         def store(number, value, carry):
@@ -235,7 +240,7 @@
         lax.fori_loop(
             0,
             COMPS,
-            apply(field.at[k], near, grown_near, coef_table.at[k], diag_table.at[k], stiff, store),
+            apply(field, near, grown_near, coef_table.at[k], diag_table.at[k], stiff, store),
             0,
         )
 
@@ -251,7 +256,7 @@
 
     @pl.loop(0, chunks)
     def grow_image(k):
-        grow(image.at[k], coef_table.at[k], grown)
+        grow(entry_of(image.at[k]), coef_table.at[k], grown)
         image_grown_high[k], image_grown_low[k] = halves(grown[...])
         image_high[k], image_low[k] = halves(image[k])
 
@@ -263,11 +268,12 @@
             (image_high, image_low, image_near),
             (image_grown_high, image_grown_low, grown_near),
         ):
-            stencil(*[(high[at], low[at]) for at in (k, k + 1, k - 1)], matrix_ref, out)
+            stencil(*[(high[at], low[at]) for at in (k, k + 1, k - 1)], matrix_ref.at[0], out)
+        field = chunk_of(tall_ref, k)
         lanes = pl.ds(pl.multiple_of((k - 1) * LANES, LANES), LANES)
         return finish_chunk(
-            field.at[k], image.at[k], image_near, grown_near, coef_table.at[k], diag_table.at[k],
-            field[k, STIFF], image_ref, second_ref, lanes, sums,
+            field, entry_of(image.at[k]), image_near, grown_near, coef_table.at[k], diag_table.at[k],
+            field(STIFF), image_ref, second_ref, lanes, sums,
         )
 
     sums = lax.fori_loop(1, chunks - 1, second, (zero, zero, zero, zero))
@@ -276,13 +282,14 @@
 
 
 def outer_kernel(
-    right_ref, left_ref, matrix_ref, rim_matrix_ref, weights_ref,
-    field, grown_high, grown_low, outer_near, outer_grown_near,
+    right_ref, left_ref, tall_ref, matrix_ref, weights_ref,
+    grown_high, grown_low, outer_near, outer_grown_near,
     image, image_high, image_low, image_grown_high, image_grown_low, coef_table, diag_table, before_ref,
     image_ref, second_ref, sums_ref,
     edge, rim, grown, near, grown_near, rim_image, edge_image, coef, diag, edge_coef, ends,
 ):
-    final = field.shape[0] - 1
+    final = image.shape[0] - 1
+    first_field, last_field = chunk_of(tall_ref, 0), chunk_of(tall_ref, final)
     lane = lax.broadcasted_iota(jnp.int32, (8, LANES), 1)
     zero = jnp.zeros((8, LANES), jnp.float32)
     edge[: STIFF + 1] = jnp.concatenate([right_ref[...], left_ref[...]], axis=2)
@@ -299,15 +306,15 @@
         return jnp.where(lane < WIDE, right, left)
 
     fill(edge_coef, [edge[FIELDS + term] for term in range(TERMS)])
-    grow(edge, edge_coef, grown)
+    grow(entry_of(edge), edge_coef, grown)
     edge_parts = halves(edge[...])
-    begin, last = halves(field[0]), halves(field[final])
-    stencil(edge_parts, begin, last, rim_matrix_ref, near)
+    begin, last = halves(first_field(slice(None))), halves(last_field(slice(None)))
+    stencil(edge_parts, begin, last, matrix_ref.at[1], near)
     stencil(
         halves(grown[...]),
         (grown_high[0], grown_low[0]),
         (grown_high[final], grown_low[final]),
-        rim_matrix_ref,
+        matrix_ref.at[1],
         grown_near,
     )
     left_rim, right_rim = lane >= 3 * CZ, lane < CZ
@@ -318,9 +325,9 @@
 
     near[...] = near[...] + own_part(outer_near[1], outer_near[0])
     grown_near[...] = grown_near[...] + own_part(outer_grown_near[1], outer_grown_near[0])
-    rim[...] = to_rim(field[final], edge[...], field[0])
+    rim[...] = to_rim(last_field(slice(None)), edge[...], first_field(slice(None)))
     fill(coef, [rim[FIELDS + term] for term in range(TERMS)])
-    fill_diag(diag, rim, near, weights_ref)
+    fill_diag(diag, entry_of(rim), near, weights_ref)
     stiff = rim[STIFF]
     inside = stiff > 0.0
 
@@ -328,8 +335,8 @@
         rim_image[number] = jnp.where(inside, value, 0.0)
         return carry
 
-    lax.fori_loop(0, COMPS, apply(rim, near, grown_near, coef, diag, stiff, store), 0)
-    grow(rim_image, coef, grown)
+    lax.fori_loop(0, COMPS, apply(entry_of(rim), near, grown_near, coef, diag, stiff, store), 0)
+    grow(entry_of(rim_image), coef, grown)
 
     def from_rim(value):
         return pltpu.roll(value, CZ, value.ndim - 1), pltpu.roll(value, LANES - CZ, value.ndim - 1)
@@ -364,7 +371,7 @@
         coef[entry] = jnp.where(lane >= 3 * CZ, to_right, diag_table[final, entry])
     image_near = near.at[pl.ds(0, FIELDS + 1)]
     sums = tuple(before_ref[number] for number in range(4))
-    for side, k, table in ((0, 0, edge_coef), (1, final, coef)):
+    for side, k, table, field in ((0, 0, edge_coef, first_field), (1, final, coef, last_field)):
         for (begin, last, beyond), high, low, out in (
             (image_parts, image_high, image_low, image_near),
             (grown_parts, image_grown_high, image_grown_low, grown_near),
@@ -373,10 +380,10 @@
                 chunk = (begin, (high[1], low[1]), beyond)
             else:
                 chunk = (last, beyond, (high[final - 1], low[final - 1]))
-            stencil(*chunk, matrix_ref, out)
+            stencil(*chunk, matrix_ref.at[0], out)
         sums = finish_chunk(
-            field.at[k], ends.at[side], image_near, grown_near, coef_table.at[k], table,
-            field[k, STIFF], image_ref, second_ref, pl.ds(side * LANES, LANES), sums,
+            field, entry_of(ends.at[side]), image_near, grown_near, coef_table.at[k], table,
+            field(STIFF), image_ref, second_ref, pl.ds(side * LANES, LANES), sums,
         )
     inner = lax.broadcasted_iota(jnp.int32, (8, LANES), 0) < ROWS
     column = lax.broadcasted_iota(jnp.int32, sums_ref.shape, 1)
@@ -419,18 +426,30 @@
     return lax.ppermute(value, axis, [(i, i + by) for i in range(size) if 0 <= i + by < size])
 
 
+def swap(value, axis, begin):
+    size = lax.axis_size(axis)
+    pairs = [(i, i + 1) for i in range(begin, size - 1, 2)]
+    return lax.ppermute(value, axis, pairs + [(j, i) for i, j in pairs])
+
+
 def per_device(right_side, stiffness, coefficients, stencil_weights):
     columns = right_side.shape[3]
     chunks = columns // LANES
     devices = lax.axis_size("down") * lax.axis_size("cross")
     own = right_side.reshape(FIELDS, ROWS, columns)
     extra = jnp.concatenate([coefficients, stiffness[None]], axis=0)
-    all_fields = jnp.concatenate([own, extra], axis=0)
-    upper = shift(all_fields[:, :2], "down", -1)
-    lower = shift(all_fields[:, ROWS - 2 :], "down", 1)
-    tall = jnp.concatenate([all_fields, upper, lower], axis=1)
-    right = shift(tall[:, :, :WIDE], "cross", -1)
-    left = shift(tall[:, :, columns - WIDE :], "cross", 1)
+    spare = jnp.zeros((1, ROWS, columns), jnp.float32)
+    all_fields = jnp.concatenate([own, extra, spare], axis=0)
+    even = lax.axis_index("down") % 2 == 0
+    head, tail = all_fields[: STIFF + 1, :2], all_fields[: STIFF + 1, ROWS - 2 :]
+    one = swap(jnp.where(even, tail, head), "down", 0)
+    other = swap(jnp.where(even, head, tail), "down", 1)
+    upper, lower = jnp.where(even, one, other), jnp.where(even, other, one)
+    beyond = jnp.concatenate([upper, lower], axis=1)
+    beyond = jnp.concatenate([beyond, spare], axis=0)
+    tall = jnp.concatenate([all_fields, beyond], axis=1)
+    right = shift(tall[: STIFF + 1, :, :WIDE], "cross", -1)
+    left = shift(tall[: STIFF + 1, :, columns - WIDE :], "cross", 1)
     vmem = pl.BlockSpec(memory_space=pltpu.VMEM)
     smem = pl.BlockSpec(memory_space=pltpu.SMEM)
     f32, bf16 = jnp.float32, jnp.bfloat16
@@ -443,7 +462,6 @@
         out_specs=pl.BlockSpec((1, 3 * SLOTS.shape[1], SLOTS.shape[2]), lambda i: (i, 0, 0)),
         name="matrix",
     )(stencil_weights, jnp.asarray(SLOTS))
-    matrix, rim_matrix = matrices[0], matrices[1]
     shape = jax.ShapeDtypeStruct
     count, wider = FIELDS + 1, STIFF + 2
     tiles = lambda number: (number, 8, LANES)
@@ -452,7 +470,6 @@
     *kept, image, second, sums = pl.pallas_call(
         inner_kernel,
         out_shape=(
-            shape((chunks,) + tiles(wider), f32),
             shape((chunks + 1,) + rows(count), bf16),
             shape((chunks + 1,) + rows(count), bf16),
             shape((2,) + tiles(wider), f32),
@@ -468,8 +485,8 @@
             shape(half, f32),
             shape(tiles(4), f32),
         ),
-        in_specs=[vmem] * 5 + [smem],
-        out_specs=(vmem,) * 15,
+        in_specs=[vmem] * 2 + [smem],
+        out_specs=(vmem,) * 14,
         scratch_shapes=[
             pltpu.VMEM((chunks + 1,) + rows(wider), bf16),
             pltpu.VMEM((chunks + 1,) + rows(wider), bf16),
@@ -480,11 +497,11 @@
         compiler_params=params,
         cost_estimate=pl.CostEstimate(flops=10**10, bytes_accessed=0, transcendentals=0),
         name="inner",
-    )(own, extra, upper, lower, matrix, stencil_weights)
+    )(tall, matrices, stencil_weights)
     outer_image, outer_second, sums = pl.pallas_call(
         outer_kernel,
         out_shape=(shape(half, f32), shape(half, f32), shape((devices, LANES), f32)),
-        in_specs=[vmem] * 4 + [smem] + [vmem] * 13,
+        in_specs=[vmem] * 4 + [smem] + [vmem] * 12,
         out_specs=(vmem,) * 3,
         scratch_shapes=[
             pltpu.VMEM(tiles(wider), f32),
@@ -501,7 +518,7 @@
         ],
         compiler_params=params,
         name="outer",
-    )(right, left, matrix, rim_matrix, stencil_weights, *kept, sums)
+    )(right, left, tall, matrices, stencil_weights, *kept, sums)
     sums = lax.all_to_all(sums, ("down", "cross"), 0, 0, tiled=True)
     solution_field, residual = pl.pallas_call(
         finish_kernel,

time: 73.8 us -> 71 us (0.962)
  starting transfers between devices: 12.9 us -> 9.4 us
  waiting for transfers between devices: 4.92 us -> 6.78 us
  local copies, waits for them, and re-layouts: 1.82 us -> 0.22 us
  other arithmetic: 1.91 us -> 2.89 us
    ppermute x0 -> x2, waiting for transfers between devices: none -> 6.77 us  [swap(): return lax.ppermute(value, axis, pairs + [(j, i) for i, j in pairs])]
    ppermute x4 -> x2, starting transfers between devices: 12.9 us -> 6.17 us  [shift(): lax.ppermute(value, axis, [(i, i + by) for i in range(size) if 0 <= i + b...]
    ppermute x4 -> x2, waiting for transfers between devices: 4.92 us -> 0.01 us  [shift(): lax.ppermute(value, axis, [(i, i + by) for i in range(size) if 0 <= i + b...]
    ppermute x0 -> x2, starting transfers between devices: none -> 3.22 us  [swap(): return lax.ppermute(value, axis, pairs + [(j, i) for i, j in pairs])]
    squeeze x1 -> x0, local copies, waits for them, and re-layouts: 1.44 us -> none  [per_device(): matrix, rim_matrix = (matrices[0], matrices[1])]
  transfers between devices with their start and end apart: 4 -> 4, of which waited for: 2 -> 1; matrix products, arithmetic and copies ran while one was open for 2% -> 0% of each run, Pallas kernels for 24% -> 24%
where the time goes in v4:
time: 71 us; the launch traced here: 70.8 us
  Pallas kernels  26.3 us (37%)
  blocking collectives  24.4 us (34%)
  starting transfers between devices  9.4 us (13%)
  waiting for transfers between devices  6.78 us (10%)
  other arithmetic  2.89 us (4%)
  between operations  0.8 us (1%)
    all_to_all x1, blocking collectives, per_device(): sums = lax.all_to_all(sums, ('down', 'cross'), 0, 0, tiled=True)  24.4 us
    pallas_call x1, Pallas kernels, per_device(): pl.pallas_call(inner_kernel, out_shape=(shape((chunks + 1,) + rows(count)...  14.5 us
    pallas_call x1, Pallas kernels, per_device(): pl.pallas_call(outer_kernel, out_shape=(shape(half, f32), shape(half, f32...  7.18 us
    ppermute x2, waiting for transfers between devices, swap(): return lax.ppermute(value, axis, pairs + [(j, i) for i, j in pairs])  6.77 us
    ppermute x2, starting transfers between devices, shift(): lax.ppermute(value, axis, [(i, i + by) for i in range(size) if 0 <= i + b...  6.17 us
    ppermute x2, starting transfers between devices, swap(): return lax.ppermute(value, axis, pairs + [(j, i) for i, j in pairs])  3.22 us
    pallas_call x1, Pallas kernels, per_device(): pl.pallas_call(matrix_kernel, grid=(2,), out_shape=jax.ShapeDtypeStruct((...  2.65 us
    pallas_call x1, Pallas kernels, per_device(): pl.pallas_call(finish_kernel, out_shape=(shape(own.shape, f32), shape(own...  1.93 us
  transfers between devices with their start and end apart: 4, of which 1 were waited for; matrix products, arithmetic and copies ran while one was open for 0% of the time, Pallas kernels for 24%

profile of v4, /device:TPU:1, one launch (start us, length us, event | category | flops | bytes accessed | tf_op | source)
XLA Modules:
  0.0 70.8 jit_solution(3228759390728867187)
XLA Ops:
  0.6 1.4 %pad_maximum_fusion.1 = f32[111,4,512]{2,1,0:T(4,128)S(1)} fusion(f32[1,4,512]{2,1,0:T(4,128)} %bitcast.13, f32[5,4,512]{2,1,0:T(4,128)} %param.7, f32[105,4,512]{2,1,0:T(4,128)} %bitcast.8), kind=kLoop, calls=%fused_computation.3 | loop fusion | flops 454656 | bytes 1818624 | tf_op jit(solution)/shard_map/concatenate | solution.py:442
  2.0 0.3 broadcast_select_fusion.3
  2.4 2.5 %collective-permute-start = (f32[111,2,512]{2,1,0:T(2,128)S(1)}, f32[111,2,512]{2,1,0:T(2,128)S(1)}, u32[]{:S(2)}, u32[]{:S(2)}) collective-permute-start(f32[111,2,512]{2,1,0:T(2,128)S(1)} %get-tuple-element.44), channel_id=1, source_target_pairs={{0,16},{32,48},{64,80},{96,112},{16,0},{48,32},{80,64},{112,96},{1... | collective-permute-start | bytes 1363976 | tf_op jit(solution)/shard_map/ppermute | solution.py:432
  4.9 0.7 collective-permute-start.1
  5.6 2.6 %matrix.1.matrix_ref = bf16[2,768,384]{2,1,0:T(8,128)(2,1)} custom-call(f32[13]{0:T(128)} %weights_ref.5, s32[2,256,384]{2,1,0:T(8,128)} %constant.24.clone.slots_ref), custom_call_target="tpu_custom_call" | custom-call | tf_op jit(solution)/shard_map/matrix/pallas_call | solution.py:457
  8.3 6.8 %collective-permute-done = f32[111,2,512]{2,1,0:T(2,128)S(1)} collective-permute-done((f32[111,2,512]{2,1,0:T(2,128)S(1)}, f32[111,2,512]{2,1,0:T(2,128)S(1)}, u32[]{:S(2)}, u32[]{:S(2)}) %collective-permute-start) | collective-permute-done | bytes 454688 | tf_op jit(solution)/shard_map/ppermute | solution.py:432
  15.1 0.0 collective-permute-done.1
  15.1 0.3 broadcast_select_fusion.1
  15.4 0.4 select_maximum_fusion
  15.8 0.0 copy-done
  15.8 0.0 copy-done.3
  15.8 0.0 copy-done.4
  15.8 0.0 copy-start.1
  15.8 0.0 copy-start.2
  15.9 0.4 pad_maximum_fusion.tall_ref
  16.3 0.2 fusion
  16.5 4.3 %collective-permute-start.3 = (f32[111,8,64]{2,1,0:T(8,128)S(1)}, f32[111,8,64]{2,1,0:T(8,128)S(1)}, u32[]{:S(2)}, u32[]{:S(2)}) collective-permute-start(f32[111,8,64]{2,1,0:T(8,128)S(1)} %get-tuple-element.40), channel_id=1, source_target_pairs={{0,1},{1,2},{2,3},{3,4},{4,5},{5,6},{6,7},{7,8},{8,9},{9,10},{10,1... | collective-permute-start | bytes 681992 | tf_op jit(solution)/shard_map/ppermute | solution.py:426
  20.7 1.9 %collective-permute-start.2 = (f32[111,8,64]{2,1,0:T(8,128)S(1)}, f32[111,8,64]{2,1,0:T(8,128)S(1)}, u32[]{:S(2)}, u32[]{:S(2)}) collective-permute-start(f32[111,8,64]{2,1,0:T(8,128)S(1)} %get-tuple-element.41), channel_id=1, source_target_pairs={{1,0},{2,1},{3,2},{4,3},{5,4},{6,5},{7,6},{8,7},{9,8},{10,9},{11,1... | collective-permute-start | bytes 681992 | tf_op jit(solution)/shard_map/ppermute | solution.py:426
  22.7 14.5 %inner.1 = (bf16[5,848,128]{2,1,0:T(8,128)(2,1)S(1)}, bf16[5,848,128]{2,1,0:T(8,128)(2,1)S(1)}, f32[2,112,8,128]{3,2,1,0:T(8,128)S(1)}, f32[2,106,8,128]{3,2,1,0...) custom-call(f32[112,8,512]{2,1,0:T(8,128)S(1)} %pad_maximum_fusion.t, ...), custom_call_target="tpu_custom_call" | custom-call | flops 10000000000 | tf_op jit(solution)/shard_map/inner/pallas_call | solution.py:470
  37.2 0.0 collective-permute-done.3.left_ref
  37.2 0.0 collective-permute-done.2.right_ref
  37.3 7.2 %outer.1 = (f32[105,4,256]{2,1,0:T(4,128)S(1)}, f32[105,4,256]{2,1,0:T(4,128)S(1)}, f32[128,128]{1,0:T(8,128)S(1)}) custom-call(f32[111,8,64]{2,1,0:T(8,128)S(1)} %collective-permute-done.2.right_ref, f32[111,8,64]{2,1,0:T(8,128)S(1)} %collective-permute-done.3.left_ref, f32[112,8,512]{2,1,0:T(8,128)S(1)} %pad_maximum_fusion.tall_ref, ...), custom_call_target="tpu_custom_call" | custom-call | tf_op jit(solution)/shard_map/outer/pallas_call | solution.py:501
  44.4 24.4 %all_to_all.11 = f32[128,1,128]{2,1,0:T(1,128)S(1)} all-to-all(f32[128,1,128]{2,1,0:T(1,128)S(1)} %bitcast.12), channel_id=1, replica_groups=mesh['down'=8,'cross'=16] {'down','cross'}, dimensions={0} | all-to-all | bytes 131072 | tf_op jit(solution)/shard_map/all_to_all | solution.py:522
  68.8 1.9 %finish.1 = (f32[105,4,512]{2,1,0:T(4,128)}, f32[105,4,512]{2,1,0:T(4,128)}) custom-call(f32[128,128]{1,0:T(8,128)S(1)} %bitcast.11, f32[105,4,512]{2,1,0:T(4,128)S(1)} %bitcast.10, f32[105,4,256]{2,1,0:T(4,128)S(1)} %get-tuple-element.34.refs_0_, f32[105,4,256]{2,1,0:T(4,128)S(1)} %get-tuple-element.35.refs_1_, ...), custom_call_target="tpu_custom_call" | custom-call | tf_op jit(solution)/shard_map/finish/pallas_call | solution.py:523
  (7 shorter events, 0.0 us)
Async XLA Ops:
  2.4 12.7 %collective-permute-start = (f32[111,2,512]{2,1,0:T(2,128)S(1)}, f32[111,2,512]{2,1,0:T(2,128)S(1)}, u32[]{:S(2)}, u32[]{:S(2)}) collective-permute-start(f32[111,2,512]{2,1,0:T(2,128)S(1)} %get-tuple-element.44), channel_id=1, source_target_pairs={{0,16},{32,48},{64,80},{96,112},{16,0},{48,32},{80,64},{112,96},{1... | collective-permute-start | bytes 1363976 | tf_op jit(solution)/shard_map/ppermute | solution.py:432
  4.9 10.1 %collective-permute-start.1 = (f32[111,2,512]{2,1,0:T(2,128)S(1)}, f32[111,2,512]{2,1,0:T(2,128)S(1)}, u32[]{:S(2)}, u32[]{:S(2)}) collective-permute-start(f32[111,2,512]{2,1,0:T(2,128)S(1)} %get-tuple-element.45), channel_id=1, source_target_pairs={{16,32},{48,64},{80,96},{32,16},{64,48},{96,80},{17,33},{49,65},{8... | collective-permute-start | bytes 1363976 | tf_op jit(solution)/shard_map/ppermute | solution.py:432
  8.3 7.5 %copy-start = (f32[3,35,4,512]{3,2,1,0:T(4,128)S(1)}, f32[3,35,4,512]{3,2,1,0:T(4,128)}, u32[]{:S(2)}) copy-start(f32[3,35,4,512]{3,2,1,0:T(4,128)} %param.5) | copy-start | bytes 2580484
  8.3 7.5 %copy-start.3 = (f32[5,4,512]{2,1,0:T(4,128)S(1)}, f32[5,4,512]{2,1,0:T(4,128)}, u32[]{:S(2)}) copy-start(f32[5,4,512]{2,1,0:T(4,128)} %param.7) | copy-start | bytes 122884
  8.3 7.5 %copy-start.4 = (f32[4,512]{1,0:T(4,128)S(1)}, f32[4,512]{1,0:T(4,128)}, u32[]{:S(2)}) copy-start(f32[4,512]{1,0:T(4,128)} %param.6) | copy-start | bytes 24580
  15.8 6.8 %copy-start.1 = (bf16[2,768,384]{2,1,0:T(8,128)(2,1)S(1)}, bf16[2,768,384]{2,1,0:T(8,128)(2,1)}, u32[]{:S(2)}) copy-start(bf16[2,768,384]{2,1,0:T(8,128)(2,1)} %matrix.1.matrix_ref) | copy-start | bytes 3538948
  15.8 6.8 %copy-start.2 = (f32[13]{0:T(128)S(1)}, f32[13]{0:T(128)}, u32[]{:S(2)}) copy-start(f32[13]{0:T(128)} %weights_ref.5) | copy-start | bytes 160
  16.5 20.8 %collective-permute-start.3 = (f32[111,8,64]{2,1,0:T(8,128)S(1)}, f32[111,8,64]{2,1,0:T(8,128)S(1)}, u32[]{:S(2)}, u32[]{:S(2)}) collective-permute-start(f32[111,8,64]{2,1,0:T(8,128)S(1)} %get-tuple-element.40), channel_id=1, source_target_pairs={{0,1},{1,2},{2,3},{3,4},{4,5},{5,6},{6,7},{7,8},{8,9},{9,10},{10,1... | collective-permute-start | bytes 681992 | tf_op jit(solution)/shard_map/ppermute | solution.py:426
  20.7 16.5 %collective-permute-start.2 = (f32[111,8,64]{2,1,0:T(8,128)S(1)}, f32[111,8,64]{2,1,0:T(8,128)S(1)}, u32[]{:S(2)}, u32[]{:S(2)}) collective-permute-start(f32[111,8,64]{2,1,0:T(8,128)S(1)} %get-tuple-element.41), channel_id=1, source_target_pairs={{1,0},{2,1},{3,2},{4,3},{5,4},{6,5},{7,6},{8,7},{9,8},{10,9},{11,1... | collective-permute-start | bytes 681992 | tf_op jit(solution)/shard_map/ppermute | solution.py:426

commit v5 on v4

--- a/solution.py
+++ b/solution.py
@@ -133,6 +133,32 @@
     return high, (value - high.astype(jnp.float32)).astype(jnp.bfloat16)
 
 
+def paired_mixes(first, second, lead):
+    left = lax.broadcasted_iota(jnp.int32, (8, LANES), 1) < WIDE
+    turned, other = pltpu.roll(first, 4, 1), pltpu.roll(second, 4, 1)
+    return (
+        jnp.where(left, jnp.where(lead, turned, other), jnp.where(lead, 0.0, turned)),
+        jnp.where(left, jnp.where(lead, other, 0.0), jnp.where(lead, turned, other)),
+    )
+
+
+def paired_stencil(pairs, lead, matrix, store):
+    mixes = paired_mixes(pairs[0], pairs[1], lead)
+    for number, (pair, beside) in enumerate(zip(pairs, mixes)):
+        own, near = halves(pair), halves(beside)
+        lines = jnp.concatenate([own[0], near[0], own[1], near[1], own[0], near[0]], axis=1)
+        parts = jnp.dot(lines, matrix[...], preferred_element_type=jnp.float32)
+        parts = [
+            parts[:, n * LANES : (n + 1) * LANES].reshape(pair.shape) for n in range(3)
+        ]
+        for chunk, mask, turns in ((2 * number, lead, (0, 7, 1)), (2 * number + 1, ~lead, (4, 3, 5))):
+            terms = [
+                pltpu.roll(value, turn, 1) if turn else value
+                for value, turn in zip([jnp.where(mask, part, 0.0) for part in parts], turns)
+            ]
+            store(chunk, terms[0] + terms[1] + terms[2])
+
+
 def fill(table, values):
     table[0] = values[0]
     for variable in range(VARS):
@@ -198,38 +224,68 @@
     return lambda number: ref[number]
 
 
+def grow_pairs(pairs, grown):
+    for number in range(2):
+        field = entry_of(pairs.at[number])
+        table = [field(FIELDS + term) for term in range(TERMS)]
+        table = [table[0]] + [
+            table[1 + variable] * CHAOS_VALUES[degree]
+            for variable in range(VARS)
+            for degree in range(DEG)
+        ]
+        grow(field, table, grown.at[number])
+        grown[number, FIELDS] = jnp.zeros((8, LANES), jnp.float32)
+
+
+def start_kernel(own_ref, extra_ref, matrix_ref, near_ref, grown_near_ref, grown_ref, pairs):
+    for number in range(2):
+        for side in range(2):
+            lanes, rows = pl.ds((2 * number + side) * LANES, LANES), pl.ds(side * ROWS, ROWS)
+            pairs[number, :FIELDS, rows, :] = own_ref[:, :, lanes]
+            pairs[number, FIELDS : STIFF + 1, rows, :] = extra_ref[:, :, lanes]
+        pairs[number, STIFF + 1] = jnp.zeros((8, LANES), jnp.float32)
+    grow_pairs(pairs, grown_ref)
+    lead = lax.broadcasted_iota(jnp.int32, (8, LANES), 0) < ROWS
+    for ref, out in ((pairs, near_ref), (grown_ref, grown_near_ref)):
+
+        def store(chunk, value):
+            out[chunk] = value
+
+        paired_stencil([ref[0], ref[1]], lead, matrix_ref.at[0], store)
+
+
 def inner_kernel(
-    tall_ref, matrix_ref, weights_ref,
-    grown_high, grown_low, outer_near, outer_grown_near,
+    tall_ref, matrix_ref, weights_ref, own_near, own_grown_near,
+    halo_grown, outer_near, outer_grown_near,
     image, image_high, image_low, image_grown_high, image_grown_low, coef_table, diag_table,
     image_ref, second_ref, sums_ref,
-    field_high, field_low, grown, near, grown_near,
+    pairs, grown, near, grown_near,
 ):
     chunks = image.shape[0]
+    final = chunks - 1
     for k in range(chunks):
         image[k, FIELDS] = jnp.zeros((8, LANES), jnp.float32)
     grown[FIELDS] = jnp.zeros((8, LANES), jnp.float32)
-    for ref in (field_high, field_low, grown_high, grown_low):
-        ref[chunks] = jnp.zeros(ref.shape[1:], jnp.bfloat16)
-
-    def step(k):
-        return lax.rem(k + 1, chunks + 1), lax.rem(k + chunks, chunks + 1)
+    lead = lax.broadcasted_iota(jnp.int32, (8, LANES), 0) >= ROWS
+    for number in range(2):
+        one, other = [tall_ref[:, :, pl.ds((2 * number + n) * LANES, LANES)] for n in range(2)]
+        pairs[number] = jnp.where(lead, one, pltpu.roll(other, ROWS, 1))
+    grow_pairs(pairs, halo_grown)
+    for ref, before, out in ((pairs, own_near, near), (halo_grown, own_grown_near, grown_near)):
+
+        def store(chunk, value):
+            out[chunk] = before[chunk] + value
+
+        paired_stencil([ref[0], ref[1]], lead, matrix_ref.at[0], store)
+    for side, k in enumerate((0, final)):
+        outer_near[side] = near[k]
+        outer_grown_near[side] = grown_near[k]
 
     @pl.loop(0, chunks)
-    def grow_field(k):
+    def first(k):
         field = chunk_of(tall_ref, k)
         fill(coef_table.at[k], [field(FIELDS + term) for term in range(TERMS)])
-        grow(field, coef_table.at[k], grown)
-        grown_high[k], grown_low[k] = halves(grown[...])
-        field_high[k], field_low[k] = halves(field(slice(None)))
-
-    @pl.loop(0, chunks)
-    def first(k):
-        after, before = step(k)
-        field = chunk_of(tall_ref, k)
-        for high, low, out in ((field_high, field_low, near), (grown_high, grown_low, grown_near)):
-            stencil(*[(high[at], low[at]) for at in (k, after, before)], matrix_ref.at[0], out)
-        fill_diag(diag_table.at[k], field, near, weights_ref)
+        fill_diag(diag_table.at[k], field, near.at[k], weights_ref)
         stiff = field(STIFF)
         inside = stiff > 0.0
 
@@ -240,19 +296,11 @@
         lax.fori_loop(
             0,
             COMPS,
-            apply(field, near, grown_near, coef_table.at[k], diag_table.at[k], stiff, store),
+            apply(
+                field, near.at[k], grown_near.at[k], coef_table.at[k], diag_table.at[k], stiff, store
+            ),
             0,
         )
-
-        @pl.when(k == 0)
-        def _():
-            outer_near[0] = near[...]
-            outer_grown_near[0] = grown_near[...]
-
-        @pl.when(k == chunks - 1)
-        def _():
-            outer_near[1] = near[...]
-            outer_grown_near[1] = grown_near[...]
 
     @pl.loop(0, chunks)
     def grow_image(k):
@@ -260,19 +308,19 @@
         image_grown_high[k], image_grown_low[k] = halves(grown[...])
         image_high[k], image_low[k] = halves(image[k])
 
-    image_near = near.at[pl.ds(0, FIELDS + 1)]
+    image_near, image_grown_near = near.at[0, pl.ds(0, FIELDS + 1)], grown_near.at[0]
     zero = jnp.zeros((8, LANES), jnp.float32)
 
     def second(k, sums):
         for high, low, out in (
             (image_high, image_low, image_near),
-            (image_grown_high, image_grown_low, grown_near),
+            (image_grown_high, image_grown_low, image_grown_near),
         ):
             stencil(*[(high[at], low[at]) for at in (k, k + 1, k - 1)], matrix_ref.at[0], out)
         field = chunk_of(tall_ref, k)
         lanes = pl.ds(pl.multiple_of((k - 1) * LANES, LANES), LANES)
         return finish_chunk(
-            field, entry_of(image.at[k]), image_near, grown_near, coef_table.at[k], diag_table.at[k],
+            field, entry_of(image.at[k]), image_near, image_grown_near, coef_table.at[k], diag_table.at[k],
             field(STIFF), image_ref, second_ref, lanes, sums,
         )
 
@@ -282,18 +330,16 @@
 
 
 def outer_kernel(
-    right_ref, left_ref, tall_ref, matrix_ref, weights_ref,
-    grown_high, grown_low, outer_near, outer_grown_near,
+    edge, tall_ref, matrix_ref, weights_ref,
+    own_grown, halo_grown, outer_near, outer_grown_near,
     image, image_high, image_low, image_grown_high, image_grown_low, coef_table, diag_table, before_ref,
     image_ref, second_ref, sums_ref,
-    edge, rim, grown, near, grown_near, rim_image, edge_image, coef, diag, edge_coef, ends,
+    rim, grown, near, grown_near, rim_image, edge_image, coef, diag, edge_coef, ends,
 ):
     final = image.shape[0] - 1
     first_field, last_field = chunk_of(tall_ref, 0), chunk_of(tall_ref, final)
     lane = lax.broadcasted_iota(jnp.int32, (8, LANES), 1)
     zero = jnp.zeros((8, LANES), jnp.float32)
-    edge[: STIFF + 1] = jnp.concatenate([right_ref[...], left_ref[...]], axis=2)
-    edge[STIFF + 1] = zero
     grown[FIELDS] = zero
     rim_image[FIELDS] = zero
     for side in range(2):
@@ -307,13 +353,14 @@
 
     fill(edge_coef, [edge[FIELDS + term] for term in range(TERMS)])
     grow(entry_of(edge), edge_coef, grown)
+    top = lax.broadcasted_iota(jnp.int32, (8, LANES), 0) < ROWS
     edge_parts = halves(edge[...])
     begin, last = halves(first_field(slice(None))), halves(last_field(slice(None)))
     stencil(edge_parts, begin, last, matrix_ref.at[1], near)
     stencil(
         halves(grown[...]),
-        (grown_high[0], grown_low[0]),
-        (grown_high[final], grown_low[final]),
+        halves(jnp.where(top, own_grown[0], halo_grown[0])),
+        halves(pltpu.roll(jnp.where(top, halo_grown[1], own_grown[1]), ROWS, 1)),
         matrix_ref.at[1],
         grown_near,
     )
@@ -448,8 +495,13 @@
     beyond = jnp.concatenate([upper, lower], axis=1)
     beyond = jnp.concatenate([beyond, spare], axis=0)
     tall = jnp.concatenate([all_fields, beyond], axis=1)
-    right = shift(tall[: STIFF + 1, :, :WIDE], "cross", -1)
-    left = shift(tall[: STIFF + 1, :, columns - WIDE :], "cross", 1)
+    even = lax.axis_index("cross") % 2 == 0
+    head, tail = tall[: STIFF + 1, :, :WIDE], tall[: STIFF + 1, :, columns - WIDE :]
+    one = swap(jnp.where(even, tail, head), "cross", 0)
+    other = swap(jnp.where(even, head, tail), "cross", 1)
+    right, left = jnp.where(even, one, other), jnp.where(even, other, one)
+    edge = jnp.concatenate([right, left], axis=2)
+    edge = jnp.concatenate([edge, jnp.zeros((1,) + edge.shape[1:], jnp.float32)], axis=0)
     vmem = pl.BlockSpec(memory_space=pltpu.VMEM)
     smem = pl.BlockSpec(memory_space=pltpu.SMEM)
     f32, bf16 = jnp.float32, jnp.bfloat16
@@ -467,11 +519,24 @@
     tiles = lambda number: (number, 8, LANES)
     rows = lambda number: (number * 8, LANES)
     half = (FIELDS, ROWS, columns // 2)
-    *kept, image, second, sums = pl.pallas_call(
+    own_near, own_grown_near, own_grown = pl.pallas_call(
+        start_kernel,
+        out_shape=(
+            shape((chunks,) + tiles(wider), f32),
+            shape((chunks,) + tiles(count), f32),
+            shape((2,) + tiles(count), f32),
+        ),
+        in_specs=[vmem] * 3,
+        out_specs=(vmem,) * 3,
+        scratch_shapes=[pltpu.VMEM((2,) + tiles(wider), f32)],
+        compiler_params=params,
+        cost_estimate=pl.CostEstimate(flops=5 * 10**9, bytes_accessed=0, transcendentals=0),
+        name="start",
+    )(own, extra, matrices)
+    halo_grown, *kept, image, second, sums = pl.pallas_call(
         inner_kernel,
         out_shape=(
-            shape((chunks + 1,) + rows(count), bf16),
-            shape((chunks + 1,) + rows(count), bf16),
+            shape((2,) + tiles(count), f32),
             shape((2,) + tiles(wider), f32),
             shape((2,) + tiles(count), f32),
             shape((chunks,) + tiles(count), f32),
@@ -485,26 +550,24 @@
             shape(half, f32),
             shape(tiles(4), f32),
         ),
-        in_specs=[vmem] * 2 + [smem],
-        out_specs=(vmem,) * 14,
+        in_specs=[vmem] * 2 + [smem] + [vmem] * 2,
+        out_specs=(vmem,) * 13,
         scratch_shapes=[
-            pltpu.VMEM((chunks + 1,) + rows(wider), bf16),
-            pltpu.VMEM((chunks + 1,) + rows(wider), bf16),
+            pltpu.VMEM((2,) + tiles(wider), f32),
             pltpu.VMEM(tiles(count), f32),
-            pltpu.VMEM(tiles(wider), f32),
-            pltpu.VMEM(tiles(count), f32),
+            pltpu.VMEM((chunks,) + tiles(wider), f32),
+            pltpu.VMEM((chunks,) + tiles(count), f32),
         ],
         compiler_params=params,
         cost_estimate=pl.CostEstimate(flops=10**10, bytes_accessed=0, transcendentals=0),
         name="inner",
-    )(tall, matrices, stencil_weights)
+    )(tall, matrices, stencil_weights, own_near, own_grown_near)
     outer_image, outer_second, sums = pl.pallas_call(
         outer_kernel,
         out_shape=(shape(half, f32), shape(half, f32), shape((devices, LANES), f32)),
-        in_specs=[vmem] * 4 + [smem] + [vmem] * 12,
+        in_specs=[vmem] * 3 + [smem] + [vmem] * 12,
         out_specs=(vmem,) * 3,
         scratch_shapes=[
-            pltpu.VMEM(tiles(wider), f32),
             pltpu.VMEM(tiles(wider), f32),
             pltpu.VMEM(tiles(count), f32),
             pltpu.VMEM(tiles(wider), f32),
@@ -518,7 +581,7 @@
         ],
         compiler_params=params,
         name="outer",
-    )(right, left, tall, matrices, stencil_weights, *kept, sums)
+    )(edge, tall, matrices, stencil_weights, own_grown, halo_grown, *kept, sums)
     sums = lax.all_to_all(sums, ("down", "cross"), 0, 0, tiled=True)
     solution_field, residual = pl.pallas_call(
         finish_kernel,

time: 71 us -> 65.5 us (0.923)
  waiting for transfers between devices: 6.78 us -> 2.48 us
  starting transfers between devices: 9.4 us -> 7.75 us
  local copies, waits for them, and re-layouts: 0.22 us -> 1.31 us
    ppermute x2 -> x0, starting transfers between devices: 6.17 us -> none  [shift(): lax.ppermute(value, axis, [(i, i + by) for i in range(size) if 0 <= i + b...]
    ppermute x2 -> x4, starting transfers between devices: 3.22 us -> 7.75 us  [swap(): return lax.ppermute(value, axis, pairs + [(j, i) for i, j in pairs])]
    ppermute x2 -> x4, waiting for transfers between devices: 6.77 us -> 2.48 us  [swap(): return lax.ppermute(value, axis, pairs + [(j, i) for i, j in pairs])]
    unnamed x10 -> x12, local copies, waits for them, and re-layouts: 0.02 us -> 1.3 us
    pallas_call x1 -> x2, Pallas kernels: 14.5 us -> 14.1 us  [the longest x1 10.8 us: per_device(): pl.pallas_call(inner_kernel, out_shape=(shape((2,) + tiles(count), f32),...]
  transfers between devices with their start and end apart: 4 -> 4, of which waited for: 1 -> 2; matrix products, arithmetic and copies ran while one was open for 0% -> 0% of each run, Pallas kernels for 24% -> 26%
where the time goes in v5:
time: 65.5 us; the launch traced here: 65.2 us
  Pallas kernels  25.7 us (39%)
  blocking collectives  23.8 us (36%)
  starting transfers between devices  7.75 us (12%)
  other arithmetic  3.34 us (5%)
  waiting for transfers between devices  2.48 us (4%)
  local copies, waits for them, and re-layouts  1.31 us (2%)
  between operations  0.84 us (1%)
    all_to_all x1, blocking collectives, per_device(): sums = lax.all_to_all(sums, ('down', 'cross'), 0, 0, tiled=True)  23.8 us
    pallas_call x1, Pallas kernels, per_device(): pl.pallas_call(inner_kernel, out_shape=(shape((2,) + tiles(count), f32),...  10.8 us
    ppermute x4, starting transfers between devices, swap(): return lax.ppermute(value, axis, pairs + [(j, i) for i, j in pairs])  7.75 us
    pallas_call x1, Pallas kernels, per_device(): pl.pallas_call(outer_kernel, out_shape=(shape(half, f32), shape(half, f32...  7.06 us
    pallas_call x1, Pallas kernels, per_device(): pl.pallas_call(start_kernel, out_shape=(shape((chunks,) + tiles(wider), f...  3.33 us
    pallas_call x1, Pallas kernels, per_device(): pl.pallas_call(matrix_kernel, grid=(2,), out_shape=jax.ShapeDtypeStruct((...  2.64 us
    ppermute x4, waiting for transfers between devices, swap(): return lax.ppermute(value, axis, pairs + [(j, i) for i, j in pairs])  2.48 us
    pallas_call x1, Pallas kernels, per_device(): pl.pallas_call(finish_kernel, out_shape=(shape(own.shape, f32), shape(own...  1.92 us
  transfers between devices with their start and end apart: 4, of which 2 were waited for; matrix products, arithmetic and copies ran while one was open for 0% of the time, Pallas kernels for 26%

profile of v5, /device:TPU:1, one launch (start us, length us, event | category | flops | bytes accessed | tf_op | source)
XLA Modules:
  0.0 65.2 jit_solution(13378316216178663929)
XLA Ops:
  0.7 1.4 %pad_maximum_fusion.1 = f32[111,4,512]{2,1,0:T(4,128)S(1)} fusion(f32[1,4,512]{2,1,0:T(4,128)} %bitcast.14, f32[5,4,512]{2,1,0:T(4,128)} %param.7, f32[105,4,512]{2,1,0:T(4,128)} %bitcast.8), kind=kLoop, calls=%fused_computation.3 | loop fusion | flops 454656 | bytes 1818624 | tf_op jit(solution)/shard_map/concatenate | solution.py:489
  2.1 0.0 copy-start
  2.1 0.3 broadcast_select_fusion.3
  2.4 2.5 %collective-permute-start = (f32[111,2,512]{2,1,0:T(2,128)S(1)}, f32[111,2,512]{2,1,0:T(2,128)S(1)}, u32[]{:S(2)}, u32[]{:S(2)}) collective-permute-start(f32[111,2,512]{2,1,0:T(2,128)S(1)} %get-tuple-element.50), channel_id=1, source_target_pairs={{0,16},{32,48},{64,80},{96,112},{16,0},{48,32},{80,64},{112,96},{1... | collective-permute-start | bytes 1363976 | tf_op jit(solution)/shard_map/ppermute | solution.py:479
  5.0 0.7 %collective-permute-start.1 = (f32[111,2,512]{2,1,0:T(2,128)S(1)}, f32[111,2,512]{2,1,0:T(2,128)S(1)}, u32[]{:S(2)}, u32[]{:S(2)}) collective-permute-start(f32[111,2,512]{2,1,0:T(2,128)S(1)} %get-tuple-element.51), channel_id=1, source_target_pairs={{16,32},{48,64},{80,96},{32,16},{64,48},{96,80},{17,33},{49,65},{8... | collective-permute-start | bytes 1363976 | tf_op jit(solution)/shard_map/ppermute | solution.py:479
  5.7 2.6 %matrix.1.matrix_ref = bf16[2,768,384]{2,1,0:T(8,128)(2,1)} custom-call(f32[13]{0:T(128)} %weights_ref.5, s32[2,256,384]{2,1,0:T(8,128)} %constant.32.clone.slots_ref), custom_call_target="tpu_custom_call" | custom-call | tf_op jit(solution)/shard_map/matrix/pallas_call | solution.py:509
  8.4 1.3 %copy-done.1 = bf16[2,768,384]{2,1,0:T(8,128)(2,1)S(1)} copy-done((bf16[2,768,384]{2,1,0:T(8,128)(2,1)S(1)}, bf16[2,768,384]{2,1,0:T(8,128)(2,1)}, u32[]{:S(2)}) %copy-start.1) | copy-done | bytes 1179672
  9.6 3.3 %start.1 = (f32[4,112,8,128]{3,2,1,0:T(8,128)S(1)}, f32[4,106,8,128]{3,2,1,0:T(8,128)S(1)}, f32[2,106,8,128]{3,2,1,0:T(8,128)S(1)}) custom-call(f32[105,4,512]{2,1,0:T(4,128)S(1)} %bitcast.9, f32[6,4,512]{2,1,0:T(4,128)S(1)} %pad_maximum_fusion.2.extra_ref, bf16[2,768,384]{2,1,0:T(8,128)(2,1)S(1)} %copy-done.1), custom_call_target="tpu_custom_call" | custom-call | flops 5000000000 | tf_op jit(solution)/shard_map/start/pallas_call | solution.py:522
  13.0 2.1 %collective-permute-done = f32[111,2,512]{2,1,0:T(2,128)S(1)} collective-permute-done((f32[111,2,512]{2,1,0:T(2,128)S(1)}, f32[111,2,512]{2,1,0:T(2,128)S(1)}, u32[]{:S(2)}, u32[]{:S(2)}) %collective-permute-start) | collective-permute-done | bytes 454688 | tf_op jit(solution)/shard_map/ppermute | solution.py:479
  15.1 0.0 collective-permute-done.1
  15.1 0.3 broadcast_select_fusion.1
  15.4 0.4 select_maximum_fusion
  15.9 0.0 copy-start.3
  15.9 0.4 pad_maximum_fusion.tall_ref
  16.3 0.2 slice_select_fusion.1
  16.5 1.3 %collective-permute-start.2 = (f32[111,8,64]{2,1,0:T(8,128)S(1)}, f32[111,8,64]{2,1,0:T(8,128)S(1)}, u32[]{:S(2)}, u32[]{:S(2)}) collective-permute-start(f32[111,8,64]{2,1,0:T(8,128)S(1)} %get-tuple-element.44), channel_id=1, source_target_pairs={{0,1},{2,3},{4,5},{6,7},{8,9},{10,11},{12,13},{14,15},{1,0},{3,2},... | collective-permute-start | bytes 681992 | tf_op jit(solution)/shard_map/ppermute | solution.py:479
  17.8 3.2 %collective-permute-start.3 = (f32[111,8,64]{2,1,0:T(8,128)S(1)}, f32[111,8,64]{2,1,0:T(8,128)S(1)}, u32[]{:S(2)}, u32[]{:S(2)}) collective-permute-start(f32[111,8,64]{2,1,0:T(8,128)S(1)} %get-tuple-element.45), channel_id=1, source_target_pairs={{1,2},{3,4},{5,6},{7,8},{9,10},{11,12},{13,14},{2,1},{4,3},{6,5},{... | collective-permute-start | bytes 681992 | tf_op jit(solution)/shard_map/ppermute | solution.py:479
  21.0 10.8 %inner.1 = (f32[2,106,8,128]{3,2,1,0:T(8,128)S(1)}, f32[2,112,8,128]{3,2,1,0:T(8,128)S(1)}, f32[2,106,8,128]{3,2,1,0:T(8,128)S(1)}, f32[4,106,8,128]{3,2,1,0:T(8...) custom-call(f32[112,8,512]{2,1,0:T(8,128)S(1)} %pad_maximum_fusion.t, ...), custom_call_target="tpu_custom_call" | custom-call | flops 10000000000 | tf_op jit(solution)/shard_map/inner/pallas_call | solution.py:536
  31.8 0.4 collective-permute-done.3
  32.2 0.1 broadcast_select_fusion.5
  32.2 0.2 select_maximum_fusion.1.edge
  32.4 7.1 %outer.1 = (f32[105,4,256]{2,1,0:T(4,128)S(1)}, f32[105,4,256]{2,1,0:T(4,128)S(1)}, f32[128,128]{1,0:T(8,128)S(1)}) custom-call(f32[112,8,128]{2,1,0:T(8,128)S(1)} %select_maximum_fusion.1.edge, f32[112,8,512]{2,1,0:T(8,128)S(1)} %pad_maximum_fusion.tall_ref, bf16[2,768,384]{2,1,0:T(8,128)(2,1)S(1)} %copy-done.2, f32[13]{0:T(128)S(1)} %copy-done.3, ...), custom_call_target="tpu_custom_call" | custom-call | tf_op jit(solution)/shard_map/outer/pallas_call | solution.py:565
  39.5 23.8 %all_to_all.11 = f32[128,1,128]{2,1,0:T(1,128)S(1)} all-to-all(f32[128,1,128]{2,1,0:T(1,128)S(1)} %bitcast.13), channel_id=1, replica_groups=mesh['down'=8,'cross'=16] {'down','cross'}, dimensions={0} | all-to-all | bytes 131072 | tf_op jit(solution)/shard_map/all_to_all | solution.py:585
  63.3 1.9 %finish.1 = (f32[105,4,512]{2,1,0:T(4,128)}, f32[105,4,512]{2,1,0:T(4,128)}) custom-call(f32[128,128]{1,0:T(8,128)S(1)} %bitcast.12, f32[105,4,512]{2,1,0:T(4,128)S(1)} %bitcast.11, f32[105,4,256]{2,1,0:T(4,128)S(1)} %get-tuple-element.38.refs_0_, f32[105,4,256]{2,1,0:T(4,128)S(1)} %get-tuple-element.39.refs_1_, ...), custom_call_target="tpu_custom_call" | custom-call | tf_op jit(solution)/shard_map/finish/pallas_call | solution.py:586
  (13 shorter events, 0.0 us)
Async XLA Ops:
  0.6 5.0 %copy-start.4 = (f32[5,4,512]{2,1,0:T(4,128)S(1)}, f32[5,4,512]{2,1,0:T(4,128)}, u32[]{:S(2)}) copy-start(f32[5,4,512]{2,1,0:T(4,128)} %param.7) | copy-start | bytes 122884
  0.6 5.0 %copy-start.5 = (f32[4,512]{1,0:T(4,128)S(1)}, f32[4,512]{1,0:T(4,128)}, u32[]{:S(2)}) copy-start(f32[4,512]{1,0:T(4,128)} %param.6) | copy-start | bytes 24580
  2.1 6.3 %copy-start = (f32[3,35,4,512]{3,2,1,0:T(4,128)S(1)}, f32[3,35,4,512]{3,2,1,0:T(4,128)}, u32[]{:S(2)}) copy-start(f32[3,35,4,512]{3,2,1,0:T(4,128)} %param.5) | copy-start | bytes 2580484
  2.4 12.7 %collective-permute-start = (f32[111,2,512]{2,1,0:T(2,128)S(1)}, f32[111,2,512]{2,1,0:T(2,128)S(1)}, u32[]{:S(2)}, u32[]{:S(2)}) collective-permute-start(f32[111,2,512]{2,1,0:T(2,128)S(1)} %get-tuple-element.50), channel_id=1, source_target_pairs={{0,16},{32,48},{64,80},{96,112},{16,0},{48,32},{80,64},{112,96},{1... | collective-permute-start | bytes 1363976 | tf_op jit(solution)/shard_map/ppermute | solution.py:479
  5.0 10.1 %collective-permute-start.1 = (f32[111,2,512]{2,1,0:T(2,128)S(1)}, f32[111,2,512]{2,1,0:T(2,128)S(1)}, u32[]{:S(2)}, u32[]{:S(2)}) collective-permute-start(f32[111,2,512]{2,1,0:T(2,128)S(1)} %get-tuple-element.51), channel_id=1, source_target_pairs={{16,32},{48,64},{80,96},{32,16},{64,48},{96,80},{17,33},{49,65},{8... | collective-permute-start | bytes 1363976 | tf_op jit(solution)/shard_map/ppermute | solution.py:479
  8.4 1.3 %copy-start.1 = (bf16[2,768,384]{2,1,0:T(8,128)(2,1)S(1)}, bf16[2,768,384]{2,1,0:T(8,128)(2,1)}, u32[]{:S(2)}) copy-start(bf16[2,768,384]{2,1,0:T(8,128)(2,1)} %matrix.1.matrix_ref) | copy-start | bytes 3538948
  15.8 5.2 %copy-start.2 = (bf16[2,768,384]{2,1,0:T(8,128)(2,1)S(1)}, bf16[2,768,384]{2,1,0:T(8,128)(2,1)}, u32[]{:S(2)}) copy-start(bf16[2,768,384]{2,1,0:T(8,128)(2,1)} %matrix.1.matrix_ref) | copy-start | bytes 3538948
  15.9 5.2 %copy-start.3 = (f32[13]{0:T(128)S(1)}, f32[13]{0:T(128)}, u32[]{:S(2)}) copy-start(f32[13]{0:T(128)} %weights_ref.5) | copy-start | bytes 160
  16.5 15.3 %collective-permute-start.2 = (f32[111,8,64]{2,1,0:T(8,128)S(1)}, f32[111,8,64]{2,1,0:T(8,128)S(1)}, u32[]{:S(2)}, u32[]{:S(2)}) collective-permute-start(f32[111,8,64]{2,1,0:T(8,128)S(1)} %get-tuple-element.44), channel_id=1, source_target_pairs={{0,1},{2,3},{4,5},{6,7},{8,9},{10,11},{12,13},{14,15},{1,0},{3,2},... | collective-permute-start | bytes 681992 | tf_op jit(solution)/shard_map/ppermute | solution.py:479
  17.8 14.4 %collective-permute-start.3 = (f32[111,8,64]{2,1,0:T(8,128)S(1)}, f32[111,8,64]{2,1,0:T(8,128)S(1)}, u32[]{:S(2)}, u32[]{:S(2)}) collective-permute-start(f32[111,8,64]{2,1,0:T(8,128)S(1)} %get-tuple-element.45), channel_id=1, source_target_pairs={{1,2},{3,4},{5,6},{7,8},{9,10},{11,12},{13,14},{2,1},{4,3},{6,5},{... | collective-permute-start | bytes 681992 | tf_op jit(solution)/shard_map/ppermute | solution.py:479

commit v6 on v4

v6 whole, which is shorter than its diff:
```python
import functools
import math

import jax
import jax.numpy as jnp
import numpy as np
from jax import lax
from jax.experimental import pallas as pl
from jax.experimental.pallas import tpu as pltpu
from jax.sharding import PartitionSpec as P

CZ = 32
VARS = 4
DEG = 3
TERMS = 5
COMPS = 3
MODES = 35
FIELDS = COMPS * MODES
STIFF = FIELDS + TERMS
ROWS = 4
LANES = 128
WIDE = 64


def multi_indices(count_left, budget_left):
    if count_left == 0:
        return [()]
    return [
        (leading,) + remainder
        for leading in range(budget_left + 1)
        for remainder in multi_indices(count_left - 1, budget_left - leading)
    ]


def chaos_terms():
    picked = sorted(
        multi_indices(VARS, DEG),
        key=lambda multi_index: (sum(multi_index),)
        + tuple((-entry_value for entry_value in multi_index)),
    )
    position = {multi_index: number for number, multi_index in enumerate(picked)}
    terms = [[] for mode in picked]
    for variable in range(VARS):
        for multi_index in picked:
            raised = list(multi_index)
            raised[variable] += 1
            raised = tuple(raised)
            if raised in position:
                degree = multi_index[variable]
                here, there = position[multi_index], position[raised]
                terms[here].append((variable, degree, there))
                terms[there].append((variable, degree, here))
    values = [(n + 1) / math.sqrt((2 * n + 1) * (2 * n + 3)) for n in range(DEG)]
    return terms, values


CHAOS, CHAOS_VALUES = chaos_terms()
TABLE = 1 + VARS * DEG


def tap_slots(y_in, y_out, reach):
    z = np.arange(CZ)
    y_in, z_in = np.repeat(y_in, CZ), np.tile(z, len(y_in))
    y_out, z_out = np.repeat(y_out, CZ), np.tile(z, len(y_out))
    dy = y_in[:, None] - y_out[None, :]
    dz = z_in[:, None] - z_out[None, :]
    near = (abs(dy) <= 1) & (abs(dz) <= 1) & np.repeat(np.repeat(reach, CZ, 0), CZ, 1)
    parts = []
    for dx in (0, 1, -1):
        linear = 9 * (dx + 1) + 3 * (dy + 1) + (dz + 1)
        slot = np.minimum(linear, 26 - linear)
        parts.append(np.where(near & (linear != 13), slot, 13))
    return np.concatenate(parts, axis=1).astype(np.int32)


def chunk_slots():
    y_in = np.array([0, 1, 2, 3, 4, 5, -2, -1])
    return tap_slots(y_in, np.arange(4), np.ones((8, 4), bool))


def rim_slots():
    far = 100
    y_in = np.array([16, 17, -2 - far, -1 - far, -far, 1 - far, 14, 15])
    y_out = np.array([15, 16, -1 - far, -far])
    reach = np.ones((8, 4), bool)
    reach[4:, 0] = False
    reach[4:, 3] = False
    return tap_slots(y_in, y_out, reach)


SLOTS = np.stack([chunk_slots(), rim_slots()])


def matrix_kernel(weights_ref, slots_ref, matrix_ref):
    slots = slots_ref[0]
    full = jnp.zeros(slots.shape, jnp.float32)
    for number in range(13):
        full = jnp.where(slots == number, 0.5 * weights_ref[number], full)
    high = full.astype(jnp.bfloat16)
    low = (full - high.astype(jnp.float32)).astype(jnp.bfloat16)
    rows = slots.shape[0]
    matrix_ref[0, :rows] = high
    matrix_ref[0, rows : 2 * rows] = high
    matrix_ref[0, 2 * rows :] = low


def mix(table, load, mode, total):
    for variable, degree, other in CHAOS[mode]:
        total = total + table[1 + variable * DEG + degree] * load(other)
    return total


PAIRS = ((0, 3), (1, 2))
OUTER, INNER = 0, 1


def tile_row():
    return lax.broadcasted_iota(jnp.int32, (8, LANES), 0)


def tile_lane():
    return lax.broadcasted_iota(jnp.int32, (8, LANES), 1)


def beside_outer(inner, lead, ahead=0.0, behind=0.0):
    left = tile_lane() < WIDE
    return jnp.where(left, jnp.where(lead, inner, ahead), jnp.where(lead, behind, inner))


def beside_inner(outer, inner, lead):
    left = tile_lane() < WIDE
    turned = pltpu.roll(inner, ROWS, 1)
    return jnp.where(left, jnp.where(lead, turned, outer), jnp.where(lead, outer, turned))


def halves(value):
    value = value.reshape(value.shape[0] * 8, LANES)
    high = value.astype(jnp.bfloat16)
    return high, (value - high.astype(jnp.float32)).astype(jnp.bfloat16)


def stencil(own, beside, matrix):
    (high, low), (near_high, near_low) = halves(own), halves(beside)
    lines = jnp.concatenate([high, near_high, low, near_low, high, near_high], axis=1)
    parts = jnp.dot(lines, matrix, preferred_element_type=jnp.float32)
    return [
        parts[:, at : at + LANES].reshape(own.shape) for at in range(0, parts.shape[1], LANES)
    ]


def turned_parts(parts):
    return pltpu.roll(parts[-2], 7, 1), pltpu.roll(parts[-1], 1, 1)


def same_rows(parts):
    ahead, behind = turned_parts(parts)
    row = tile_row() % ROWS
    return parts[0] + jnp.where(row == ROWS - 1, 0.0, ahead) + jnp.where(row == 0, 0.0, behind)


def other_rows(parts):
    ahead, behind = turned_parts(parts)
    row = tile_row() % ROWS
    return jnp.where(row == ROWS - 1, ahead, jnp.where(row == 0, behind, 0.0))


def entry_of(ref):
    return lambda number: ref[number]


def coef_values(field):
    values = [field(FIELDS + term) for term in range(TERMS)]
    return spread_values(values)


def spread_values(values):
    return [values[0]] + [
        values[1 + variable] * CHAOS_VALUES[degree]
        for variable in range(VARS)
        for degree in range(DEG)
    ]


def diag_values(field, near, weights_ref):
    weight_sum = sum(weights_ref[number] for number in range(13))
    return spread_values(
        [field(FIELDS + term) * weight_sum + near(FIELDS + term) for term in range(TERMS)]
    )


def grow(field, table, out):
    @pl.loop(0, COMPS)
    def each(comp):
        base = comp * MODES
        for mode in range(MODES):
            load = lambda other: field(base + other)
            out[base + mode] = mix(table, load, mode, table[0] * load(mode))

    out[FIELDS] = jnp.zeros((8, LANES), jnp.float32)


def apply(field, near, grown_near, coef, diag, stiff, store, carry=0):
    def each(comp, carry):
        base = comp * MODES
        for mode in range(MODES):
            load = lambda other: field(base + other)
            close = lambda other: near(base + other)
            value = mix(diag, load, mode, (stiff + diag[0]) * load(mode))
            value = value - mix(
                coef, close, mode, coef[0] * close(mode) + grown_near(base + mode)
            )
            carry = store(base + mode, value, carry)
        return carry

    return lax.fori_loop(0, COMPS, each, carry)


def masked_store(out, inside):
    def store(number, value, carry):
        out[number] = jnp.where(inside, value, 0.0)
        return carry

    return store


def second_store(start, image, out):
    def store(number, value, sums):
        rr, rq, qq, qz = sums
        first, here = start(number), image(number)
        out[number] = value
        return rr + first * first, rq + first * here, qq + here * here, qz + here * value

    return store


def second_near(own, own_beside, halo, halo_beside, matrix_ref):
    own_parts = stencil(own, own_beside, matrix_ref[0])
    halo_parts = stencil(halo, halo_beside, matrix_ref[0, :, LANES:])
    return same_rows(own_parts) + other_rows(halo_parts)


def start_kernel(
    own_ref, extra_ref, matrix_ref, pairs, grown, near, halo_near, grown_near, halo_grown_near
):
    for number, chunks in enumerate(PAIRS):
        for side, chunk in enumerate(chunks):
            lanes, rows = pl.ds(chunk * LANES, LANES), pl.ds(side * ROWS, ROWS)
            pairs[number, :FIELDS, rows, :] = own_ref[:, :, lanes]
            pairs[number, FIELDS : STIFF + 1, rows, :] = extra_ref[:, :, lanes]
        pairs[number, STIFF + 1] = jnp.zeros((8, LANES), jnp.float32)
        field = entry_of(pairs.at[number])
        grow(field, coef_values(field), grown.at[number])
    lead = tile_row() < ROWS
    for ref, out, halo_out in ((pairs, near, halo_near), (grown, grown_near, halo_grown_near)):
        outer, inner = ref[OUTER], ref[INNER]
        for number, own, beside in (
            (OUTER, outer, beside_outer(inner, lead)),
            (INNER, inner, beside_inner(outer, inner, lead)),
        ):
            parts = stencil(own, beside, matrix_ref[0])
            out[number] = same_rows(parts)
            halo_out[number] = other_rows(parts)


def inner_kernel(
    beyond_ref, pairs, matrix_ref, weights_ref,
    before_near, before_halo_near, before_grown_near, before_halo_grown_near,
    halo, halo_grown, near, halo_near, grown_near, halo_grown_near,
    image, halo_image, image_grown, halo_image_grown, diag, second_ref, sums_ref,
):
    for number, (first, second) in enumerate(PAIRS):
        halo[number, :, ROWS:, :] = beyond_ref[:, :, pl.ds(first * LANES, LANES)]
        halo[number, :, :ROWS, :] = beyond_ref[:, :, pl.ds(second * LANES, LANES)]
        field = entry_of(halo.at[number])
        grow(field, coef_values(field), halo_grown.at[number])
    lead = tile_row() >= ROWS
    for ref, before, before_halo, out, halo_out in (
        (halo, before_near, before_halo_near, near, halo_near),
        (halo_grown, before_grown_near, before_halo_grown_near, grown_near, halo_grown_near),
    ):
        outer, inner = ref[OUTER], ref[INNER]
        for number, own, beside in (
            (OUTER, outer, beside_outer(inner, lead)),
            (INNER, inner, beside_inner(outer, inner, lead)),
        ):
            parts = stencil(own, beside, matrix_ref[0])
            halo_out[number] = before_halo[number] + same_rows(parts)
            out[number] = before[number] + other_rows(parts)

    for ref, close, grown_close, out, out_grown in (
        (pairs, near, grown_near, image, image_grown),
        (halo, halo_near, halo_grown_near, halo_image, halo_image_grown),
    ):

        @pl.loop(0, len(PAIRS))
        def each(number):
            field, around = entry_of(ref.at[number]), entry_of(close.at[number])
            coef = coef_values(field)
            values = diag_values(field, around, weights_ref)
            if ref is pairs:
                for entry, value in enumerate(values):
                    diag[number, entry] = value
            stiff = field(STIFF)
            target = out.at[number]
            apply(
                field, around, entry_of(grown_close.at[number]), coef, values, stiff,
                masked_store(target, stiff > 0.0),
            )
            target[FIELDS] = jnp.zeros((8, LANES), jnp.float32)
            grow(entry_of(target), coef, out_grown.at[number])

    own_lead = tile_row() < ROWS
    image_near, image_grown_near = near.at[INNER, pl.ds(0, FIELDS + 1)], grown_near.at[INNER]
    for own, far, out in (
        (image, halo_image, image_near),
        (image_grown, halo_image_grown, image_grown_near),
    ):
        out[...] = second_near(
            own[INNER],
            beside_inner(own[OUTER], own[INNER], own_lead),
            far[INNER],
            beside_inner(far[OUTER], far[INNER], lead),
            matrix_ref,
        )
    field, here = entry_of(pairs.at[INNER]), entry_of(image.at[INNER])
    zero = jnp.zeros((8, LANES), jnp.float32)
    sums = apply(
        here, entry_of(image_near), entry_of(image_grown_near), coef_values(field),
        [diag[INNER, entry] for entry in range(TABLE)], field(STIFF),
        second_store(field, here, second_ref), (zero, zero, zero, zero),
    )
    for number, value in enumerate(sums):
        sums_ref[number] = value


def outer_kernel(
    edge, pairs, halo, matrix_ref, weights_ref, own_grown, halo_grown,
    near, halo_near, grown_near, halo_grown_near,
    image, halo_image, image_grown, halo_image_grown, diag, before_ref,
    image_ref, second_ref, sums_ref,
    rim, grown, rim_near, rim_grown_near, rim_image,
):
    lane, top = tile_lane(), tile_row() < ROWS
    bottom = ~top
    left = lane < WIDE

    def first_chunk(own, far):
        return jnp.where(top, own, far)

    def last_chunk(own, far):
        return pltpu.roll(jnp.where(top, far, own), ROWS, own.ndim - 2)

    def to_rim(last, beyond, begin):
        right = pltpu.roll(jnp.where(lane >= 3 * CZ, last, beyond), CZ, 2)
        return jnp.where(
            left, right, pltpu.roll(jnp.where(lane < CZ, begin, beyond), LANES - CZ, 2)
        )

    def rim_stencil(around, own, far, own_near, far_near):
        beside = jnp.where(left, first_chunk(own, far), last_chunk(own, far))
        parts = stencil(around, beside, matrix_ref[1])
        ahead, behind = turned_parts(parts)
        begin = first_chunk(own_near, far_near)
        last = last_chunk(own_near, far_near)
        return parts[0] + ahead + behind + to_rim(last, jnp.zeros_like(last), begin)

    field = entry_of(edge)
    grow(field, coef_values(field), grown)
    rim_near[...] = rim_stencil(
        edge[...], pairs[OUTER], halo[OUTER], near[OUTER], halo_near[OUTER]
    )
    rim_grown_near[...] = rim_stencil(
        grown[...], own_grown[OUTER], halo_grown[OUTER], grown_near[OUTER], halo_grown_near[OUTER]
    )
    rim[...] = to_rim(
        last_chunk(pairs[OUTER], halo[OUTER]), edge[...], first_chunk(pairs[OUTER], halo[OUTER])
    )
    field, around = entry_of(rim), entry_of(rim_near)
    coef, rim_diag = coef_values(field), diag_values(field, around, weights_ref)
    stiff = field(STIFF)
    apply(
        field, around, entry_of(rim_grown_near), coef, rim_diag, stiff,
        masked_store(rim_image, stiff > 0.0),
    )
    rim_image[FIELDS] = jnp.zeros((8, LANES), jnp.float32)
    grow(entry_of(rim_image), coef, grown)

    def from_rim(value):
        last = pltpu.roll(value, LANES - CZ, value.ndim - 1)
        return pltpu.roll(value, CZ, value.ndim - 1), pltpu.roll(last, ROWS, value.ndim - 2)

    def placed(lead, begin, last, value):
        value = jnp.where(lead & (lane < CZ), begin, value)
        return jnp.where(~lead & (lane >= 3 * CZ), last, value)

    image_near, image_grown_near = rim_near.at[pl.ds(0, FIELDS + 1)], rim_grown_near
    for value, own, far, out, keep in (
        (rim_image, image, halo_image, image_near, True),
        (grown, image_grown, halo_image_grown, image_grown_near, False),
    ):
        begin, last = from_rim(value[...])
        here = placed(top, begin, last, own[OUTER])
        if keep:
            image_ref[...] = here
        out[...] = second_near(
            here,
            beside_outer(own[INNER], top, last, begin),
            placed(bottom, begin, last, far[OUTER]),
            beside_outer(far[INNER], bottom, last, begin),
            matrix_ref,
        )
    values = []
    for entry in range(TABLE):
        begin, last = from_rim(rim_diag[entry])
        values.append(placed(top, begin, last, diag[OUTER, entry]))
    field, here = entry_of(pairs.at[OUTER]), entry_of(image_ref)
    sums = apply(
        here, entry_of(image_near), entry_of(image_grown_near), coef_values(field), values,
        field(STIFF), second_store(field, here, second_ref),
        tuple(before_ref[number] for number in range(4)),
    )
    column = lax.broadcasted_iota(jnp.int32, sums_ref.shape, 1)
    row = jnp.zeros(sums_ref.shape, jnp.float32)
    for number, value in enumerate(sums):
        row = jnp.where(column == number, jnp.sum(value), row)
    sums_ref[...] = row


FINISH_STEPS = 5


def finish_kernel(
    sums_ref, pairs, images, inner_second, outer_image, outer_second, field_ref, residual_ref
):
    total = jnp.sum(sums_ref[...], axis=0, keepdims=True)
    lane = lax.broadcasted_iota(jnp.int32, total.shape, 1)
    rr, rq, qq, qz = [
        jnp.sum(jnp.where(lane == number, total, 0.0), axis=1, keepdims=True)[None]
        for number in range(4)
    ]
    step = rr / rq
    fresh = rr - 2.0 * step * rq + step * step * qq
    larger = 1.0 + fresh / rr
    curvature = larger * larger * rq - 2.0 * larger * step * qq + step * step * qz
    later = fresh / curvature
    both = step + later * larger
    cross = later * step
    here = pl.ds(pl.program_id(0) * field_ref.shape[0], field_ref.shape[0])
    for number, image_ref, second_ref in (
        (OUTER, outer_image, outer_second),
        (INNER, images.at[INNER], inner_second),
    ):
        start, image, second = pairs[number, here], image_ref[here], second_ref[here]
        field = both * start - cross * image
        residual = start - both * image + cross * second
        for side, chunk in enumerate(PAIRS[number]):
            lanes, rows = pl.ds(chunk * LANES, LANES), slice(side * ROWS, (side + 1) * ROWS)
            field_ref[:, :, lanes] = field[:, rows]
            residual_ref[:, :, lanes] = residual[:, rows]


def swap(value, axis, begin):
    size = lax.axis_size(axis)
    pairs = [(i, i + 1) for i in range(begin, size - 1, 2)]
    return lax.ppermute(value, axis, pairs + [(j, i) for i, j in pairs])


def per_device(right_side, stiffness, coefficients, stencil_weights):
    columns = right_side.shape[3]
    devices = lax.axis_size("down") * lax.axis_size("cross")
    own = right_side.reshape(FIELDS, ROWS, columns)
    extra = jnp.concatenate([coefficients, stiffness[None]], axis=0)
    all_fields = jnp.concatenate([own, extra], axis=0)
    even = lax.axis_index("down") % 2 == 0
    head, tail = all_fields[:, :2], all_fields[:, ROWS - 2 :]
    one = swap(jnp.where(even, tail, head), "down", 0)
    other = swap(jnp.where(even, head, tail), "down", 1)
    upper, lower = jnp.where(even, one, other), jnp.where(even, other, one)
    beyond = jnp.concatenate([upper, lower], axis=1)
    even = lax.axis_index("cross") % 2 == 0
    tall = jnp.concatenate([all_fields, beyond], axis=1)
    head, tail = tall[:, :, :WIDE], tall[:, :, columns - WIDE :]
    one = swap(jnp.where(even, tail, head), "cross", 0)
    other = swap(jnp.where(even, head, tail), "cross", 1)
    right, left = jnp.where(even, one, other), jnp.where(even, other, one)
    edge = jnp.concatenate([right, left], axis=2)
    edge = jnp.concatenate([edge, jnp.zeros((1,) + edge.shape[1:], jnp.float32)], axis=0)
    beyond = jnp.concatenate([beyond, jnp.zeros((1, ROWS, columns), jnp.float32)], axis=0)
    vmem = pl.BlockSpec(memory_space=pltpu.VMEM)
    smem = pl.BlockSpec(memory_space=pltpu.SMEM)
    f32, bf16 = jnp.float32, jnp.bfloat16
    params = pltpu.CompilerParams(vmem_limit_bytes=32 * 1024 * 1024)
    matrices = pl.pallas_call(
        matrix_kernel,
        grid=(2,),
        out_shape=jax.ShapeDtypeStruct((2, 3 * SLOTS.shape[1], SLOTS.shape[2]), bf16),
        in_specs=[smem, pl.BlockSpec((1,) + SLOTS.shape[1:], lambda i: (i, 0, 0))],
        out_specs=pl.BlockSpec((1, 3 * SLOTS.shape[1], SLOTS.shape[2]), lambda i: (i, 0, 0)),
        name="matrix",
    )(stencil_weights, jnp.asarray(SLOTS))
    count, wider = FIELDS + 1, STIFF + 2
    one_of = lambda number: jax.ShapeDtypeStruct((number, 8, LANES), f32)
    pair_of = lambda number: jax.ShapeDtypeStruct((2, number, 8, LANES), f32)
    pairs, own_grown, *nears = pl.pallas_call(
        start_kernel,
        out_shape=(
            pair_of(wider), pair_of(count),
            pair_of(wider), pair_of(wider), pair_of(count), pair_of(count),
        ),
        in_specs=[vmem] * 3,
        out_specs=(vmem,) * 6,
        compiler_params=params,
        cost_estimate=pl.CostEstimate(flops=5 * 10**9, bytes_accessed=0, transcendentals=0),
        name="start",
    )(own, extra, matrices)
    halo, halo_grown, *kept, inner_second, sums = pl.pallas_call(
        inner_kernel,
        out_shape=(
            pair_of(wider), pair_of(count),
            pair_of(wider), pair_of(wider), pair_of(count), pair_of(count),
            pair_of(count), pair_of(count), pair_of(count), pair_of(count),
            pair_of(TABLE), one_of(FIELDS), one_of(4),
        ),
        in_specs=[vmem] * 3 + [smem] + [vmem] * 4,
        out_specs=(vmem,) * 13,
        compiler_params=params,
        cost_estimate=pl.CostEstimate(flops=10**10, bytes_accessed=0, transcendentals=0),
        name="inner",
    )(beyond, pairs, matrices, stencil_weights, *nears)
    images = kept[4]
    outer_image, outer_second, sums = pl.pallas_call(
        outer_kernel,
        out_shape=(one_of(count), one_of(FIELDS), jax.ShapeDtypeStruct((devices, LANES), f32)),
        in_specs=[vmem] * 4 + [smem] + [vmem] * 12,
        out_specs=(vmem,) * 3,
        scratch_shapes=[
            pltpu.VMEM((number, 8, LANES), f32) for number in (wider, count, wider, count, count)
        ],
        compiler_params=params,
        name="outer",
    )(edge, pairs, halo, matrices, stencil_weights, own_grown, halo_grown, *kept, sums)
    sums = lax.all_to_all(sums, ("down", "cross"), 0, 0, tiled=True)
    block = pl.BlockSpec((FIELDS // FINISH_STEPS, ROWS, columns), lambda i: (i, 0, 0))
    solution_field, residual = pl.pallas_call(
        finish_kernel,
        grid=(FINISH_STEPS,),
        out_shape=(jax.ShapeDtypeStruct(own.shape, f32), jax.ShapeDtypeStruct(own.shape, f32)),
        in_specs=[vmem] * 6,
        out_specs=(block, block),
        compiler_params=params,
        name="finish",
    )(sums, pairs, images, inner_second, outer_image, outer_second)
    return solution_field.reshape(right_side.shape), residual.reshape(right_side.shape)


def solution(mesh):
    return jax.shard_map(
        per_device,
        mesh=mesh,
        in_specs=(
            P(None, None, "down", "cross"),
            P("down", "cross"),
            P(None, "down", "cross"),
            P(),
        ),
        out_specs=(P(None, None, "down", "cross"), P(None, None, "down", "cross")),
        check_vma=False,
    )
```

time: 71 us -> 64.3 us (0.906)
  waiting for transfers between devices: 6.78 us -> 3.05 us
  Pallas kernels: 26.3 us -> 23.5 us
  starting transfers between devices: 9.4 us -> 7.88 us
  local copies, waits for them, and re-layouts: 0.22 us -> 1.3 us
    ppermute x2 -> x0, starting transfers between devices: 6.17 us -> none  [shift(): lax.ppermute(value, axis, [(i, i + by) for i in range(size) if 0 <= i + b...]
    ppermute x2 -> x4, starting transfers between devices: 3.22 us -> 7.88 us  [swap(): return lax.ppermute(value, axis, pairs + [(j, i) for i, j in pairs])]
    ppermute x2 -> x4, waiting for transfers between devices: 6.77 us -> 3.05 us  [swap(): return lax.ppermute(value, axis, pairs + [(j, i) for i, j in pairs])]
    pallas_call x3 -> x4, Pallas kernels: 23.7 us -> 20.9 us  [the longest x1 8.87 us: per_device(): pl.pallas_call(inner_kernel, out_shape=(pair_of(wider), pair_of(count), p...]
    unnamed x10 -> x12, local copies, waits for them, and re-layouts: 0.02 us -> 1.3 us
    concatenate x2 -> x3, other arithmetic: 1.83 us -> 1.61 us  [the longest x1 1.4 us: per_device(): all_fields = jnp.concatenate([own, extra], axis=0)]
  transfers between devices with their start and end apart: 4 -> 4, of which waited for: 1 -> 2; matrix products, arithmetic and copies ran while one was open for 0% -> 0% of each run, Pallas kernels for 24% -> 23%
where the time goes in v6:
time: 64.3 us; the launch traced here: 64 us
  blocking collectives  24.2 us (38%)
  Pallas kernels  23.5 us (37%)
  starting transfers between devices  7.88 us (12%)
  other arithmetic  3.28 us (5%)
  waiting for transfers between devices  3.05 us (5%)
  local copies, waits for them, and re-layouts  1.3 us (2%)
  between operations  0.82 us (1%)
    all_to_all x1, blocking collectives, per_device(): sums = lax.all_to_all(sums, ('down', 'cross'), 0, 0, tiled=True)  24.2 us
    pallas_call x1, Pallas kernels, per_device(): pl.pallas_call(inner_kernel, out_shape=(pair_of(wider), pair_of(count), p...  8.87 us
    ppermute x4, starting transfers between devices, swap(): return lax.ppermute(value, axis, pairs + [(j, i) for i, j in pairs])  7.88 us
    pallas_call x1, Pallas kernels, per_device(): pl.pallas_call(outer_kernel, out_shape=(one_of(count), one_of(FIELDS), ja...  5.91 us
    pallas_call x1, Pallas kernels, per_device(): pl.pallas_call(start_kernel, out_shape=(pair_of(wider), pair_of(count), p...  3.27 us
    ppermute x4, waiting for transfers between devices, swap(): return lax.ppermute(value, axis, pairs + [(j, i) for i, j in pairs])  3.05 us
    pallas_call x1, Pallas kernels, per_device(): pl.pallas_call(finish_kernel, grid=(FINISH_STEPS,), out_shape=(jax.ShapeD...  2.8 us
    pallas_call x1, Pallas kernels, per_device(): pl.pallas_call(matrix_kernel, grid=(2,), out_shape=jax.ShapeDtypeStruct((...  2.64 us
  transfers between devices with their start and end apart: 4, of which 2 were waited for; matrix products, arithmetic and copies ran while one was open for 0% of the time, Pallas kernels for 23%

profile of v6, /device:TPU:1, one launch (start us, length us, event | category | flops | bytes accessed | tf_op | source)
XLA Modules:
  0.0 64.0 jit_solution(4915841768532915856)
XLA Ops:
  0.6 1.4 %pad_maximum_fusion = f32[111,4,512]{2,1,0:T(4,128)S(1)} fusion(f32[1,4,512]{2,1,0:T(4,128)} %bitcast.13, f32[5,4,512]{2,1,0:T(4,128)} %param.7, f32[105,4,512]{2,1,0:T(4,128)} %bitcast.8), kind=kLoop, calls=%fused_computation.2 | loop fusion | flops 454656 | bytes 1818624 | tf_op jit(solution)/shard_map/concatenate | solution.py:473
  2.1 0.0 copy-start.5
  2.1 0.3 broadcast_select_fusion.3
  2.4 0.0 copy-start.2
  2.4 2.5 %collective-permute-start = (f32[111,2,512]{2,1,0:T(2,128)S(1)}, f32[111,2,512]{2,1,0:T(2,128)S(1)}, u32[]{:S(2)}, u32[]{:S(2)}) collective-permute-start(f32[111,2,512]{2,1,0:T(2,128)S(1)} %get-tuple-element.57), channel_id=1, source_target_pairs={{0,16},{32,48},{64,80},{96,112},{16,0},{48,32},{80,64},{112,96},{1... | collective-permute-start | bytes 1363976 | tf_op jit(solution)/shard_map/ppermute | solution.py:465
  5.0 0.7 %collective-permute-start.1 = (f32[111,2,512]{2,1,0:T(2,128)S(1)}, f32[111,2,512]{2,1,0:T(2,128)S(1)}, u32[]{:S(2)}, u32[]{:S(2)}) collective-permute-start(f32[111,2,512]{2,1,0:T(2,128)S(1)} %get-tuple-element.58), channel_id=1, source_target_pairs={{16,32},{48,64},{80,96},{32,16},{64,48},{96,80},{17,33},{49,65},{8... | collective-permute-start | bytes 1363976 | tf_op jit(solution)/shard_map/ppermute | solution.py:465
  5.7 2.6 %matrix.1.matrix_ref = bf16[2,768,384]{2,1,0:T(8,128)(2,1)} custom-call(f32[13]{0:T(128)} %weights_ref.5, s32[2,256,384]{2,1,0:T(8,128)} %constant.32.clone.slots_ref), custom_call_target="tpu_custom_call" | custom-call | tf_op jit(solution)/shard_map/matrix/pallas_call | solution.py:493
  8.4 1.3 %copy-done = bf16[2,768,384]{2,1,0:T(8,128)(2,1)S(1)} copy-done((bf16[2,768,384]{2,1,0:T(8,128)(2,1)S(1)}, bf16[2,768,384]{2,1,0:T(8,128)(2,1)}, u32[]{:S(2)}) %copy-start) | copy-done | bytes 1179672
  9.6 3.3 %start.1 = (f32[2,112,8,128]{3,2,1,0:T(8,128)S(1)}, f32[2,106,8,128]{3,2,1,0:T(8,128)S(1)}, f32[2,112,8,128]{3,2,1,0:T(8,128)S(1)}, f32[2,112,8,128]{3,2,1,0:T(8...) custom-call(f32[105,4,512]{2,1,0:T(4,128)S(1)} %bitcast.9, ...), custom_call_target="tpu_custom_call" | custom-call | flops 5000000000 | tf_op jit(solution)/shard_map/start/pallas_call | solution.py:504
  12.9 2.2 %collective-permute-done = f32[111,2,512]{2,1,0:T(2,128)S(1)} collective-permute-done((f32[111,2,512]{2,1,0:T(2,128)S(1)}, f32[111,2,512]{2,1,0:T(2,128)S(1)}, u32[]{:S(2)}, u32[]{:S(2)}) %collective-permute-start) | collective-permute-done | bytes 454688 | tf_op jit(solution)/shard_map/ppermute | solution.py:465
  15.1 0.3 broadcast_select_fusion.1
  15.4 0.4 select_maximum_fusion.beyond_ref
  15.8 0.4 broadcast_select_fusion.7
  16.3 0.0 copy-start.3
  16.3 0.1 broadcast_select_fusion.6
  16.4 4.4 %collective-permute-start.3 = (f32[111,8,64]{2,1,0:T(8,128)S(1)}, f32[111,8,64]{2,1,0:T(8,128)S(1)}, u32[]{:S(2)}, u32[]{:S(2)}) collective-permute-start(f32[111,8,64]{2,1,0:T(8,128)S(1)} %broadcast_select_fusion.6), channel_id=1, source_target_pairs={{1,2},{3,4},{5,6},{7,8},{9,10},{11,12},{13,14},{2,1},{4,3},{6,5},{... | collective-permute-start | bytes 681992 | tf_op jit(solution)/shard_map/ppermute | solution.py:465
  20.8 0.3 collective-permute-start.2
  21.1 8.9 %inner.1 = (f32[2,112,8,128]{3,2,1,0:T(8,128)S(1)}, f32[2,106,8,128]{3,2,1,0:T(8,128)S(1)}, f32[2,112,8,128]{3,2,1,0:T(8,128)S(1)}, f32[2,112,8,128]{3,2,1,0:T(8...) custom-call(f32[112,4,512]{2,1,0:T(4,128)S(1)} %select_maximum_fusio, ...), custom_call_target="tpu_custom_call" | custom-call | flops 10000000000 | tf_op jit(solution)/shard_map/inner/pallas_call | solution.py:516
  29.9 0.8 %collective-permute-done.3 = f32[111,8,64]{2,1,0:T(8,128)S(1)} collective-permute-done((f32[111,8,64]{2,1,0:T(8,128)S(1)}, f32[111,8,64]{2,1,0:T(8,128)S(1)}, u32[]{:S(2)}, u32[]{:S(2)}) %collective-permute-start.3) | collective-permute-done | bytes 227360 | tf_op jit(solution)/shard_map/ppermute | solution.py:465
  30.8 0.1 broadcast_select_fusion.5
  30.9 0.2 select_maximum_fusion.1.edge
  31.1 5.9 %outer.1 = (f32[106,8,128]{2,1,0:T(8,128)S(1)}, f32[105,8,128]{2,1,0:T(8,128)S(1)}, f32[128,128]{1,0:T(8,128)S(1)}) custom-call(f32[112,8,128]{2,1,0:T(8,128)S(1)} %select_maximum_fusion.1.edge, f32[2,112,8,128]{3,2,1,0:T(8,128)S(1)} %get-tuple-element.26.pairs, f32[2,112,8,128]{3,2,1,0:T(8,128)S(1)} %get-tuple-element.31.halo, ...), custom_call_target="tpu_custom_call" | custom-call | tf_op jit(solution)/shard_map/outer/pallas_call | solution.py:531
  37.0 24.2 %all_to_all.11 = f32[128,1,128]{2,1,0:T(1,128)S(1)} all-to-all(f32[128,1,128]{2,1,0:T(1,128)S(1)} %bitcast.12), channel_id=1, replica_groups=mesh['down'=8,'cross'=16] {'down','cross'}, dimensions={0} | all-to-all | bytes 131072 | tf_op jit(solution)/shard_map/all_to_all | solution.py:542
  61.2 2.8 %finish.1 = (f32[105,4,512]{2,1,0:T(4,128)}, f32[105,4,512]{2,1,0:T(4,128)}) custom-call(f32[128,128]{1,0:T(8,128)S(1)} %bitcast.11, f32[2,112,8,128]{3,2,1,0:T(8,128)S(1)} %get-tuple-element.26.pairs, f32[2,106,8,128]{3,2,1,0:T(8,128)S(1)} %get-tuple-element.38.image.images, f32[105,8,128]{2,1,0:T(8,128)S(1)} %get-tuple-element.45.inner_second, ...), custom_call_target="tpu_custom_call" | custom-call | tf_op jit(solution)/shard_map/finish/pallas_call | solution.py:544
  (11 shorter events, 0.0 us)
Async XLA Ops:
  2.0 3.6 %copy-start.4 = (f32[5,4,512]{2,1,0:T(4,128)S(1)}, f32[5,4,512]{2,1,0:T(4,128)}, u32[]{:S(2)}) copy-start(f32[5,4,512]{2,1,0:T(4,128)} %param.7) | copy-start | bytes 122884
  2.1 3.6 %copy-start.5 = (f32[4,512]{1,0:T(4,128)S(1)}, f32[4,512]{1,0:T(4,128)}, u32[]{:S(2)}) copy-start(f32[4,512]{1,0:T(4,128)} %param.6) | copy-start | bytes 24580
  2.4 5.9 %copy-start.2 = (f32[3,35,4,512]{3,2,1,0:T(4,128)S(1)}, f32[3,35,4,512]{3,2,1,0:T(4,128)}, u32[]{:S(2)}) copy-start(f32[3,35,4,512]{3,2,1,0:T(4,128)} %param.5) | copy-start | bytes 2580484
  2.4 12.7 %collective-permute-start = (f32[111,2,512]{2,1,0:T(2,128)S(1)}, f32[111,2,512]{2,1,0:T(2,128)S(1)}, u32[]{:S(2)}, u32[]{:S(2)}) collective-permute-start(f32[111,2,512]{2,1,0:T(2,128)S(1)} %get-tuple-element.57), channel_id=1, source_target_pairs={{0,16},{32,48},{64,80},{96,112},{16,0},{48,32},{80,64},{112,96},{1... | collective-permute-start | bytes 1363976 | tf_op jit(solution)/shard_map/ppermute | solution.py:465
  5.0 10.1 %collective-permute-start.1 = (f32[111,2,512]{2,1,0:T(2,128)S(1)}, f32[111,2,512]{2,1,0:T(2,128)S(1)}, u32[]{:S(2)}, u32[]{:S(2)}) collective-permute-start(f32[111,2,512]{2,1,0:T(2,128)S(1)} %get-tuple-element.58), channel_id=1, source_target_pairs={{16,32},{48,64},{80,96},{32,16},{64,48},{96,80},{17,33},{49,65},{8... | collective-permute-start | bytes 1363976 | tf_op jit(solution)/shard_map/ppermute | solution.py:465
  8.4 1.3 %copy-start = (bf16[2,768,384]{2,1,0:T(8,128)(2,1)S(1)}, bf16[2,768,384]{2,1,0:T(8,128)(2,1)}, u32[]{:S(2)}) copy-start(bf16[2,768,384]{2,1,0:T(8,128)(2,1)} %matrix.1.matrix_ref) | copy-start | bytes 3538948
  16.3 4.8 %copy-start.1 = (bf16[2,768,384]{2,1,0:T(8,128)(2,1)S(1)}, bf16[2,768,384]{2,1,0:T(8,128)(2,1)}, u32[]{:S(2)}) copy-start(bf16[2,768,384]{2,1,0:T(8,128)(2,1)} %matrix.1.matrix_ref) | copy-start | bytes 3538948
  16.3 4.8 %copy-start.3 = (f32[13]{0:T(128)S(1)}, f32[13]{0:T(128)}, u32[]{:S(2)}) copy-start(f32[13]{0:T(128)} %weights_ref.5) | copy-start | bytes 160
  16.4 14.4 %collective-permute-start.3 = (f32[111,8,64]{2,1,0:T(8,128)S(1)}, f32[111,8,64]{2,1,0:T(8,128)S(1)}, u32[]{:S(2)}, u32[]{:S(2)}) collective-permute-start(f32[111,8,64]{2,1,0:T(8,128)S(1)} %broadcast_select_fusion.6), channel_id=1, source_target_pairs={{1,2},{3,4},{5,6},{7,8},{9,10},{11,12},{13,14},{2,1},{4,3},{6,5},{... | collective-permute-start | bytes 681992 | tf_op jit(solution)/shard_map/ppermute | solution.py:465
  20.8 10.0 %collective-permute-start.2 = (f32[111,8,64]{2,1,0:T(8,128)S(1)}, f32[111,8,64]{2,1,0:T(8,128)S(1)}, u32[]{:S(2)}, u32[]{:S(2)}) collective-permute-start(f32[111,8,64]{2,1,0:T(8,128)S(1)} %get-tuple-element.50), channel_id=1, source_target_pairs={{0,1},{2,3},{4,5},{6,7},{8,9},{10,11},{12,13},{14,15},{1,0},{3,2},... | collective-permute-start | bytes 681992 | tf_op jit(solution)/shard_map/ppermute | solution.py:465

commit v7 on v6

--- a/solution.py
+++ b/solution.py
@@ -260,6 +260,28 @@
             parts = stencil(own, beside, matrix_ref[0])
             out[number] = same_rows(parts)
             halo_out[number] = other_rows(parts)
+
+
+def join_kernel(flags_ref, one_ref, other_ref, own_ref, extra_ref, beyond_ref, first_ref, second_ref, ends):
+    even_down, even_cross = flags_ref[0] == 1, flags_ref[1] == 1
+    upper = jnp.where(even_down, one_ref[...], other_ref[...])
+    lower = jnp.where(even_down, other_ref[...], one_ref[...])
+    fields = pl.ds(0, STIFF + 1)
+    beyond_ref[fields, :2] = upper
+    beyond_ref[fields, 2:] = lower
+    beyond_ref[STIFF + 1] = jnp.zeros(beyond_ref.shape[1:], jnp.float32)
+    for side, chunk in enumerate(PAIRS[OUTER]):
+        lanes = pl.ds(chunk * LANES, LANES)
+        ends[side, :FIELDS, :ROWS] = own_ref[:, :, lanes]
+        ends[side, FIELDS : STIFF + 1, :ROWS] = extra_ref[:, :, lanes]
+        ends[side, fields, ROWS:] = beyond_ref[fields, :, lanes]
+        ends[side, STIFF + 1] = jnp.zeros((8, LANES), jnp.float32)
+    half = first_ref.shape[0]
+    left = tile_lane() < WIDE
+    head = jnp.where(left, ends[0, :half], pltpu.roll(ends[0, half:], WIDE, 2))
+    tail = jnp.where(left, pltpu.roll(ends[1, :half], WIDE, 2), ends[1, half:])
+    first_ref[...] = jnp.where(even_cross, tail, head)
+    second_ref[...] = jnp.where(even_cross, head, tail)
 
 
 def inner_kernel(
@@ -334,11 +356,11 @@
 
 
 def outer_kernel(
-    edge, pairs, halo, matrix_ref, weights_ref, own_grown, halo_grown,
+    flags_ref, one_ref, other_ref, pairs, halo, matrix_ref, weights_ref, own_grown, halo_grown,
     near, halo_near, grown_near, halo_grown_near,
     image, halo_image, image_grown, halo_image_grown, diag, before_ref,
     image_ref, second_ref, sums_ref,
-    rim, grown, rim_near, rim_grown_near, rim_image,
+    edge, rim, grown, rim_near, rim_grown_near, rim_image,
 ):
     lane, top = tile_lane(), tile_row() < ROWS
     bottom = ~top
@@ -364,6 +386,12 @@
         last = last_chunk(own_near, far_near)
         return parts[0] + ahead + behind + to_rim(last, jnp.zeros_like(last), begin)
 
+    even_cross = flags_ref[1] == 1
+    right = jnp.where(even_cross, one_ref[...], other_ref[...])
+    before = jnp.where(even_cross, other_ref[...], one_ref[...])
+    half = one_ref.shape[0]
+    edge[:half] = jnp.where(left, right, pltpu.roll(before, WIDE, 2))
+    edge[half:] = jnp.where(left, pltpu.roll(right, WIDE, 2), before)
     field = entry_of(edge)
     grow(field, coef_values(field), grown)
     rim_near[...] = rim_stencil(
@@ -426,11 +454,12 @@
     sums_ref[...] = row
 
 
-FINISH_STEPS = 5
+FINISH_STEPS = 3
 
 
 def finish_kernel(
-    sums_ref, pairs, images, inner_second, outer_image, outer_second, field_ref, residual_ref
+    sums_ref, pairs, images, inner_second, outer_image, outer_second,
+    field_out, residual_out, field_ref, residual_ref, sems,
 ):
     total = jnp.sum(sums_ref[...], axis=0, keepdims=True)
     lane = lax.broadcasted_iota(jnp.int32, total.shape, 1)
@@ -445,18 +474,27 @@
     later = fresh / curvature
     both = step + later * larger
     cross = later * step
-    here = pl.ds(pl.program_id(0) * field_ref.shape[0], field_ref.shape[0])
-    for number, image_ref, second_ref in (
-        (OUTER, outer_image, outer_second),
-        (INNER, images.at[INNER], inner_second),
-    ):
-        start, image, second = pairs[number, here], image_ref[here], second_ref[here]
-        field = both * start - cross * image
-        residual = start - both * image + cross * second
-        for side, chunk in enumerate(PAIRS[number]):
-            lanes, rows = pl.ds(chunk * LANES, LANES), slice(side * ROWS, (side + 1) * ROWS)
-            field_ref[:, :, lanes] = field[:, rows]
-            residual_ref[:, :, lanes] = residual[:, rows]
+    count = FIELDS // FINISH_STEPS
+    copies = []
+    for at in range(FINISH_STEPS):
+        here = pl.ds(at * count, count)
+        for number, image_ref, second_ref in (
+            (OUTER, outer_image, outer_second),
+            (INNER, images.at[INNER], inner_second),
+        ):
+            start, image, second = pairs[number, here], image_ref[here], second_ref[here]
+            field = both * start - cross * image
+            residual = start - both * image + cross * second
+            for side, chunk in enumerate(PAIRS[number]):
+                lanes, rows = pl.ds(chunk * LANES, LANES), slice(side * ROWS, (side + 1) * ROWS)
+                field_ref[here, :, lanes] = field[:, rows]
+                residual_ref[here, :, lanes] = residual[:, rows]
+        for number, (ref, out) in enumerate(((field_ref, field_out), (residual_ref, residual_out))):
+            copy = pltpu.make_async_copy(ref.at[here], out.at[here], sems.at[at, number])
+            copy.start()
+            copies.append(copy)
+    for copy in copies:
+        copy.wait()
 
 
 def swap(value, axis, begin):
@@ -470,22 +508,15 @@
     devices = lax.axis_size("down") * lax.axis_size("cross")
     own = right_side.reshape(FIELDS, ROWS, columns)
     extra = jnp.concatenate([coefficients, stiffness[None]], axis=0)
-    all_fields = jnp.concatenate([own, extra], axis=0)
     even = lax.axis_index("down") % 2 == 0
-    head, tail = all_fields[:, :2], all_fields[:, ROWS - 2 :]
-    one = swap(jnp.where(even, tail, head), "down", 0)
-    other = swap(jnp.where(even, head, tail), "down", 1)
-    upper, lower = jnp.where(even, one, other), jnp.where(even, other, one)
-    beyond = jnp.concatenate([upper, lower], axis=1)
-    even = lax.axis_index("cross") % 2 == 0
-    tall = jnp.concatenate([all_fields, beyond], axis=1)
-    head, tail = tall[:, :, :WIDE], tall[:, :, columns - WIDE :]
-    one = swap(jnp.where(even, tail, head), "cross", 0)
-    other = swap(jnp.where(even, head, tail), "cross", 1)
-    right, left = jnp.where(even, one, other), jnp.where(even, other, one)
-    edge = jnp.concatenate([right, left], axis=2)
-    edge = jnp.concatenate([edge, jnp.zeros((1,) + edge.shape[1:], jnp.float32)], axis=0)
-    beyond = jnp.concatenate([beyond, jnp.zeros((1, ROWS, columns), jnp.float32)], axis=0)
+    flags = jnp.stack([even, lax.axis_index("cross") % 2 == 0]).astype(jnp.int32)
+
+    def rows_for(lower):
+        parts = [jnp.where(lower, x[:, ROWS - 2 :], x[:, :2]) for x in (own, extra)]
+        return jnp.concatenate(parts, axis=0)
+
+    one = swap(rows_for(even), "down", 0)
+    other = swap(rows_for(~even), "down", 1)
     vmem = pl.BlockSpec(memory_space=pltpu.VMEM)
     smem = pl.BlockSpec(memory_space=pltpu.SMEM)
     f32, bf16 = jnp.float32, jnp.bfloat16
@@ -513,6 +544,17 @@
         cost_estimate=pl.CostEstimate(flops=5 * 10**9, bytes_accessed=0, transcendentals=0),
         name="start",
     )(own, extra, matrices)
+    half = jax.ShapeDtypeStruct((wider // 2, 8, LANES), f32)
+    beyond, first, second = pl.pallas_call(
+        join_kernel,
+        out_shape=(jax.ShapeDtypeStruct((wider, ROWS, columns), f32), half, half),
+        in_specs=[smem] + [vmem] * 4,
+        out_specs=(vmem,) * 3,
+        scratch_shapes=[pltpu.VMEM((2, wider, 8, LANES), f32)],
+        compiler_params=params,
+        name="join",
+    )(flags, one, other, own, extra)
+    first, second = swap(first, "cross", 0), swap(second, "cross", 1)
     halo, halo_grown, *kept, inner_second, sums = pl.pallas_call(
         inner_kernel,
         out_shape=(
@@ -531,22 +573,27 @@
     outer_image, outer_second, sums = pl.pallas_call(
         outer_kernel,
         out_shape=(one_of(count), one_of(FIELDS), jax.ShapeDtypeStruct((devices, LANES), f32)),
-        in_specs=[vmem] * 4 + [smem] + [vmem] * 12,
+        in_specs=[smem] + [vmem] * 5 + [smem] + [vmem] * 12,
         out_specs=(vmem,) * 3,
         scratch_shapes=[
-            pltpu.VMEM((number, 8, LANES), f32) for number in (wider, count, wider, count, count)
+            pltpu.VMEM((number, 8, LANES), f32)
+            for number in (wider, wider, count, wider, count, count)
         ],
         compiler_params=params,
         name="outer",
-    )(edge, pairs, halo, matrices, stencil_weights, own_grown, halo_grown, *kept, sums)
+    )(flags, first, second, pairs, halo, matrices, stencil_weights, own_grown, halo_grown, *kept, sums)
     sums = lax.all_to_all(sums, ("down", "cross"), 0, 0, tiled=True)
-    block = pl.BlockSpec((FIELDS // FINISH_STEPS, ROWS, columns), lambda i: (i, 0, 0))
+    anywhere = pl.BlockSpec(memory_space=pl.ANY)
     solution_field, residual = pl.pallas_call(
         finish_kernel,
-        grid=(FINISH_STEPS,),
         out_shape=(jax.ShapeDtypeStruct(own.shape, f32), jax.ShapeDtypeStruct(own.shape, f32)),
         in_specs=[vmem] * 6,
-        out_specs=(block, block),
+        out_specs=(anywhere, anywhere),
+        scratch_shapes=[
+            pltpu.VMEM(own.shape, f32),
+            pltpu.VMEM(own.shape, f32),
+            pltpu.SemaphoreType.DMA((FINISH_STEPS, 2)),
+        ],
         compiler_params=params,
         name="finish",
     )(sums, pairs, images, inner_second, outer_image, outer_second)

time: 64.3 us -> 61.3 us (0.953)
  waiting for transfers between devices: 3.05 us -> 1.76 us
  other arithmetic: 3.28 us -> 2.31 us
  blocking collectives: 24.2 us -> 23.5 us
    concatenate x3 -> x2, other arithmetic: 2.01 us -> 0.39 us  [rows_for(): return jnp.concatenate(parts, axis=0)]
    ppermute x4, waiting for transfers between devices: 3.05 us -> 1.76 us  [swap(): return lax.ppermute(value, axis, pairs + [(j, i) for i, j in pairs])]
    all_to_all x1, blocking collectives: 24.2 us -> 23.5 us  [per_device(): sums = lax.all_to_all(sums, ('down', 'cross'), 0, 0, tiled=True)]
    select_n x5 -> x2, other arithmetic: 1.26 us -> 1.82 us  [rows_for(): parts = [jnp.where(lower, x[:, ROWS - 2:], x[:, :2]) for x in (own, extra)]]
    pallas_call x1 -> x2, Pallas kernels: 2.8 us -> 2.49 us  [the longest x1 1.51 us: per_device(): pl.pallas_call(finish_kernel, out_shape=(jax.ShapeDtypeStruct(own.shape,...]
  transfers between devices with their start and end apart: 4 -> 4, of which waited for: 2 -> 1; matrix products, arithmetic and copies ran while one was open for 0% -> 0% of each run, Pallas kernels for 23% -> 24%
where the time goes in v7:
time: 61.3 us; the launch traced here: 61.1 us
  blocking collectives  23.5 us (38%)
  Pallas kernels  23.3 us (38%)
  starting transfers between devices  7.9 us (13%)
  other arithmetic  2.31 us (4%)
  waiting for transfers between devices  1.76 us (3%)
  local copies, waits for them, and re-layouts  1.3 us (2%)
  between operations  0.98 us (2%)
    all_to_all x1, blocking collectives, per_device(): sums = lax.all_to_all(sums, ('down', 'cross'), 0, 0, tiled=True)  23.5 us
    pallas_call x1, Pallas kernels, per_device(): pl.pallas_call(inner_kernel, out_shape=(pair_of(wider), pair_of(count), p...  8.85 us
    ppermute x4, starting transfers between devices, swap(): return lax.ppermute(value, axis, pairs + [(j, i) for i, j in pairs])  7.9 us
    pallas_call x1, Pallas kernels, per_device(): pl.pallas_call(outer_kernel, out_shape=(one_of(count), one_of(FIELDS), ja...  6.05 us
    pallas_call x1, Pallas kernels, per_device(): pl.pallas_call(start_kernel, out_shape=(pair_of(wider), pair_of(count), p...  3.29 us
    pallas_call x1, Pallas kernels, per_device(): pl.pallas_call(matrix_kernel, grid=(2,), out_shape=jax.ShapeDtypeStruct((...  2.63 us
    select_n x2, other arithmetic, rows_for(): parts = [jnp.where(lower, x[:, ROWS - 2:], x[:, :2]) for x in (own, extra)]  1.82 us
    ppermute x4, waiting for transfers between devices, swap(): return lax.ppermute(value, axis, pairs + [(j, i) for i, j in pairs])  1.76 us
  transfers between devices with their start and end apart: 4, of which 1 were waited for; matrix products, arithmetic and copies ran while one was open for 0% of the time, Pallas kernels for 24%

profile of v7, /device:TPU:1, one launch (start us, length us, event | category | flops | bytes accessed | tf_op | source)
XLA Modules:
  0.0 61.1 jit_solution(6268774605506209851)
XLA Ops:
  0.7 1.8 %broadcast_select_fusion = (f32[105,2,512]{2,1,0:T(2,128)S(1)}, f32[105,2,512]{2,1,0:T(2,128)S(1)}) fusion(pred[]{:T(512)S(6)} %not.3, f32[105,4,512]{2,1,0:T(4,128)} %bitcast.10, pred[]{:T(512)} %eq.9), kind=kLoop, calls=%fused_computation.2 | loop fusion | flops 215040 | bytes 1720322 | tf_op jit(solution)/shard_map/jit(_where)/select_n | solution.py:515
  2.5 0.0 copy-done.4
  2.5 0.0 copy-done.5
  2.5 0.2 pad_maximum_fusion
  2.7 2.5 %collective-permute-start = (f32[111,2,512]{2,1,0:T(2,128)S(1)}, f32[111,2,512]{2,1,0:T(2,128)S(1)}, u32[]{:S(2)}, u32[]{:S(2)}) collective-permute-start(f32[111,2,512]{2,1,0:T(2,128)S(1)} %pad_maximum_fusion), channel_id=1, source_target_pairs={{0,16},{32,48},{64,80},{96,112},{16,0},{48,32},{80,64},{112,96},{1... | collective-permute-start | bytes 1363976 | tf_op jit(solution)/shard_map/ppermute | solution.py:503
  5.3 0.2 pad_maximum_fusion.1
  5.5 0.0 copy-start.2
  5.5 0.8 %collective-permute-start.1 = (f32[111,2,512]{2,1,0:T(2,128)S(1)}, f32[111,2,512]{2,1,0:T(2,128)S(1)}, u32[]{:S(2)}, u32[]{:S(2)}) collective-permute-start(f32[111,2,512]{2,1,0:T(2,128)S(1)} %pad_maximum_fusion.1), channel_id=1, source_target_pairs={{16,32},{48,64},{80,96},{32,16},{64,48},{96,80},{17,33},{49,65},{8... | collective-permute-start | bytes 1363976 | tf_op jit(solution)/shard_map/ppermute | solution.py:503
  6.3 0.1 add_convert_fusion.flags_ref
  6.4 2.6 %matrix.1.matrix_ref = bf16[2,768,384]{2,1,0:T(8,128)(2,1)} custom-call(f32[13]{0:T(128)} %weights_ref.5, s32[2,256,384]{2,1,0:T(8,128)} %constant.29.clone.slots_ref), custom_call_target="tpu_custom_call" | custom-call | tf_op jit(solution)/shard_map/matrix/pallas_call | solution.py:524
  9.1 1.3 %copy-done = bf16[2,768,384]{2,1,0:T(8,128)(2,1)S(1)} copy-done((bf16[2,768,384]{2,1,0:T(8,128)(2,1)S(1)}, bf16[2,768,384]{2,1,0:T(8,128)(2,1)}, u32[]{:S(2)}) %copy-start) | copy-done | bytes 1179672
  10.3 3.3 %start.1 = (f32[2,112,8,128]{3,2,1,0:T(8,128)S(1)}, f32[2,106,8,128]{3,2,1,0:T(8,128)S(1)}, f32[2,112,8,128]{3,2,1,0:T(8,128)S(1)}, f32[2,112,8,128]{3,2,1,0:T(8...) custom-call(f32[105,4,512]{2,1,0:T(4,128)S(1)} %bitcast.11, ...), custom_call_target="tpu_custom_call" | custom-call | flops 5000000000 | tf_op jit(solution)/shard_map/start/pallas_call | solution.py:535
  13.6 0.0 copy-start.3
  13.6 1.8 %collective-permute-done.one_ref = f32[111,2,512]{2,1,0:T(2,128)S(1)} collective-permute-done((f32[111,2,512]{2,1,0:T(2,128)S(1)}, f32[111,2,512]{2,1,0:T(2,128)S(1)}, u32[]{:S(2)}, u32[]{:S(2)}) %collective-permute-start) | collective-permute-done | bytes 454688 | tf_op jit(solution)/shard_map/ppermute | solution.py:503
  15.4 0.0 collective-permute-done.1.other_ref
  15.4 1.0 %join.1 = (f32[112,4,512]{2,1,0:T(4,128)S(1)}, f32[56,8,128]{2,1,0:T(8,128)S(1)}, f32[56,8,128]{2,1,0:T(8,128)S(1)}) custom-call(s32[2]{0:T(128)S(1)} %add_convert_fusion.flags_ref, f32[111,2,512]{2,1,0:T(2,128)S(1)} %collective-permute-done.one_ref, f32[111,2,512]{2,1,0:T(2,128)S(1)} %collective-permute-done.1.other_ref, f32[105,4,512]{2,1,0:T(4,128)S(1)} %bitcast.12, ...), custom_call_target="tpu_custom_call" | custom-call | tf_op jit(solution)/shard_map/join/pallas_call | solution.py:548
  16.4 1.3 %collective-permute-start.2 = (f32[56,8,128]{2,1,0:T(8,128)S(1)}, f32[56,8,128]{2,1,0:T(8,128)S(1)}, u32[]{:S(2)}, u32[]{:S(2)}) collective-permute-start(f32[56,8,128]{2,1,0:T(8,128)S(1)} %get-tuple-element.29), channel_id=1, source_target_pairs={{0,1},{2,3},{4,5},{6,7},{8,9},{10,11},{12,13},{14,15},{1,0},{3,2},... | collective-permute-start | bytes 688136 | tf_op jit(solution)/shard_map/ppermute | solution.py:503
  17.7 3.2 %collective-permute-start.3 = (f32[56,8,128]{2,1,0:T(8,128)S(1)}, f32[56,8,128]{2,1,0:T(8,128)S(1)}, u32[]{:S(2)}, u32[]{:S(2)}) collective-permute-start(f32[56,8,128]{2,1,0:T(8,128)S(1)} %get-tuple-element.30), channel_id=1, source_target_pairs={{1,2},{3,4},{5,6},{7,8},{9,10},{11,12},{13,14},{2,1},{4,3},{6,5},{... | collective-permute-start | bytes 688136 | tf_op jit(solution)/shard_map/ppermute | solution.py:503
  20.9 8.8 %inner.1 = (f32[2,112,8,128]{3,2,1,0:T(8,128)S(1)}, f32[2,106,8,128]{3,2,1,0:T(8,128)S(1)}, f32[2,112,8,128]{3,2,1,0:T(8,128)S(1)}, f32[2,112,8,128]{3,2,1,0:T(8...) custom-call(f32[112,4,512]{2,1,0:T(4,128)S(1)} %get-tuple-element.32, ...), custom_call_target="tpu_custom_call" | custom-call | flops 10000000000 | tf_op jit(solution)/shard_map/inner/pallas_call | solution.py:558
  29.8 0.0 collective-permute-done.2.one_ref
  29.8 0.0 collective-permute-done.3.other_ref
  29.8 6.1 %outer.1 = (f32[106,8,128]{2,1,0:T(8,128)S(1)}, f32[105,8,128]{2,1,0:T(8,128)S(1)}, f32[128,128]{1,0:T(8,128)S(1)}) custom-call(s32[2]{0:T(128)S(1)} %add_convert_fusion.flags_ref, f32[56,8,128]{2,1,0:T(8,128)S(1)} %collective-permute-done.2.one_ref, f32[56,8,128]{2,1,0:T(8,128)S(1)} %collective-permute-done.3.other_ref, ...), custom_call_target="tpu_custom_call" | custom-call | tf_op jit(solution)/shard_map/outer/pallas_call | solution.py:573
  35.9 23.5 %all_to_all.11 = f32[128,1,128]{2,1,0:T(1,128)S(1)} all-to-all(f32[128,1,128]{2,1,0:T(1,128)S(1)} %bitcast.14), channel_id=1, replica_groups=mesh['down'=8,'cross'=16] {'down','cross'}, dimensions={0} | all-to-all | bytes 131072 | tf_op jit(solution)/shard_map/all_to_all | solution.py:585
  59.4 1.5 %finish.1 = (f32[105,4,512]{2,1,0:T(4,128)}, f32[105,4,512]{2,1,0:T(4,128)}) custom-call(f32[128,128]{1,0:T(8,128)S(1)} %bitcast.13, f32[2,112,8,128]{3,2,1,0:T(8,128)S(1)} %get-tuple-element.31.pairs, f32[2,106,8,128]{3,2,1,0:T(8,128)S(1)} %get-tuple-element.44.image.images, f32[105,8,128]{2,1,0:T(8,128)S(1)} %get-tuple-element.51.inner_second, ...), custom_call_target="tpu_custom_call" | custom-call | tf_op jit(solution)/shard_map/finish/pallas_call | solution.py:587
  (9 shorter events, 0.1 us)
Async XLA Ops:
  0.6 1.8 %copy-start.4 = (f32[5,4,512]{2,1,0:T(4,128)S(1)}, f32[5,4,512]{2,1,0:T(4,128)}, u32[]{:S(2)}) copy-start(f32[5,4,512]{2,1,0:T(4,128)} %param.7) | copy-start | bytes 122884
  0.6 1.8 %copy-start.5 = (f32[4,512]{1,0:T(4,128)S(1)}, f32[4,512]{1,0:T(4,128)}, u32[]{:S(2)}) copy-start(f32[4,512]{1,0:T(4,128)} %param.6) | copy-start | bytes 24580
  2.7 12.7 %collective-permute-start = (f32[111,2,512]{2,1,0:T(2,128)S(1)}, f32[111,2,512]{2,1,0:T(2,128)S(1)}, u32[]{:S(2)}, u32[]{:S(2)}) collective-permute-start(f32[111,2,512]{2,1,0:T(2,128)S(1)} %pad_maximum_fusion), channel_id=1, source_target_pairs={{0,16},{32,48},{64,80},{96,112},{16,0},{48,32},{80,64},{112,96},{1... | collective-permute-start | bytes 1363976 | tf_op jit(solution)/shard_map/ppermute | solution.py:503
  5.5 3.6 %copy-start.2 = (f32[3,35,4,512]{3,2,1,0:T(4,128)S(1)}, f32[3,35,4,512]{3,2,1,0:T(4,128)}, u32[]{:S(2)}) copy-start(f32[3,35,4,512]{3,2,1,0:T(4,128)} %param.5) | copy-start | bytes 2580484
  5.5 9.9 %collective-permute-start.1 = (f32[111,2,512]{2,1,0:T(2,128)S(1)}, f32[111,2,512]{2,1,0:T(2,128)S(1)}, u32[]{:S(2)}, u32[]{:S(2)}) collective-permute-start(f32[111,2,512]{2,1,0:T(2,128)S(1)} %pad_maximum_fusion.1), channel_id=1, source_target_pairs={{16,32},{48,64},{80,96},{32,16},{64,48},{96,80},{17,33},{49,65},{8... | collective-permute-start | bytes 1363976 | tf_op jit(solution)/shard_map/ppermute | solution.py:503
  9.1 1.3 %copy-start = (bf16[2,768,384]{2,1,0:T(8,128)(2,1)S(1)}, bf16[2,768,384]{2,1,0:T(8,128)(2,1)}, u32[]{:S(2)}) copy-start(bf16[2,768,384]{2,1,0:T(8,128)(2,1)} %matrix.1.matrix_ref) | copy-start | bytes 3538948
  13.6 7.3 %copy-start.1 = (bf16[2,768,384]{2,1,0:T(8,128)(2,1)S(1)}, bf16[2,768,384]{2,1,0:T(8,128)(2,1)}, u32[]{:S(2)}) copy-start(bf16[2,768,384]{2,1,0:T(8,128)(2,1)} %matrix.1.matrix_ref) | copy-start | bytes 3538948
  13.6 7.3 %copy-start.3 = (f32[13]{0:T(128)S(1)}, f32[13]{0:T(128)}, u32[]{:S(2)}) copy-start(f32[13]{0:T(128)} %weights_ref.5) | copy-start | bytes 160
  16.4 13.4 %collective-permute-start.2 = (f32[56,8,128]{2,1,0:T(8,128)S(1)}, f32[56,8,128]{2,1,0:T(8,128)S(1)}, u32[]{:S(2)}, u32[]{:S(2)}) collective-permute-start(f32[56,8,128]{2,1,0:T(8,128)S(1)} %get-tuple-element.29), channel_id=1, source_target_pairs={{0,1},{2,3},{4,5},{6,7},{8,9},{10,11},{12,13},{14,15},{1,0},{3,2},... | collective-permute-start | bytes 688136 | tf_op jit(solution)/shard_map/ppermute | solution.py:503
  17.7 12.1 %collective-permute-start.3 = (f32[56,8,128]{2,1,0:T(8,128)S(1)}, f32[56,8,128]{2,1,0:T(8,128)S(1)}, u32[]{:S(2)}, u32[]{:S(2)}) collective-permute-start(f32[56,8,128]{2,1,0:T(8,128)S(1)} %get-tuple-element.30), channel_id=1, source_target_pairs={{1,2},{3,4},{5,6},{7,8},{9,10},{11,12},{13,14},{2,1},{4,3},{6,5},{... | collective-permute-start | bytes 688136 | tf_op jit(solution)/shard_map/ppermute | solution.py:503

commit v8 on v7

--- a/solution.py
+++ b/solution.py
@@ -189,8 +189,7 @@
 
 
 def grow(field, table, out):
-    @pl.loop(0, COMPS)
-    def each(comp):
+    for comp in range(COMPS):
         base = comp * MODES
         for mode in range(MODES):
             load = lambda other: field(base + other)
@@ -212,7 +211,9 @@
             carry = store(base + mode, value, carry)
         return carry
 
-    return lax.fori_loop(0, COMPS, each, carry)
+    for comp in range(COMPS):
+        carry = each(comp, carry)
+    return carry
 
 
 def masked_store(out, inside):
@@ -314,8 +315,7 @@
         (halo, halo_near, halo_grown_near, halo_image, halo_image_grown),
     ):
 
-        @pl.loop(0, len(PAIRS))
-        def each(number):
+        for number in range(len(PAIRS)):
             field, around = entry_of(ref.at[number]), entry_of(close.at[number])
             coef = coef_values(field)
             values = diag_values(field, around, weights_ref)
@@ -511,12 +511,14 @@
     even = lax.axis_index("down") % 2 == 0
     flags = jnp.stack([even, lax.axis_index("cross") % 2 == 0]).astype(jnp.int32)
 
-    def rows_for(lower):
-        parts = [jnp.where(lower, x[:, ROWS - 2 :], x[:, :2]) for x in (own, extra)]
+    def rows_for(lower, arrays):
+        parts = [jnp.where(lower, x[:, ROWS - 2 :], x[:, :2]) for x in arrays]
         return jnp.concatenate(parts, axis=0)
 
-    one = swap(rows_for(even), "down", 0)
-    other = swap(rows_for(~even), "down", 1)
+    sent = rows_for(~even, (own, extra))
+    other = swap(sent, "down", 1)
+    here, there, _ = lax.optimization_barrier((own, extra, sent))
+    one = swap(rows_for(even, (here, there)), "down", 0)
     vmem = pl.BlockSpec(memory_space=pltpu.VMEM)
     smem = pl.BlockSpec(memory_space=pltpu.SMEM)
     f32, bf16 = jnp.float32, jnp.bfloat16

time: 61.3 us -> 58.8 us (0.959)
  blocking collectives: 23.5 us -> 18.9 us
  starting transfers between devices: 7.9 us -> 10.9 us
  Pallas kernels: 23.3 us -> 21.2 us
  waiting for transfers between devices: 1.76 us -> 2.66 us
    all_to_all x1, blocking collectives: 23.5 us -> 18.9 us  [per_device(): sums = lax.all_to_all(sums, ('down', 'cross'), 0, 0, tiled=True)]
    ppermute x4, starting transfers between devices: 7.9 us -> 10.9 us  [swap(): return lax.ppermute(value, axis, pairs + [(j, i) for i, j in pairs])]
    pallas_call x1, Pallas kernels: 8.85 us -> 7.42 us  [per_device(): pl.pallas_call(inner_kernel, out_shape=(pair_of(wider), pair_of(count), p...]
    ppermute x4, waiting for transfers between devices: 1.76 us -> 2.66 us  [swap(): return lax.ppermute(value, axis, pairs + [(j, i) for i, j in pairs])]
    select_n x2 -> x4, other arithmetic: 1.82 us -> 2.1 us  [rows_for(): parts = [jnp.where(lower, x[:, ROWS - 2:], x[:, :2]) for x in arrays]]
  transfers between devices with their start and end apart: 4 -> 4, of which waited for: 1 -> 1; matrix products, arithmetic and copies ran while one was open for 0% -> 1% of each run, Pallas kernels for 24% -> 23%
where the time goes in v8:
time: 58.8 us; the launch traced here: 58.5 us
  Pallas kernels  21.2 us (36%)
  blocking collectives  18.9 us (32%)
  starting transfers between devices  10.9 us (19%)
  waiting for transfers between devices  2.66 us (5%)
  other arithmetic  2.59 us (4%)
  local copies, waits for them, and re-layouts  1.29 us (2%)
  between operations  0.99 us (2%)
    all_to_all x1, blocking collectives, per_device(): sums = lax.all_to_all(sums, ('down', 'cross'), 0, 0, tiled=True)  18.9 us
    ppermute x4, starting transfers between devices, swap(): return lax.ppermute(value, axis, pairs + [(j, i) for i, j in pairs])  10.9 us
    pallas_call x1, Pallas kernels, per_device(): pl.pallas_call(inner_kernel, out_shape=(pair_of(wider), pair_of(count), p...  7.42 us
    pallas_call x1, Pallas kernels, per_device(): pl.pallas_call(outer_kernel, out_shape=(one_of(count), one_of(FIELDS), ja...  5.45 us
    pallas_call x1, Pallas kernels, per_device(): pl.pallas_call(start_kernel, out_shape=(pair_of(wider), pair_of(count), p...  3.18 us
    ppermute x4, waiting for transfers between devices, swap(): return lax.ppermute(value, axis, pairs + [(j, i) for i, j in pairs])  2.66 us
    pallas_call x1, Pallas kernels, per_device(): pl.pallas_call(matrix_kernel, grid=(2,), out_shape=jax.ShapeDtypeStruct((...  2.63 us
    select_n x4, other arithmetic, rows_for(): parts = [jnp.where(lower, x[:, ROWS - 2:], x[:, :2]) for x in arrays]  2.1 us
  transfers between devices with their start and end apart: 4, of which 1 were waited for; matrix products, arithmetic and copies ran while one was open for 1% of the time, Pallas kernels for 23%

profile of v8, /device:TPU:1, one launch (start us, length us, event | category | flops | bytes accessed | tf_op | source)
XLA Modules:
  0.0 58.5 jit_solution(1863141451217879746)
XLA Ops:
  0.6 0.0 copy-start.4
  0.7 0.0 copy-start
  0.7 1.8 %slice_select_fusion = f32[105,2,512]{2,1,0:T(2,128)S(1)} fusion(f32[105,4,512]{2,1,0:T(4,128)} %bitcast.10, pred[]{:T(512)S(6)} %not.3), kind=kLoop, calls=%fused_computation.2 | loop fusion | flops 107520 | bytes 1290241 | tf_op jit(solution)/shard_map/jit(_where)/select_n | solution.py:515
  2.6 0.2 pad_maximum_fusion
  2.8 0.7 %collective-permute-start.1 = (f32[111,2,512]{2,1,0:T(2,128)S(1)}, f32[111,2,512]{2,1,0:T(2,128)S(1)}, u32[]{:S(2)}, u32[]{:S(2)}) collective-permute-start(f32[111,2,512]{2,1,0:T(2,128)S(1)} %pad_maximum_fusion), channel_id=1, source_target_pairs={{16,32},{48,64},{80,96},{32,16},{64,48},{96,80},{17,33},{49,65},{8... | collective-permute-start | bytes 1363976 | tf_op jit(solution)/shard_map/ppermute | solution.py:503
  3.5 0.2 slice_select_fusion.1
  3.8 0.2 pad_maximum_fusion.1
  4.0 5.4 %collective-permute-start = (f32[111,2,512]{2,1,0:T(2,128)S(1)}, f32[111,2,512]{2,1,0:T(2,128)S(1)}, u32[]{:S(2)}, u32[]{:S(2)}) collective-permute-start(f32[111,2,512]{2,1,0:T(2,128)S(1)} %pad_maximum_fusion.1), channel_id=1, source_target_pairs={{0,16},{32,48},{64,80},{96,112},{16,0},{48,32},{80,64},{112,96},{1... | collective-permute-start | bytes 1363976 | tf_op jit(solution)/shard_map/ppermute | solution.py:503
  9.4 0.1 add_convert_fusion.flags_ref
  9.4 2.6 %matrix.1.matrix_ref = bf16[2,768,384]{2,1,0:T(8,128)(2,1)} custom-call(f32[13]{0:T(128)} %weights_ref.5, s32[2,256,384]{2,1,0:T(8,128)} %constant.29.clone.slots_ref), custom_call_target="tpu_custom_call" | custom-call | tf_op jit(solution)/shard_map/matrix/pallas_call | solution.py:526
  12.1 1.3 %copy-done.1 = bf16[2,768,384]{2,1,0:T(8,128)(2,1)S(1)} copy-done((bf16[2,768,384]{2,1,0:T(8,128)(2,1)S(1)}, bf16[2,768,384]{2,1,0:T(8,128)(2,1)}, u32[]{:S(2)}) %copy-start.1) | copy-done | bytes 1179672
  13.3 3.2 %start.1 = (f32[2,112,8,128]{3,2,1,0:T(8,128)S(1)}, f32[2,106,8,128]{3,2,1,0:T(8,128)S(1)}, f32[2,112,8,128]{3,2,1,0:T(8,128)S(1)}, f32[2,112,8,128]{3,2,1,0:T(8...) custom-call(f32[105,4,512]{2,1,0:T(4,128)S(1)} %bitcast.12, ...), custom_call_target="tpu_custom_call" | custom-call | flops 5000000000 | tf_op jit(solution)/shard_map/start/pallas_call | solution.py:537
  16.5 0.0 copy-start.3
  16.6 2.6 %collective-permute-done.one_ref = f32[111,2,512]{2,1,0:T(2,128)S(1)} collective-permute-done((f32[111,2,512]{2,1,0:T(2,128)S(1)}, f32[111,2,512]{2,1,0:T(2,128)S(1)}, u32[]{:S(2)}, u32[]{:S(2)}) %collective-permute-start) | collective-permute-done | bytes 454688 | tf_op jit(solution)/shard_map/ppermute | solution.py:503
  19.2 0.0 collective-permute-done.1.other_ref
  19.2 1.0 %join.1 = (f32[112,4,512]{2,1,0:T(4,128)S(1)}, f32[56,8,128]{2,1,0:T(8,128)S(1)}, f32[56,8,128]{2,1,0:T(8,128)S(1)}) custom-call(s32[2]{0:T(128)S(1)} %add_convert_fusion.flags_ref, f32[111,2,512]{2,1,0:T(2,128)S(1)} %collective-permute-done.one_ref, f32[111,2,512]{2,1,0:T(2,128)S(1)} %collective-permute-done.1.other_ref, f32[105,4,512]{2,1,0:T(4,128)S(1)} %bitcast.13, ...), custom_call_target="tpu_custom_call" | custom-call | tf_op jit(solution)/shard_map/join/pallas_call | solution.py:550
  20.2 1.6 %collective-permute-start.2 = (f32[56,8,128]{2,1,0:T(8,128)S(1)}, f32[56,8,128]{2,1,0:T(8,128)S(1)}, u32[]{:S(2)}, u32[]{:S(2)}) collective-permute-start(f32[56,8,128]{2,1,0:T(8,128)S(1)} %get-tuple-element.33), channel_id=1, source_target_pairs={{0,1},{2,3},{4,5},{6,7},{8,9},{10,11},{12,13},{14,15},{1,0},{3,2},... | collective-permute-start | bytes 688136 | tf_op jit(solution)/shard_map/ppermute | solution.py:503
  21.8 3.2 %collective-permute-start.3 = (f32[56,8,128]{2,1,0:T(8,128)S(1)}, f32[56,8,128]{2,1,0:T(8,128)S(1)}, u32[]{:S(2)}, u32[]{:S(2)}) collective-permute-start(f32[56,8,128]{2,1,0:T(8,128)S(1)} %get-tuple-element.34), channel_id=1, source_target_pairs={{1,2},{3,4},{5,6},{7,8},{9,10},{11,12},{13,14},{2,1},{4,3},{6,5},{... | collective-permute-start | bytes 688136 | tf_op jit(solution)/shard_map/ppermute | solution.py:503
  25.0 7.4 %inner.1 = (f32[2,112,8,128]{3,2,1,0:T(8,128)S(1)}, f32[2,106,8,128]{3,2,1,0:T(8,128)S(1)}, f32[2,112,8,128]{3,2,1,0:T(8,128)S(1)}, f32[2,112,8,128]{3,2,1,0:T(8...) custom-call(f32[112,4,512]{2,1,0:T(4,128)S(1)} %get-tuple-element.36, ...), custom_call_target="tpu_custom_call" | custom-call | flops 10000000000 | tf_op jit(solution)/shard_map/inner/pallas_call | solution.py:560
  32.5 0.0 collective-permute-done.2.one_ref
  32.5 0.0 collective-permute-done.3.other_ref
  32.5 5.4 %outer.1 = (f32[106,8,128]{2,1,0:T(8,128)S(1)}, f32[105,8,128]{2,1,0:T(8,128)S(1)}, f32[128,128]{1,0:T(8,128)S(1)}) custom-call(s32[2]{0:T(128)S(1)} %add_convert_fusion.flags_ref, f32[56,8,128]{2,1,0:T(8,128)S(1)} %collective-permute-done.2.one_ref, f32[56,8,128]{2,1,0:T(8,128)S(1)} %collective-permute-done.3.other_ref, ...), custom_call_target="tpu_custom_call" | custom-call | tf_op jit(solution)/shard_map/outer/pallas_call | solution.py:575
  37.9 18.9 %all_to_all.11 = f32[128,1,128]{2,1,0:T(1,128)S(1)} all-to-all(f32[128,1,128]{2,1,0:T(1,128)S(1)} %bitcast.15), channel_id=1, replica_groups=mesh['down'=8,'cross'=16] {'down','cross'}, dimensions={0} | all-to-all | bytes 131072 | tf_op jit(solution)/shard_map/all_to_all | solution.py:587
  56.9 1.5 %finish.1 = (f32[105,4,512]{2,1,0:T(4,128)}, f32[105,4,512]{2,1,0:T(4,128)}) custom-call(f32[128,128]{1,0:T(8,128)S(1)} %bitcast.14, f32[2,112,8,128]{3,2,1,0:T(8,128)S(1)} %get-tuple-element.35.pairs, f32[2,106,8,128]{3,2,1,0:T(8,128)S(1)} %get-tuple-element.48.image.images, f32[105,8,128]{2,1,0:T(8,128)S(1)} %get-tuple-element.55.inner_second, ...), custom_call_target="tpu_custom_call" | custom-call | tf_op jit(solution)/shard_map/finish/pallas_call | solution.py:589
  (11 shorter events, 0.1 us)
Async XLA Ops:
  0.6 1.9 %copy-start.4 = (f32[5,4,512]{2,1,0:T(4,128)S(1)}, f32[5,4,512]{2,1,0:T(4,128)}, u32[]{:S(2)}) copy-start(f32[5,4,512]{2,1,0:T(4,128)} %param.7) | copy-start | bytes 122884
  0.6 1.9 %copy-start.5 = (f32[4,512]{1,0:T(4,128)S(1)}, f32[4,512]{1,0:T(4,128)}, u32[]{:S(2)}) copy-start(f32[4,512]{1,0:T(4,128)} %param.6) | copy-start | bytes 24580
  0.7 2.8 %copy-start = (f32[3,35,4,512]{3,2,1,0:T(4,128)S(1)}, f32[3,35,4,512]{3,2,1,0:T(4,128)}, u32[]{:S(2)}) copy-start(f32[3,35,4,512]{3,2,1,0:T(4,128)} %param.5) | copy-start | bytes 2580484
  2.8 16.4 %collective-permute-start.1 = (f32[111,2,512]{2,1,0:T(2,128)S(1)}, f32[111,2,512]{2,1,0:T(2,128)S(1)}, u32[]{:S(2)}, u32[]{:S(2)}) collective-permute-start(f32[111,2,512]{2,1,0:T(2,128)S(1)} %pad_maximum_fusion), channel_id=1, source_target_pairs={{16,32},{48,64},{80,96},{32,16},{64,48},{96,80},{17,33},{49,65},{8... | collective-permute-start | bytes 1363976 | tf_op jit(solution)/shard_map/ppermute | solution.py:503
  4.0 15.2 %collective-permute-start = (f32[111,2,512]{2,1,0:T(2,128)S(1)}, f32[111,2,512]{2,1,0:T(2,128)S(1)}, u32[]{:S(2)}, u32[]{:S(2)}) collective-permute-start(f32[111,2,512]{2,1,0:T(2,128)S(1)} %pad_maximum_fusion.1), channel_id=1, source_target_pairs={{0,16},{32,48},{64,80},{96,112},{16,0},{48,32},{80,64},{112,96},{1... | collective-permute-start | bytes 1363976 | tf_op jit(solution)/shard_map/ppermute | solution.py:503
  12.1 1.3 %copy-start.1 = (bf16[2,768,384]{2,1,0:T(8,128)(2,1)S(1)}, bf16[2,768,384]{2,1,0:T(8,128)(2,1)}, u32[]{:S(2)}) copy-start(bf16[2,768,384]{2,1,0:T(8,128)(2,1)} %matrix.1.matrix_ref) | copy-start | bytes 3538948
  16.5 8.5 %copy-start.2 = (bf16[2,768,384]{2,1,0:T(8,128)(2,1)S(1)}, bf16[2,768,384]{2,1,0:T(8,128)(2,1)}, u32[]{:S(2)}) copy-start(bf16[2,768,384]{2,1,0:T(8,128)(2,1)} %matrix.1.matrix_ref) | copy-start | bytes 3538948
  16.5 8.5 %copy-start.3 = (f32[13]{0:T(128)S(1)}, f32[13]{0:T(128)}, u32[]{:S(2)}) copy-start(f32[13]{0:T(128)} %weights_ref.5) | copy-start | bytes 160
  20.2 12.3 %collective-permute-start.2 = (f32[56,8,128]{2,1,0:T(8,128)S(1)}, f32[56,8,128]{2,1,0:T(8,128)S(1)}, u32[]{:S(2)}, u32[]{:S(2)}) collective-permute-start(f32[56,8,128]{2,1,0:T(8,128)S(1)} %get-tuple-element.33), channel_id=1, source_target_pairs={{0,1},{2,3},{4,5},{6,7},{8,9},{10,11},{12,13},{14,15},{1,0},{3,2},... | collective-permute-start | bytes 688136 | tf_op jit(solution)/shard_map/ppermute | solution.py:503
  21.8 10.7 %collective-permute-start.3 = (f32[56,8,128]{2,1,0:T(8,128)S(1)}, f32[56,8,128]{2,1,0:T(8,128)S(1)}, u32[]{:S(2)}, u32[]{:S(2)}) collective-permute-start(f32[56,8,128]{2,1,0:T(8,128)S(1)} %get-tuple-element.34), channel_id=1, source_target_pairs={{1,2},{3,4},{5,6},{7,8},{9,10},{11,12},{13,14},{2,1},{4,3},{6,5},{... | collective-permute-start | bytes 688136 | tf_op jit(solution)/shard_map/ppermute | solution.py:503

commit v9 on v8

--- a/solution.py
+++ b/solution.py
@@ -263,7 +263,7 @@
             halo_out[number] = other_rows(parts)
 
 
-def join_kernel(flags_ref, one_ref, other_ref, own_ref, extra_ref, beyond_ref, first_ref, second_ref, ends):
+def join_kernel(flags_ref, one_ref, other_ref, pairs, beyond_ref, first_ref, second_ref, ends):
     even_down, even_cross = flags_ref[0] == 1, flags_ref[1] == 1
     upper = jnp.where(even_down, one_ref[...], other_ref[...])
     lower = jnp.where(even_down, other_ref[...], one_ref[...])
@@ -272,11 +272,11 @@
     beyond_ref[fields, 2:] = lower
     beyond_ref[STIFF + 1] = jnp.zeros(beyond_ref.shape[1:], jnp.float32)
     for side, chunk in enumerate(PAIRS[OUTER]):
-        lanes = pl.ds(chunk * LANES, LANES)
-        ends[side, :FIELDS, :ROWS] = own_ref[:, :, lanes]
-        ends[side, FIELDS : STIFF + 1, :ROWS] = extra_ref[:, :, lanes]
-        ends[side, fields, ROWS:] = beyond_ref[fields, :, lanes]
-        ends[side, STIFF + 1] = jnp.zeros((8, LANES), jnp.float32)
+        ends[side, :, ROWS:] = beyond_ref[:, :, pl.ds(chunk * LANES, LANES)]
+    top = tile_row() < ROWS
+    outer = pairs[OUTER]
+    ends[0] = jnp.where(top, outer, ends[0])
+    ends[1] = jnp.where(top, pltpu.roll(outer, ROWS, 1), ends[1])
     half = first_ref.shape[0]
     left = tile_lane() < WIDE
     head = jnp.where(left, ends[0, :half], pltpu.roll(ends[0, half:], WIDE, 2))
@@ -454,7 +454,7 @@
     sums_ref[...] = row
 
 
-FINISH_STEPS = 3
+FINISH_STEPS = 7
 
 
 def finish_kernel(
@@ -550,12 +550,12 @@
     beyond, first, second = pl.pallas_call(
         join_kernel,
         out_shape=(jax.ShapeDtypeStruct((wider, ROWS, columns), f32), half, half),
-        in_specs=[smem] + [vmem] * 4,
+        in_specs=[smem] + [vmem] * 3,
         out_specs=(vmem,) * 3,
         scratch_shapes=[pltpu.VMEM((2, wider, 8, LANES), f32)],
         compiler_params=params,
         name="join",
-    )(flags, one, other, own, extra)
+    )(flags, one, other, pairs)
     first, second = swap(first, "cross", 0), swap(second, "cross", 1)
     halo, halo_grown, *kept, inner_second, sums = pl.pallas_call(
         inner_kernel,

time: 58.8 us -> 58.9 us (level)
  no operation moved by 1% of the time
where the time goes in v9:
time: 58.9 us; the launch traced here: 58.7 us
  Pallas kernels  21.3 us (36%)
  blocking collectives  18.9 us (32%)
  starting transfers between devices  10.9 us (19%)
  waiting for transfers between devices  2.69 us (5%)
  other arithmetic  2.59 us (4%)
  local copies, waits for them, and re-layouts  1.29 us (2%)
  between operations  0.99 us (2%)
    all_to_all x1, blocking collectives, per_device(): sums = lax.all_to_all(sums, ('down', 'cross'), 0, 0, tiled=True)  18.9 us
    ppermute x4, starting transfers between devices, swap(): return lax.ppermute(value, axis, pairs + [(j, i) for i, j in pairs])  10.9 us
    pallas_call x1, Pallas kernels, per_device(): pl.pallas_call(inner_kernel, out_shape=(pair_of(wider), pair_of(count), p...  7.55 us
    pallas_call x1, Pallas kernels, per_device(): pl.pallas_call(outer_kernel, out_shape=(one_of(count), one_of(FIELDS), ja...  5.49 us
    pallas_call x1, Pallas kernels, per_device(): pl.pallas_call(start_kernel, out_shape=(pair_of(wider), pair_of(count), p...  3.15 us
    ppermute x4, waiting for transfers between devices, swap(): return lax.ppermute(value, axis, pairs + [(j, i) for i, j in pairs])  2.69 us
    pallas_call x1, Pallas kernels, per_device(): pl.pallas_call(matrix_kernel, grid=(2,), out_shape=jax.ShapeDtypeStruct((...  2.63 us
    select_n x4, other arithmetic, rows_for(): parts = [jnp.where(lower, x[:, ROWS - 2:], x[:, :2]) for x in arrays]  2.1 us
  transfers between devices with their start and end apart: 4, of which 1 were waited for; matrix products, arithmetic and copies ran while one was open for 1% of the time, Pallas kernels for 23%

profile of v9, /device:TPU:1, one launch (start us, length us, event | category | flops | bytes accessed | tf_op | source)
XLA Modules:
  0.0 58.7 jit_solution(4221123503129500262)
XLA Ops:
  0.6 0.0 copy-start.4
  0.7 0.0 copy-start.2
  0.7 1.8 %slice_select_fusion = f32[105,2,512]{2,1,0:T(2,128)S(1)} fusion(f32[105,4,512]{2,1,0:T(4,128)} %bitcast.10, pred[]{:T(512)S(6)} %not.3), kind=kLoop, calls=%fused_computation.2 | loop fusion | flops 107520 | bytes 1290241 | tf_op jit(solution)/shard_map/jit(_where)/select_n | solution.py:515
  2.6 0.2 pad_maximum_fusion
  2.8 0.7 %collective-permute-start.1 = (f32[111,2,512]{2,1,0:T(2,128)S(1)}, f32[111,2,512]{2,1,0:T(2,128)S(1)}, u32[]{:S(2)}, u32[]{:S(2)}) collective-permute-start(f32[111,2,512]{2,1,0:T(2,128)S(1)} %pad_maximum_fusion), channel_id=1, source_target_pairs={{16,32},{48,64},{80,96},{32,16},{64,48},{96,80},{17,33},{49,65},{8... | collective-permute-start | bytes 1363976 | tf_op jit(solution)/shard_map/ppermute | solution.py:503
  3.5 0.2 slice_select_fusion.1
  3.8 0.2 pad_maximum_fusion.1
  4.0 5.4 %collective-permute-start = (f32[111,2,512]{2,1,0:T(2,128)S(1)}, f32[111,2,512]{2,1,0:T(2,128)S(1)}, u32[]{:S(2)}, u32[]{:S(2)}) collective-permute-start(f32[111,2,512]{2,1,0:T(2,128)S(1)} %pad_maximum_fusion.1), channel_id=1, source_target_pairs={{0,16},{32,48},{64,80},{96,112},{16,0},{48,32},{80,64},{112,96},{1... | collective-permute-start | bytes 1363976 | tf_op jit(solution)/shard_map/ppermute | solution.py:503
  9.4 0.1 add_convert_fusion.flags_ref
  9.4 2.6 %matrix.1.matrix_ref = bf16[2,768,384]{2,1,0:T(8,128)(2,1)} custom-call(f32[13]{0:T(128)} %weights_ref.5, s32[2,256,384]{2,1,0:T(8,128)} %constant.29.clone.slots_ref), custom_call_target="tpu_custom_call" | custom-call | tf_op jit(solution)/shard_map/matrix/pallas_call | solution.py:526
  12.1 1.3 %copy-done = bf16[2,768,384]{2,1,0:T(8,128)(2,1)S(1)} copy-done((bf16[2,768,384]{2,1,0:T(8,128)(2,1)S(1)}, bf16[2,768,384]{2,1,0:T(8,128)(2,1)}, u32[]{:S(2)}) %copy-start) | copy-done | bytes 1179672
  13.3 3.1 %start.1 = (f32[2,112,8,128]{3,2,1,0:T(8,128)S(1)}, f32[2,106,8,128]{3,2,1,0:T(8,128)S(1)}, f32[2,112,8,128]{3,2,1,0:T(8,128)S(1)}, f32[2,112,8,128]{3,2,1,0:T(8...) custom-call(f32[105,4,512]{2,1,0:T(4,128)S(1)} %bitcast.12, ...), custom_call_target="tpu_custom_call" | custom-call | flops 5000000000 | tf_op jit(solution)/shard_map/start/pallas_call | solution.py:537
  16.5 0.0 copy-start.3
  16.5 2.7 %collective-permute-done.one_ref = f32[111,2,512]{2,1,0:T(2,128)S(1)} collective-permute-done((f32[111,2,512]{2,1,0:T(2,128)S(1)}, f32[111,2,512]{2,1,0:T(2,128)S(1)}, u32[]{:S(2)}, u32[]{:S(2)}) %collective-permute-start) | collective-permute-done | bytes 454688 | tf_op jit(solution)/shard_map/ppermute | solution.py:503
  19.2 0.0 collective-permute-done.1.other_ref
  19.2 1.0 %join.1 = (f32[112,4,512]{2,1,0:T(4,128)S(1)}, f32[56,8,128]{2,1,0:T(8,128)S(1)}, f32[56,8,128]{2,1,0:T(8,128)S(1)}) custom-call(s32[2]{0:T(128)S(1)} %add_convert_fusion.flags_ref, f32[111,2,512]{2,1,0:T(2,128)S(1)} %collective-permute-done.one_ref, f32[111,2,512]{2,1,0:T(2,128)S(1)} %collective-permute-done.1.other_ref, ...), custom_call_target="tpu_custom_call" | custom-call | tf_op jit(solution)/shard_map/join/pallas_call | solution.py:550
  20.2 1.6 %collective-permute-start.2 = (f32[56,8,128]{2,1,0:T(8,128)S(1)}, f32[56,8,128]{2,1,0:T(8,128)S(1)}, u32[]{:S(2)}, u32[]{:S(2)}) collective-permute-start(f32[56,8,128]{2,1,0:T(8,128)S(1)} %get-tuple-element.34), channel_id=1, source_target_pairs={{0,1},{2,3},{4,5},{6,7},{8,9},{10,11},{12,13},{14,15},{1,0},{3,2},... | collective-permute-start | bytes 688136 | tf_op jit(solution)/shard_map/ppermute | solution.py:503
  21.8 3.2 %collective-permute-start.3 = (f32[56,8,128]{2,1,0:T(8,128)S(1)}, f32[56,8,128]{2,1,0:T(8,128)S(1)}, u32[]{:S(2)}, u32[]{:S(2)}) collective-permute-start(f32[56,8,128]{2,1,0:T(8,128)S(1)} %get-tuple-element.35), channel_id=1, source_target_pairs={{1,2},{3,4},{5,6},{7,8},{9,10},{11,12},{13,14},{2,1},{4,3},{6,5},{... | collective-permute-start | bytes 688136 | tf_op jit(solution)/shard_map/ppermute | solution.py:503
  25.1 7.5 %inner.1 = (f32[2,112,8,128]{3,2,1,0:T(8,128)S(1)}, f32[2,106,8,128]{3,2,1,0:T(8,128)S(1)}, f32[2,112,8,128]{3,2,1,0:T(8,128)S(1)}, f32[2,112,8,128]{3,2,1,0:T(8...) custom-call(f32[112,4,512]{2,1,0:T(4,128)S(1)} %get-tuple-element.36, ...), custom_call_target="tpu_custom_call" | custom-call | flops 10000000000 | tf_op jit(solution)/shard_map/inner/pallas_call | solution.py:560
  32.6 0.0 collective-permute-done.2.one_ref
  32.6 0.0 collective-permute-done.3.other_ref
  32.6 5.5 %outer.1 = (f32[106,8,128]{2,1,0:T(8,128)S(1)}, f32[105,8,128]{2,1,0:T(8,128)S(1)}, f32[128,128]{1,0:T(8,128)S(1)}) custom-call(s32[2]{0:T(128)S(1)} %add_convert_fusion.flags_ref, f32[56,8,128]{2,1,0:T(8,128)S(1)} %collective-permute-done.2.one_ref, f32[56,8,128]{2,1,0:T(8,128)S(1)} %collective-permute-done.3.other_ref, ...), custom_call_target="tpu_custom_call" | custom-call | tf_op jit(solution)/shard_map/outer/pallas_call | solution.py:575
  38.1 18.9 %all_to_all.11 = f32[128,1,128]{2,1,0:T(1,128)S(1)} all-to-all(f32[128,1,128]{2,1,0:T(1,128)S(1)} %bitcast.14), channel_id=1, replica_groups=mesh['down'=8,'cross'=16] {'down','cross'}, dimensions={0} | all-to-all | bytes 131072 | tf_op jit(solution)/shard_map/all_to_all | solution.py:587
  57.0 1.5 %finish.1 = (f32[105,4,512]{2,1,0:T(4,128)}, f32[105,4,512]{2,1,0:T(4,128)}) custom-call(f32[128,128]{1,0:T(8,128)S(1)} %bitcast.13, f32[2,112,8,128]{3,2,1,0:T(8,128)S(1)} %get-tuple-element.33.pairs, f32[2,106,8,128]{3,2,1,0:T(8,128)S(1)} %get-tuple-element.48.image.images, f32[105,8,128]{2,1,0:T(8,128)S(1)} %get-tuple-element.55.inner_second, ...), custom_call_target="tpu_custom_call" | custom-call | tf_op jit(solution)/shard_map/finish/pallas_call | solution.py:589
  (11 shorter events, 0.1 us)
Async XLA Ops:
  0.6 1.9 %copy-start.4 = (f32[5,4,512]{2,1,0:T(4,128)S(1)}, f32[5,4,512]{2,1,0:T(4,128)}, u32[]{:S(2)}) copy-start(f32[5,4,512]{2,1,0:T(4,128)} %param.7) | copy-start | bytes 122884
  0.6 1.9 %copy-start.5 = (f32[4,512]{1,0:T(4,128)S(1)}, f32[4,512]{1,0:T(4,128)}, u32[]{:S(2)}) copy-start(f32[4,512]{1,0:T(4,128)} %param.6) | copy-start | bytes 24580
  0.7 2.8 %copy-start.2 = (f32[3,35,4,512]{3,2,1,0:T(4,128)S(1)}, f32[3,35,4,512]{3,2,1,0:T(4,128)}, u32[]{:S(2)}) copy-start(f32[3,35,4,512]{3,2,1,0:T(4,128)} %param.5) | copy-start | bytes 2580484
  2.8 16.4 %collective-permute-start.1 = (f32[111,2,512]{2,1,0:T(2,128)S(1)}, f32[111,2,512]{2,1,0:T(2,128)S(1)}, u32[]{:S(2)}, u32[]{:S(2)}) collective-permute-start(f32[111,2,512]{2,1,0:T(2,128)S(1)} %pad_maximum_fusion), channel_id=1, source_target_pairs={{16,32},{48,64},{80,96},{32,16},{64,48},{96,80},{17,33},{49,65},{8... | collective-permute-start | bytes 1363976 | tf_op jit(solution)/shard_map/ppermute | solution.py:503
  4.0 15.2 %collective-permute-start = (f32[111,2,512]{2,1,0:T(2,128)S(1)}, f32[111,2,512]{2,1,0:T(2,128)S(1)}, u32[]{:S(2)}, u32[]{:S(2)}) collective-permute-start(f32[111,2,512]{2,1,0:T(2,128)S(1)} %pad_maximum_fusion.1), channel_id=1, source_target_pairs={{0,16},{32,48},{64,80},{96,112},{16,0},{48,32},{80,64},{112,96},{1... | collective-permute-start | bytes 1363976 | tf_op jit(solution)/shard_map/ppermute | solution.py:503
  12.1 1.3 %copy-start = (bf16[2,768,384]{2,1,0:T(8,128)(2,1)S(1)}, bf16[2,768,384]{2,1,0:T(8,128)(2,1)}, u32[]{:S(2)}) copy-start(bf16[2,768,384]{2,1,0:T(8,128)(2,1)} %matrix.1.matrix_ref) | copy-start | bytes 3538948
  16.5 8.5 %copy-start.1 = (bf16[2,768,384]{2,1,0:T(8,128)(2,1)S(1)}, bf16[2,768,384]{2,1,0:T(8,128)(2,1)}, u32[]{:S(2)}) copy-start(bf16[2,768,384]{2,1,0:T(8,128)(2,1)} %matrix.1.matrix_ref) | copy-start | bytes 3538948
  16.5 8.5 %copy-start.3 = (f32[13]{0:T(128)S(1)}, f32[13]{0:T(128)}, u32[]{:S(2)}) copy-start(f32[13]{0:T(128)} %weights_ref.5) | copy-start | bytes 160
  20.2 12.4 %collective-permute-start.2 = (f32[56,8,128]{2,1,0:T(8,128)S(1)}, f32[56,8,128]{2,1,0:T(8,128)S(1)}, u32[]{:S(2)}, u32[]{:S(2)}) collective-permute-start(f32[56,8,128]{2,1,0:T(8,128)S(1)} %get-tuple-element.34), channel_id=1, source_target_pairs={{0,1},{2,3},{4,5},{6,7},{8,9},{10,11},{12,13},{14,15},{1,0},{3,2},... | collective-permute-start | bytes 688136 | tf_op jit(solution)/shard_map/ppermute | solution.py:503
  21.8 10.8 %collective-permute-start.3 = (f32[56,8,128]{2,1,0:T(8,128)S(1)}, f32[56,8,128]{2,1,0:T(8,128)S(1)}, u32[]{:S(2)}, u32[]{:S(2)}) collective-permute-start(f32[56,8,128]{2,1,0:T(8,128)S(1)} %get-tuple-element.35), channel_id=1, source_target_pairs={{1,2},{3,4},{5,6},{7,8},{9,10},{11,12},{13,14},{2,1},{4,3},{6,5},{... | collective-permute-start | bytes 688136 | tf_op jit(solution)/shard_map/ppermute | solution.py:503
